TPU v7x, 32 devices: a whole 2x2x4 slice. The times are simulated.
32 devices in a mesh: groups: 2 (over x), row: 16 (over z, y, core).
Axes of the slice: x: 2, y: 2, z: 4, core: 2. Of those that a mesh axis runs over, the one named last changes fastest.
Arguments:
- panels: bfloat16 [512, 6, 64, 128], P(('groups', 'row')), parts along dimension 0, may hold values from -1 to 1
- blocks: int32 [512, 6], P(('groups', 'row')), parts along dimension 0, may hold values from 0 to 15, all different within a row; in each aligned block of 16 rows (0 to 15, 16 to 31, ...) at most 6 rows name the same one
- row_block: int32 [32], P('groups'), parts along dimension 0, may hold values from 0 to 15, each once
- coeffs: float32 [512, 6, 128], P(('groups', 'row')), parts along dimension 0, may hold values from -0.109375 to 0.109375
- metric_inv: float32 [128, 64], P('groups'), parts along dimension 0, may hold values from -1 to 3, as said below
- three_index: bfloat16 [32, 64, 128, 128], P(('groups', 'row')), parts along dimension 0, may hold values from -0.75 to 0.75
Outputs:
- exchange: bfloat16 [32, 128, 2048], P(('groups', 'row')), parts along dimension 0
- coulomb: bfloat16 [32, 128, 128], P(('groups', 'row')), parts along dimension 0
- fitted: float32 [128], P('groups'), parts along dimension 0
There are 2 independent parts, one for each index of `groups`. A program takes and returns all parts, laid end to end along the dimension named above; each array names one. Nothing has to cross between parts.
Inputs may be any that keep to these rules, and one draw needn't show every extreme that they name: Each orbital names 6 different blocks; among the orbitals of one device (aligned runs of 16 orbitals) no block is named more than 6 times, and that bound is reached. `row_block`: each block appears once. `metric_inv`: Symmetric.
All inputs are finite; a program needn't handle non-finite values.
Results may differ from a plain program's by a relative error of at most 0.001.
Values may be sent and summed in bfloat16 or wider, within the bound.
No kernel may reach another device: no remote copies, remote signals or barrier semaphores. Data moves between devices by JAX's collectives and lax.ppermute only.
A program may use at most 192 MiB of HBM per device.

v0:
```python
import jax
import jax.numpy as jnp
from jax import lax
from jax.sharding import PartitionSpec as P


def row_terms(rows_in, row_ids, owned, count):
    total_rows = rows_in.shape[0]
    group = 32
    slots = rows_in.shape[1]
    width = rows_in.shape[3]
    grouped = rows_in.reshape((total_rows // group, group) + rows_in.shape[1:])
    grouped_ids = row_ids.reshape(total_rows // group, group, slots)

    def step(total, item):
        block_rows, block_ids = item
        chosen = (block_ids == owned).astype(jnp.bfloat16)
        picked = jnp.einsum(
            "gs,gspk->gpk", chosen, block_rows, preferred_element_type=jnp.float32
        ).astype(jnp.bfloat16)
        prods = jnp.einsum("gpk,gspn->gskn", picked, block_rows, preferred_element_type=jnp.float32)
        target = jnp.maximum(block_ids, 0).reshape(-1)
        added = jax.ops.segment_sum(prods.reshape(-1, width, width), target, num_segments=count)
        return (total + added, None)

    start = jnp.zeros((count, width, width), jnp.float32)
    total, _ = lax.scan(step, start, (grouped, grouped_ids))
    return total


def per_device(panels, blocks, row_block, coeffs, metric_inv, three_index):
    count = row_block.shape[0]
    orbits, slots, aux, width = panels.shape
    capacity = max(2, (orbits * slots + count - 1) // count)
    here = lax.axis_index("row")
    owned = row_block[here]
    ranks = jnp.arange(count, dtype=jnp.int32)
    flat_ids = blocks.reshape(-1)
    matches = (row_block[None, :] == flat_ids[:, None]).astype(jnp.int32)
    target = jnp.sum(matches * ranks[None, :], axis=1)
    hits = (ranks[None, :] == target[:, None]).astype(jnp.int32)
    before = jnp.cumsum(hits, axis=0) - hits
    place = jnp.sum(before * hits, axis=1)
    source = jnp.repeat(panels, slots, axis=0)
    source_ids = jnp.repeat(blocks, slots, axis=0).astype(jnp.bfloat16)
    outgoing = (
        jnp.zeros((count, capacity, slots, aux, width), jnp.bfloat16).at[target, place].set(source)
    )
    outgoing_ids = (
        jnp.full((count, capacity, slots), -1.0, jnp.bfloat16).at[target, place].set(source_ids)
    )
    partial_terms = jnp.einsum(
        "ispm,ism->p", panels.astype(jnp.float32), coeffs, precision=lax.Precision.HIGHEST
    )
    gamma = lax.psum(partial_terms, "row")
    fitted = jnp.dot(metric_inv, gamma, precision=lax.Precision.HIGHEST)
    coulomb = jnp.einsum(
        "p,rpmn->rmn", fitted, three_index.astype(jnp.float32), precision=lax.Precision.HIGHEST
    )
    arrived, arrived_ids = (
        lax.all_to_all(outgoing, "row", split_axis=0, concat_axis=0, tiled=True),
        lax.all_to_all(outgoing_ids, "row", split_axis=0, concat_axis=0, tiled=True),
    )
    accum = row_terms(
        arrived.reshape(-1, slots, aux, width),
        arrived_ids.reshape(-1, slots).astype(jnp.int32),
        owned,
        count,
    )
    exchange = accum.transpose(1, 0, 2).reshape(width, count * width)[None].astype(jnp.bfloat16)
    return (exchange, coulomb.astype(jnp.bfloat16), fitted)


def solution(mesh):
    placed = (
        P(("groups", "row"), None, None, None),
        P(("groups", "row"), None),
        P("groups"),
        P(("groups", "row"), None, None),
        P("groups", None),
        P(("groups", "row"), None, None, None),
    )
    return jax.shard_map(
        per_device,
        mesh=mesh,
        in_specs=placed,
        out_specs=(P(("groups", "row"), None, None), P(("groups", "row"), None, None), P("groups")),
        check_vma=False,
    )
```

profile of v0, /device:TPU:18, one launch (start us, length us, event | category | flops | bytes accessed | tf_op | source)
XLA Modules:
  0.0 441.7 jit_solution(12969555933166204063)
XLA Ops:
  0.6 0.9 copy.27
  1.6 0.7 convert_element_type.48
  2.3 0.8 select_reduce_fusion.1
  3.9 5.5 %scatter_fusion.1 = bf16[16,6,6]{2,0,1:T(8,128)(2,1)S(1)} fusion(bf16[16,6,6]{2,0,1:T(8,128)(2,1)S(1)} %broadcast_in_dim.8, s32[96]{0:T(128)S(1)} %fusion.14, bf16[96,6]{1,0:T(8,128)(2,1)S(1)} %copy.28), kind=kCustom, calls=%fused_computation.1 | custom fusion | bytes 4224 | tf_op jit(solution)/shard_map/scatter | solution.py:50
  10.1 6.2 %all-to-all-start = ((bf16[16,6,6]{2,1,0:T(8,128)(2,1)}), bf16[16,6,6]{2,1,0:T(8,128)(2,1)S(1)}, u32[]{:S(2)}, u32[]{:S(2)}) async-start(bf16[16,6,6]{2,1,0:T(8,128)(2,1)} %copy.29), calls=%async_computation | async-start | bytes 65536 | tf_op jit(solution)/shard_map/all_to_all | solution.py:62
  16.3 7.6 %broadcast_in_dim.11 = bf16[16,6,6,64,128]{4,3,2,1,0:T(8,128)(2,1)} broadcast(bf16[16,6,64,128]{3,2,1,0:T(8,128)(2,1)} %param.8), dimensions={0,2,3,4} | broadcast | bytes 11010048 | tf_op jit(solution)/shard_map/broadcast_in_dim | solution.py:44
  23.9 6.0 %broadcast_in_dim.10 = bf16[16,6,6,64,128]{4,3,2,1,0:T(8,128)(2,1)} broadcast(bf16[]{:T(256)} %constant.15.clone.1), dimensions={} | broadcast | bytes 9437186 | tf_op jit(solution)/shard_map/broadcast_in_dim | solution.py:47
  29.9 30.4 %scatter_fusion.2 = bf16[16,6,6,64,128]{4,3,2,1,0:T(8,128)(2,1)} fusion(bf16[16,6,6,64,128]{4,3,2,1,0:T(8,128)(2,1)} %broadcast_in_dim.10, s32[96]{0:T(128)S(1)} %fusion.14, bf16[96,6,64,128]{3,2,1,0:T(8,128)(2,1)} %bitcast.69), kind=kCustom, calls=%fused_computation.2 | custom fusion | bytes 28312320 | tf_op jit(solution)/shard_map/scatter | solution.py:47
  60.3 6.4 %all-to-all-start.1 = ((bf16[16,6,6,64,128]{4,3,2,1,0:T(8,128)(2,1)}), bf16[16,6,6,64,128]{4,3,2,1,0:T(8,128)(2,1)}, u32[]{:S(2)}, u32[]{:S(2)}) async-start(bf16[16,6,6,64,128]{4,3,2,1,0:T(8,128)(2,1)} %scatter_fusion.2), calls=%async_computation.1 | async-start | bytes 18874368 | tf_op jit(solution)/shard_map/all_to_all | solution.py:61
  67.3 2.7 convolution_bitcast_fusion
  70.0 219.8 %psum.7 = f32[64]{0:T(128)S(1)} all-reduce(f32[64]{0:T(128)S(1)} %convolution_bitcast_fusion), channel_id=1, replica_groups=mesh['groups'=2,'row'=16] {'row'}, use_global_device_ids=true, to_apply=%region_8.9 | all-reduce | flops 64 | bytes 512 | tf_op jit(solution)/shard_map/psum | solution.py:55
  290.0 1.8 fusion.6
  292.8 147.4 %while.10 = (s32[]{:T(128)}, f32[16,128,128]{2,1,0:T(8,128)S(1)}, s32[3,32,6]{2,1,0:T(8,128)S(1)}, bf16[3,32,6,64,128]{4,3,2,1,0:T(8,128)(2,1)}, s32[]{:T(128)}, /*index=5*/s32[]{:T(128)}) while((s32[]{:T(128)}, f32[16,128,128]{2,1,0:T(8,128)S(1)}, s32[3,32,6]{2,1,0:T(8,128)S(1)}, bf16[3,32,6,64,128]{4,3,2,1,0:T(8,128)(2,1)}, s32[]{:T(128)}, ...), condition=%wide.region_7.8_spmd, body=%wide.region_5.7_spmd.sunk | while | flops 409207168 | bytes 90182616 | solution.py:27
  292.8 0.6 compare_bitcast_fusion.2
  293.5 2.6 dynamic-slice_bitcast_fusion.2
  296.1 2.2 fusion.28
  298.3 5.7 %fusion.29 = f32[32,6,128,128]{3,2,1,0:T(8,128)} fusion(bf16[32,6,64,128]{3,2,1,0:T(8,128)(2,1)S(1)} %dynamic-slice_bitcast_fusion.2, f32[32,64,128]{2,1,0:T(8,128)S(1)} %bitcast.68), kind=kOutput, calls=%fused_computation.6.clone.1 | convolution fusion | flops 402915328 | bytes 16777216 | tf_op jit(solution)/shard_map/while/body/eval_jaxpr/gpk,gspn->gskn/dot_general | solution.py:21
  304.0 12.6 %copy.57 = f32[192,128,128]{2,1,0:T(8,128)} copy(f32[192,128,128]{1,2,0:T(8,128)} %bitcast.67) | data formatting | bytes 25165824 | tf_op jit(solution)/shard_map/while/body/eval_jaxpr/reshape | solution.py:23
  316.7 25.3 %scatter_fusion = f32[16,128,128]{2,1,0:T(8,128)S(1)} fusion(f32[16,128,128]{2,1,0:T(8,128)S(1)} %get-tuple-element.94, s32[192]{0:T(256)S(1)} %reshape.120, f32[192,128,128]{2,1,0:T(8,128)} %copy.57), kind=kCustom, calls=%fused_computation.clone.1 | custom fusion | flops 3145728 | bytes 37749504 | tf_op jit(solution)/shard_map/while/body/eval_jaxpr/scatter-add | solution.py:23
  342.0 0.6 compare_bitcast_fusion.2
  342.6 2.6 dynamic-slice_bitcast_fusion.2
  345.2 2.2 fusion.28
  347.4 5.7 %fusion.29 = f32[32,6,128,128]{3,2,1,0:T(8,128)} fusion(bf16[32,6,64,128]{3,2,1,0:T(8,128)(2,1)S(1)} %dynamic-slice_bitcast_fusion.2, f32[32,64,128]{2,1,0:T(8,128)S(1)} %bitcast.68), kind=kOutput, calls=%fused_computation.6.clone.1 | convolution fusion | flops 402915328 | bytes 16777216 | tf_op jit(solution)/shard_map/while/body/eval_jaxpr/gpk,gspn->gskn/dot_general | solution.py:21
  353.1 12.6 %copy.57 = f32[192,128,128]{2,1,0:T(8,128)} copy(f32[192,128,128]{1,2,0:T(8,128)} %bitcast.67) | data formatting | bytes 25165824 | tf_op jit(solution)/shard_map/while/body/eval_jaxpr/reshape | solution.py:23
  365.8 25.3 %scatter_fusion = f32[16,128,128]{2,1,0:T(8,128)S(1)} fusion(f32[16,128,128]{2,1,0:T(8,128)S(1)} %get-tuple-element.94, s32[192]{0:T(256)S(1)} %reshape.120, f32[192,128,128]{2,1,0:T(8,128)} %copy.57), kind=kCustom, calls=%fused_computation.clone.1 | custom fusion | flops 3145728 | bytes 37749504 | tf_op jit(solution)/shard_map/while/body/eval_jaxpr/scatter-add | solution.py:23
  391.1 0.6 compare_bitcast_fusion.2
  391.8 2.6 dynamic-slice_bitcast_fusion.2
  394.3 2.2 fusion.28
  396.6 5.7 %fusion.29 = f32[32,6,128,128]{3,2,1,0:T(8,128)} fusion(bf16[32,6,64,128]{3,2,1,0:T(8,128)(2,1)S(1)} %dynamic-slice_bitcast_fusion.2, f32[32,64,128]{2,1,0:T(8,128)S(1)} %bitcast.68), kind=kOutput, calls=%fused_computation.6.clone.1 | convolution fusion | flops 402915328 | bytes 16777216 | tf_op jit(solution)/shard_map/while/body/eval_jaxpr/gpk,gspn->gskn/dot_general | solution.py:21
  402.2 12.6 %copy.57 = f32[192,128,128]{2,1,0:T(8,128)} copy(f32[192,128,128]{1,2,0:T(8,128)} %bitcast.67) | data formatting | bytes 25165824 | tf_op jit(solution)/shard_map/while/body/eval_jaxpr/reshape | solution.py:23
  414.9 25.3 %scatter_fusion = f32[16,128,128]{2,1,0:T(8,128)S(1)} fusion(f32[16,128,128]{2,1,0:T(8,128)S(1)} %get-tuple-element.94, s32[192]{0:T(256)S(1)} %reshape.120, f32[192,128,128]{2,1,0:T(8,128)} %copy.57), kind=kCustom, calls=%fused_computation.clone.1 | custom fusion | flops 3145728 | bytes 37749504 | tf_op jit(solution)/shard_map/while/body/eval_jaxpr/scatter-add | solution.py:23
  440.7 1.0 convert_element_type.54
  (38 shorter events, 4.0 us)
Async XLA Ops:
  0.6 289.3 %copy-start = (bf16[1,64,128,128]{3,2,1,0:T(8,128)(2,1)S(1)}, bf16[1,64,128,128]{3,2,1,0:T(8,128)(2,1)}, u32[]{:S(2)}) copy-start(bf16[1,64,128,128]{3,2,1,0:T(8,128)(2,1)} %param.13) | copy-start | bytes 6291460
  10.1 50.2 %all-to-all-start = ((bf16[16,6,6]{2,1,0:T(8,128)(2,1)}), bf16[16,6,6]{2,1,0:T(8,128)(2,1)S(1)}, u32[]{:S(2)}, u32[]{:S(2)}) async-start(bf16[16,6,6]{2,1,0:T(8,128)(2,1)} %copy.29), calls=%async_computation | async-start | bytes 65536 | tf_op jit(solution)/shard_map/all_to_all | solution.py:62
  60.3 6.4 %copy-start.4 = (s32[16]{0:T(128)S(1)}, s32[16]{0:T(128)}, u32[]{:S(2)}) copy-start(s32[16]{0:T(128)} %param.10) | copy-start | bytes 196
  60.3 7.0 %copy-start.3 = (f32[16,6,128]{2,0,1:T(8,128)S(1)}, f32[16,6,128]{2,0,1:T(8,128)}, u32[]{:S(2)}) copy-start(f32[16,6,128]{2,0,1:T(8,128)} %param.11) | copy-start | bytes 147460
  60.3 229.5 %copy-start.1 = (f32[64,64]{1,0:T(8,128)S(1)}, f32[64,64]{1,0:T(8,128)}, u32[]{:S(2)}) copy-start(f32[64,64]{1,0:T(8,128)} %param.12) | copy-start | bytes 49156
  60.3 232.4 %all-to-all-start.1 = ((bf16[16,6,6,64,128]{4,3,2,1,0:T(8,128)(2,1)}), bf16[16,6,6,64,128]{4,3,2,1,0:T(8,128)(2,1)}, u32[]{:S(2)}, u32[]{:S(2)}) async-start(bf16[16,6,6,64,128]{4,3,2,1,0:T(8,128)(2,1)} %scatter_fusion.2), calls=%async_computation.1 | async-start | bytes 18874368 | tf_op jit(solution)/shard_map/all_to_all | solution.py:61
  289.9 2.9 copy-start.2
where the time goes:
time: 444 us; the launch traced here: 442 us
  blocking collectives  220 us (50%)
  local copies, waits for them, and re-layouts  99.7 us (22%)
  other arithmetic  80.4 us (18%)
  matrix products  28.3 us (6%)
  starting transfers between devices  12.6 us (3%)
    psum x1, blocking collectives, per_device(): gamma = lax.psum(partial_terms, 'row')  220 us
    scatter-add x3, other arithmetic, step(): jax.ops.segment_sum(prods.reshape(-1, width, width), target, num_segments...  75.8 us
    reshape x3, local copies, waits for them, and re-layouts, step(): prods.reshape(-1, width, width)  37.8 us
    scatter x1, local copies, waits for them, and re-layouts, per_device(): jnp.zeros((count, capacity, slots, aux, width), jnp.bfloat16)  30.4 us
    dot_general x3, matrix products, step(): jnp.einsum('gpk,gspn->gskn', picked, block_rows, preferred_element_type=j...  16.9 us
  transfers between devices with their start and end apart: 2, of which 0 were waited for; matrix products, arithmetic and copies ran while one was open for 11% of the time, Pallas kernels for 0%

commit v1 on v0

--- a/solution.py
+++ b/solution.py
@@ -1,6 +1,9 @@
+import functools
 import jax
 import jax.numpy as jnp
 from jax import lax
+from jax.experimental import pallas as pl
+from jax.experimental.pallas import tpu as pltpu
 from jax.sharding import PartitionSpec as P
 
 
@@ -28,7 +31,7 @@
     return total
 
 
-def per_device(panels, blocks, row_block, coeffs, metric_inv, three_index):
+def sent_panels(panels, blocks, row_block, coeffs, metric_inv, three_index):
     count = row_block.shape[0]
     orbits, slots, aux, width = panels.shape
     capacity = max(2, (orbits * slots + count - 1) // count)
@@ -71,6 +74,155 @@
     return (exchange, coulomb.astype(jnp.bfloat16), fitted)
 
 
+DEPTH = 4
+ROWS = 4 * DEPTH
+HALF = ROWS // 2
+Z_FIRST = ((1, 3),)
+Y_FIRST = ((4, 5), (0, 1))
+
+
+def piece_of(z, k):
+    inner = jnp.where(k < 2, 3 - k, k - 2)
+    return jnp.where(z == 0, 3 - k, jnp.where(z == 3, k, jnp.where(z == 1, inner, 3 - inner)))
+
+
+def dense_kernel(runs, y_major, holders_ref, mine_ids, other_ids, mine, other, out, rank_of, dense):
+    orbits, slots, aux, width = mine.shape
+    step = pl.program_id(0)
+    me = lax.axis_index("row")
+
+    @pl.when(step == 0)
+    def _():
+        for k in range(ROWS):
+            rank_of[holders_ref[k]] = k
+        dense[...] = jnp.zeros_like(dense)
+
+        def place(i, carry):
+            for which, (ids, rows) in enumerate(((mine_ids, mine), (other_ids, other))):
+                at = pl.ds(pl.multiple_of((which * orbits + i) * aux, aux), aux)
+                for s in range(slots):
+                    rank = rank_of[ids[i, s]]
+                    tile = rows[i, s]
+                    dense[at, pl.ds(pl.multiple_of(rank * width, width), width)] = tile
+                    again = jnp.where(rank < HALF, rank + ROWS, rank)
+                    dense[at, pl.ds(pl.multiple_of(again * width, width), width)] = tile
+            return carry
+
+        lax.fori_loop(0, orbits, place, 0)
+
+    if y_major:
+        y, k = step // DEPTH, step % DEPTH
+    else:
+        k, y = step // 2, step % 2
+    row = piece_of(me // 4, k) * 4 + y * 2 + me % 2
+    left = dense[:, pl.ds(pl.multiple_of(row * width, width), width)]
+    at = 0
+    for first, number in runs:
+        right = dense[:, pl.ds(pl.multiple_of((row + first) * width, width), number * width)]
+        out[0, 0, :, at : at + number * width] = lax.dot_general(
+            left, right, (((0,), (0,)), ((), ())), preferred_element_type=jnp.float32
+        )
+        at += number * width
+
+
+def partial_rows(runs, y_major, row_block, mine_ids, other_ids, mine, other):
+    orbits, slots, aux, width = mine.shape
+    columns = sum(number for _, number in runs) * width
+    outer, inner = (2, DEPTH) if y_major else (DEPTH, 2)
+    scalars = pl.BlockSpec(memory_space=pltpu.SMEM)
+    whole = pl.BlockSpec(mine.shape, lambda g: (0, 0, 0, 0))
+    flops = 2 * outer * inner * width * columns * 2 * orbits * aux
+    return pl.pallas_call(
+        functools.partial(dense_kernel, runs, y_major),
+        grid=(outer * inner,),
+        in_specs=[scalars, scalars, scalars, whole, whole],
+        out_specs=pl.BlockSpec((1, 1, width, columns), lambda g: (g // inner, g % inner, 0, 0)),
+        out_shape=jax.ShapeDtypeStruct((outer, inner, width, columns), jnp.float32),
+        scratch_shapes=[
+            pltpu.SMEM((ROWS,), jnp.int32),
+            pltpu.VMEM((2 * orbits * aux, (ROWS + HALF) * width), jnp.bfloat16),
+        ],
+        compiler_params=pltpu.CompilerParams(vmem_limit_bytes=48 << 20),
+        cost_estimate=pl.CostEstimate(
+            flops=flops, bytes_accessed=4 * outer * inner * width * columns, transcendentals=0
+        ),
+    )(row_block, mine_ids, other_ids, mine, other)
+
+
+def pairs(move):
+    return [(i, move(i)) for i in range(ROWS) if move(i) is not None]
+
+
+ACROSS_CORE = pairs(lambda i: i ^ 1)
+ACROSS_Y = pairs(lambda i: i ^ 2)
+
+
+def rightward(upto):
+    return [(i, i + 4) for i in range(ROWS) if i // 4 <= upto and i // 4 < 3]
+
+
+def leftward(upto):
+    return [(i, i - 4) for i in range(ROWS) if 3 - i // 4 <= upto and i // 4 > 0]
+
+
+def sum_along_z(pieces, z):
+    ends = (z == 0) | (z == DEPTH - 1)
+    came = lax.ppermute(pieces[0], "row", rightward(0) + leftward(0))
+    going = jnp.where(ends, pieces[1], pieces[0]) + came
+    right = lax.ppermute(going, "row", rightward(1))
+    left = lax.ppermute(going, "row", leftward(1))
+    right = lax.ppermute(jnp.where(z == 1, pieces[1], pieces[2]) + right, "row", rightward(2))
+    left = lax.ppermute(jnp.where(z == 2, pieces[1], pieces[2]) + left, "row", leftward(2))
+    return pieces[3] + right + left
+
+
+def summed_rows(panels, blocks, row_block, coeffs, metric_inv, three_index):
+    width = panels.shape[3]
+    me = lax.axis_index("row")
+    z, y = me // 4, (me // 2) % 2
+
+    other = lax.ppermute(panels, "row", ACROSS_CORE)
+    other_ids = lax.ppermute(blocks, "row", ACROSS_CORE)
+
+    gamma = jnp.einsum(
+        "ispm,ism->p", panels.astype(jnp.float32), coeffs, precision=lax.Precision.HIGHEST
+    )
+    for bit in (1, 2, 4, 8):
+        gamma = gamma + lax.ppermute(gamma, "row", pairs(lambda i: i ^ bit))
+    fitted = jnp.dot(metric_inv, gamma, precision=lax.Precision.HIGHEST)
+    coulomb = jnp.einsum(
+        "p,rpmn->rmn", fitted, three_index.astype(jnp.float32), precision=lax.Precision.HIGHEST
+    )
+
+    z_first = partial_rows(Z_FIRST, False, row_block, blocks, other_ids, panels, other)
+    y_first = partial_rows(Y_FIRST, True, row_block, blocks, other_ids, panels, other)
+
+    own = lax.dynamic_index_in_dim(y_first, y, 0, keepdims=False)
+    theirs = lax.dynamic_index_in_dim(y_first, 1 - y, 0, keepdims=False)
+    pieces = [own[k] + lax.ppermute(theirs[k], "row", ACROSS_Y) for k in range(DEPTH)]
+    late = sum_along_z(pieces, z)
+
+    early = sum_along_z([z_first[k] for k in range(DEPTH)], z)
+    early = lax.dynamic_index_in_dim(early, y, 0, keepdims=False) + lax.ppermute(
+        lax.dynamic_index_in_dim(early, 1 - y, 0, keepdims=False), "row", ACROSS_Y
+    )
+
+    held = {}
+    for runs, rows in ((Z_FIRST, early), (Y_FIRST, late)):
+        at = 0
+        for first, number in runs:
+            for d in range(first, first + number):
+                held[d] = rows[:, at * width : (at + 1) * width].astype(jnp.bfloat16)
+                at += 1
+    ring = [held[d] for d in range(HALF + 1)]
+    for d in range(HALF - 1, 0, -1):
+        ring.append(lax.ppermute(held[d].T, "row", pairs(lambda i: (i + d) % ROWS)))
+    place = (row_block[:, None] == jnp.arange(ROWS)[None, :]).astype(jnp.int32)
+    source = (jnp.sum(place * jnp.arange(ROWS)[:, None], axis=0) - me) % ROWS
+    exchange = jnp.stack(ring)[source].transpose(1, 0, 2).reshape(1, width, ROWS * width)
+    return (exchange, coulomb.astype(jnp.bfloat16), fitted)
+
+
 def solution(mesh):
     placed = (
         P(("groups", "row"), None, None, None),
@@ -81,7 +233,7 @@
         P(("groups", "row"), None, None, None),
     )
     return jax.shard_map(
-        per_device,
+        summed_rows if mesh.shape["row"] == ROWS else sent_panels,
         mesh=mesh,
         in_specs=placed,
         out_specs=(P(("groups", "row"), None, None), P(("groups", "row"), None, None), P("groups")),

time: 444 us -> 119 us (0.27)
  the two profiles are of different devices: /device:TPU:18 before, /device:TPU:0 now
where the time goes in v1:
time: 119 us
  starting transfers between devices  48.6 us (41%)
  waiting for transfers between devices  22.6 us (19%)
  Pallas kernels  20.3 us (17%)
  local copies, waits for them, and re-layouts  12.6 us (11%)
  other arithmetic  8.84 us (7%)
  matrix products  4.66 us (4%)
    pallas_call x2, Pallas kernels, partial_rows(): pl.pallas_call(functools.partial(dense_kernel, runs, y_major), grid=(oute...  20.3 us
    ppermute x7, starting transfers between devices, summed_rows(): ring.append(lax.ppermute(held[d].T, 'row', pairs(lambda i: (i + d) % ROWS)))  10.1 us
    ppermute x4, starting transfers between devices, summed_rows(): gamma = gamma + lax.ppermute(gamma, 'row', pairs(lambda i: i ^ bit))  8.28 us
    ppermute x7, waiting for transfers between devices, summed_rows(): ring.append(lax.ppermute(held[d].T, 'row', pairs(lambda i: (i + d) % ROWS)))  8.25 us
    ppermute x2, starting transfers between devices, sum_along_z(): lax.ppermute(jnp.where(z == 1, pieces[1], pieces[2]) + right, 'row', righ...  7.97 us
    ppermute x4, waiting for transfers between devices, summed_rows(): lax.ppermute(theirs[k], 'row', ACROSS_Y)  7.75 us
    ppermute x2, starting transfers between devices, sum_along_z(): right = lax.ppermute(going, 'row', rightward(1))  6.45 us
    unnamed x31, local copies, waits for them, and re-layouts  6.08 us
  transfers between devices with their start and end apart: 28, of which 9 were waited for; matrix products, arithmetic and copies ran while one was open for 18% of the time, Pallas kernels for 17%

profile of v1, /device:TPU:0, one launch (start us, length us, event | category | flops | bytes accessed | tf_op | source)
XLA Modules:
  0.0 118.5 jit_solution(14612145504189762400)
XLA Ops:
  2.1 2.7 %convolution_bitcast_fusion = f32[64]{0:T(128)S(1)} fusion(bf16[16,6,64,128]{3,2,1,0:T(8,128)(2,1)} %mine.3, f32[16,6,128,1]{2,0,1,3:T(8,128)} %bitcast.144), kind=kOutput, calls=%fused_computation.3 | convolution fusion | flops 9437184 | bytes 1622272 | tf_op jit(solution)/shard_map/ispm,ism->p/dot_general | solution.py:187
  6.1 2.7 %collective-permute-start.25 = (f32[64]{0:T(128)S(1)}, f32[64]{0:T(128)S(1)}, u32[]{:S(2)}, u32[]{:S(2)}) collective-permute-start(f32[64]{0:T(128)S(1)} %add.117), channel_id=1, source_target_pairs={{0,2},{1,3},{2,0},{3,1},{4,6},{5,7},{6,4},{7,5},{8,10},{9,11},{10,... | collective-permute-start | bytes 776 | tf_op jit(solution)/shard_map/ppermute | solution.py:191
  8.8 1.5 %collective-permute-done.25 = f32[64]{0:T(128)S(1)} collective-permute-done((f32[64]{0:T(128)S(1)}, f32[64]{0:T(128)S(1)}, u32[]{:S(2)}, u32[]{:S(2)}) %collective-permute-start.25) | collective-permute-done | bytes 288 | tf_op jit(solution)/shard_map/ppermute | solution.py:191
  10.3 2.1 %collective-permute-start.26 = (f32[64]{0:T(128)S(1)}, f32[64]{0:T(128)S(1)}, u32[]{:S(2)}, u32[]{:S(2)}) collective-permute-start(f32[64]{0:T(128)S(1)} %add.118), channel_id=1, source_target_pairs={{0,4},{1,5},{2,6},{3,7},{4,0},{5,1},{6,2},{7,3},{8,12},{9,13},{10,... | collective-permute-start | bytes 776 | tf_op jit(solution)/shard_map/ppermute | solution.py:191
  12.4 1.5 %collective-permute-done.26 = f32[64]{0:T(128)S(1)} collective-permute-done((f32[64]{0:T(128)S(1)}, f32[64]{0:T(128)S(1)}, u32[]{:S(2)}, u32[]{:S(2)}) %collective-permute-start.26) | collective-permute-done | bytes 288 | tf_op jit(solution)/shard_map/ppermute | solution.py:191
  13.9 3.0 %collective-permute-start.27 = (f32[64]{0:T(128)S(1)}, f32[64]{0:T(128)S(1)}, u32[]{:S(2)}, u32[]{:S(2)}) collective-permute-start(f32[64]{0:T(128)S(1)} %add.119), channel_id=1, source_target_pairs={{0,8},{1,9},{2,10},{3,11},{4,12},{5,13},{6,14},{7,15},{8,0},{9,1},... | collective-permute-start | bytes 776 | tf_op jit(solution)/shard_map/ppermute | solution.py:191
  17.0 1.4 %copy-done.1 = bf16[16,6,64,128]{3,2,1,0:T(8,128)(2,1)S(1)} copy-done((bf16[16,6,64,128]{3,2,1,0:T(8,128)(2,1)S(1)}, bf16[16,6,64,128]{3,2,1,0:T(8,128)(2,1)}, u32[]{:S(2)}) %copy-start.1) | copy-done | bytes 1572888
  19.0 8.4 %shard_map.86 = f32[4,2,128,384]{3,2,1,0:T(8,128)S(1)} custom-call(s32[16]{0:T(128)S(1)} %copy-done.2, s32[16,6]{1,0:T(8,128)S(1)} %copy.42.mine_ids, s32[16,6]{1,0:T(8,128)S(1)} %collective-permute-done.other_ids, bf16[16,6,64,128]{3,2,1,0:T(8,128)(2,1)S(1)} %copy-done.1, bf16[16,6,64,128]{3,2,1,0:T(8,128)(2,1)} %collective-permute-done.1.other), custom_call_target="tpu_custom_call" | custom-call | flops 1610612736 | bytes 1572864 | tf_op jit(solution)/shard_map/pallas_call | solution.py:135
  27.5 3.5 %collective-permute-start.11 = (f32[2,128,384]{2,1,0:T(8,128)S(1)}, f32[2,128,384]{2,1,0:T(8,128)S(1)}, u32[]{:S(2)}, u32[]{:S(2)}) collective-permute-start(f32[2,128,384]{2,1,0:T(8,128)S(1)} %slice_bitcast_fusion), channel_id=1, source_target_pairs={{0,4},{1,5},{2,6},{3,7},{12,8},{13,9},{14,10},{15,11},{16,20},{17,... | collective-permute-start | bytes 1179656 | tf_op jit(solution)/shard_map/ppermute | solution.py:170
  31.0 11.9 %shard_map.85 = f32[2,4,128,768]{3,2,1,0:T(8,128)} custom-call(s32[16]{0:T(128)S(1)} %copy-done.2, s32[16,6]{1,0:T(8,128)S(1)} %copy.42.mine_ids, s32[16,6]{1,0:T(8,128)S(1)} %collective-permute-done.other_ids, bf16[16,6,64,128]{3,2,1,0:T(8,128)(2,1)S(1)} %copy-done.1, bf16[16,6,64,128]{3,2,1,0:T(8,128)(2,1)} %collective-permute-done.1.other), custom_call_target="tpu_custom_call" | custom-call | flops 3221225472 | bytes 3145728 | tf_op jit(solution)/shard_map/pallas_call | solution.py:135
  42.9 2.4 %dynamic-slice_bitcast_fusion.6 = (f32[128,768]{1,0:T(8,128)}, f32[128,768]{1,0:T(8,128)}, f32[128,768]{1,0:T(8,128)S(1)}, f32[128,768]{1,0:T(8,128)S(1)}) fusion(f32[2,4,128,768]{3,2,1,0:T(8,128)} %shard_map.85, s32[]{:T(128)S(6)} %select_n.90, s32[]{:T(128)S(6)} %add.121, s32[]{:T(128)S(6)} %add.125, s32[]{:T(128)S(6)} %add.123), kind=kLoop, calls=%fused_computation.19 | loop fusion | bytes 3145744 | tf_op jit(solution)/shard_map/squeeze | solution.py:202
  45.3 1.5 %collective-permute-start.5 = (f32[128,768]{1,0:T(8,128)S(1)}, f32[128,768]{1,0:T(8,128)S(1)}, u32[]{:S(2)}, u32[]{:S(2)}) collective-permute-start(f32[128,768]{1,0:T(8,128)S(1)} %get-tuple-element.16), channel_id=1, source_target_pairs={{0,2},{1,3},{2,0},{3,1},{4,6},{5,7},{6,4},{7,5},{8,10},{9,11},{10,... | collective-permute-start | bytes 1179656 | tf_op jit(solution)/shard_map/ppermute | solution.py:202
  47.6 1.3 %collective-permute-start.12 = (f32[2,128,384]{2,1,0:T(8,128)S(1)}, f32[2,128,384]{2,1,0:T(8,128)S(1)}, u32[]{:S(2)}, u32[]{:S(2)}) collective-permute-start(f32[2,128,384]{2,1,0:T(8,128)S(1)} %select_add_fusion.1), channel_id=1, source_target_pairs={{0,4},{1,5},{2,6},{3,7},{4,8},{5,9},{6,10},{7,11},{16,20},{17,21},... | collective-permute-start | bytes 1179656 | tf_op jit(solution)/shard_map/ppermute | solution.py:172
  49.6 7.7 %collective-permute-done.5 = f32[128,768]{1,0:T(8,128)S(1)} collective-permute-done((f32[128,768]{1,0:T(8,128)S(1)}, f32[128,768]{1,0:T(8,128)S(1)}, u32[]{:S(2)}, u32[]{:S(2)}) %collective-permute-start.5) | collective-permute-done | bytes 393248 | tf_op jit(solution)/shard_map/ppermute | solution.py:202
  58.4 1.3 %collective-permute-start.6 = (f32[128,768]{1,0:T(8,128)S(1)}, f32[128,768]{1,0:T(8,128)S(1)}, u32[]{:S(2)}, u32[]{:S(2)}) collective-permute-start(f32[128,768]{1,0:T(8,128)S(1)} %fusion.4), channel_id=1, source_target_pairs={{0,4},{1,5},{2,6},{3,7},{12,8},{13,9},{14,10},{15,11},{16,20},{17,... | collective-permute-start | bytes 1179656 | tf_op jit(solution)/shard_map/ppermute | solution.py:170
  59.7 1.8 %fusion = f32[1,128,128]{2,0,1:T(1,128)S(1)} fusion(bf16[64,128,128]{2,1,0:T(8,128)(2,1)S(1)} %bitcast.131, f32[1,64]{1,0:T(1,128)S(1)} %fusion.17), kind=kOutput, calls=%fused_computation.1 | convolution fusion | flops 12582912 | bytes 2162944 | tf_op jit(solution)/shard_map/p,rpmn->rmn/dot_general | solution.py:193
  61.5 1.6 %collective-permute-start.4 = (f32[128,768]{1,0:T(8,128)}, f32[128,768]{1,0:T(8,128)S(1)}, u32[]{:S(2)}, u32[]{:S(2)}) collective-permute-start(f32[128,768]{1,0:T(8,128)} %get-tuple-element.14), channel_id=1, source_target_pairs={{0,2},{1,3},{2,0},{3,1},{4,6},{5,7},{6,4},{7,5},{8,10},{9,11},{10,... | collective-permute-start | bytes 1179656 | tf_op jit(solution)/shard_map/ppermute | solution.py:202
  63.2 1.3 %collective-permute-start.13 = (f32[2,128,384]{2,1,0:T(8,128)S(1)}, f32[2,128,384]{2,1,0:T(8,128)S(1)}, u32[]{:S(2)}, u32[]{:S(2)}) collective-permute-start(f32[2,128,384]{2,1,0:T(8,128)S(1)} %get-tuple-element.17), channel_id=1, source_target_pairs={{0,4},{1,5},{2,6},{3,7},{4,8},{5,9},{6,10},{7,11},{8,12},{9,13},{1... | collective-permute-start | bytes 1179656 | tf_op jit(solution)/shard_map/ppermute | solution.py:174
  64.5 1.3 %collective-permute-start.15 = (f32[2,128,384]{2,1,0:T(8,128)S(1)}, f32[2,128,384]{2,1,0:T(8,128)S(1)}, u32[]{:S(2)}, u32[]{:S(2)}) collective-permute-start(f32[2,128,384]{2,1,0:T(8,128)S(1)} %get-tuple-element.18), channel_id=1, source_target_pairs={{4,0},{5,1},{6,2},{7,3},{8,4},{9,5},{10,6},{11,7},{12,8},{13,9},{1... | collective-permute-start | bytes 1179656 | tf_op jit(solution)/shard_map/ppermute | solution.py:175
  65.8 3.0 %collective-permute-done.6 = f32[128,768]{1,0:T(8,128)S(1)} collective-permute-done((f32[128,768]{1,0:T(8,128)S(1)}, f32[128,768]{1,0:T(8,128)S(1)}, u32[]{:S(2)}, u32[]{:S(2)}) %collective-permute-start.6) | collective-permute-done | bytes 393248 | tf_op jit(solution)/shard_map/ppermute | solution.py:170
  68.8 1.8 %select_add_fusion.4 = (f32[128,768]{1,0:T(8,128)}, f32[128,768]{1,0:T(8,128)S(1)}) fusion(f32[128,768]{1,0:T(8,128)S(1)} %collective-permute-done.6, f32[128,768]{1,0:T(8,128)S(1)} %fusion.4, pred[]{:T(512)S(6)} %or.4, f32[128,768]{1,0:T(8,128)S(1)} %collective-permute-done.3, f32[2,4,128,768]{3,2,1,0:T(8,128)} %shard_map.85, s32[]{:T(128)S(6)} %select_n.89, ...), kind=kLoop, calls=%fused_computation.29 | loop fusion | flops 294912 | bytes 2359305 | tf_op jit(solution)/shard_map/add | solution.py:171
  70.7 5.1 %collective-permute-start.7 = (f32[128,768]{1,0:T(8,128)}, f32[128,768]{1,0:T(8,128)}, u32[]{:S(2)}, u32[]{:S(2)}) collective-permute-start(f32[128,768]{1,0:T(8,128)} %get-tuple-element.9), channel_id=1, source_target_pairs={{0,4},{1,5},{2,6},{3,7},{4,8},{5,9},{6,10},{7,11},{16,20},{17,21},... | collective-permute-start | bytes 1179656 | tf_op jit(solution)/shard_map/ppermute | solution.py:172
  75.8 1.4 %collective-permute-start.9 = (f32[128,768]{1,0:T(8,128)}, f32[128,768]{1,0:T(8,128)}, u32[]{:S(2)}, u32[]{:S(2)}) collective-permute-start(f32[128,768]{1,0:T(8,128)} %get-tuple-element.9), channel_id=1, source_target_pairs={{8,4},{9,5},{10,6},{11,7},{12,8},{13,9},{14,10},{15,11},{24,20},{2... | collective-permute-start | bytes 1179656 | tf_op jit(solution)/shard_map/ppermute | solution.py:173
  77.8 1.5 %collective-permute-start.2 = (f32[128,768]{1,0:T(8,128)}, f32[128,768]{1,0:T(8,128)}, u32[]{:S(2)}, u32[]{:S(2)}) collective-permute-start(f32[128,768]{1,0:T(8,128)} %get-tuple-element.13), channel_id=1, source_target_pairs={{0,2},{1,3},{2,0},{3,1},{4,6},{5,7},{6,4},{7,5},{8,10},{9,11},{10,... | collective-permute-start | bytes 1179656 | tf_op jit(solution)/shard_map/ppermute | solution.py:202
  80.9 2.2 %select_add_fusion.5 = (f32[128,768]{1,0:T(8,128)}, f32[128,768]{1,0:T(8,128)}) fusion(f32[128,768]{1,0:T(8,128)} %collective-permute-done.7, f32[128,768]{1,0:T(8,128)S(1)} %get-tuple-element.10, pred[]{:T(512)S(6)} %eq.17, f32[128,768]{1,0:T(8,128)S(1)} %collective-permute-done.4, f32[2,4,128,768]{3,2,1,0:T(8,128)} %shard_map.85, s32[]{:T(128)S(6)} %select_n.89, ...), kind=kLoop, calls=%fused_computation.30 | loop fusion | flops 491520 | bytes 2752522 | tf_op jit(solution)/shard_map/add | solution.py:174
  84.5 6.7 %collective-permute-start.8 = (f32[128,768]{1,0:T(8,128)}, f32[128,768]{1,0:T(8,128)S(1)}, u32[]{:S(2)}, u32[]{:S(2)}) collective-permute-start(f32[128,768]{1,0:T(8,128)} %get-tuple-element.11), channel_id=1, source_target_pairs={{0,4},{1,5},{2,6},{3,7},{4,8},{5,9},{6,10},{7,11},{8,12},{9,13},{1... | collective-permute-start | bytes 1179656 | tf_op jit(solution)/shard_map/ppermute | solution.py:174
  93.2 1.7 %collective-permute-start.22 = (bf16[128,128]{1,0:T(8,128)(2,1)S(1)}, bf16[128,128]{1,0:T(8,128)(2,1)}, u32[]{:S(2)}, u32[]{:S(2)}) collective-permute-start(bf16[128,128]{1,0:T(8,128)(2,1)S(1)} %get-tuple-element.26), channel_id=1, source_target_pairs={{0,2},{1,3},{2,4},{3,5},{4,6},{5,7},{6,8},{7,9},{8,10},{9,11},{10,... | collective-permute-start | bytes 98312 | tf_op jit(solution)/shard_map/ppermute | solution.py:219
  94.8 1.8 %collective-permute-start.23 = (bf16[128,128]{1,0:T(8,128)(2,1)S(1)}, bf16[128,128]{1,0:T(8,128)(2,1)}, u32[]{:S(2)}, u32[]{:S(2)}) collective-permute-start(bf16[128,128]{1,0:T(8,128)(2,1)S(1)} %get-tuple-element.25), channel_id=1, source_target_pairs={{0,1},{1,2},{2,3},{3,4},{4,5},{5,6},{6,7},{7,8},{8,9},{9,10},{10,1... | collective-permute-start | bytes 98312 | tf_op jit(solution)/shard_map/ppermute | solution.py:219
  99.9 3.4 %collective-permute-start.18 = (bf16[128,128]{1,0:T(8,128)(2,1)S(1)}, bf16[128,128]{1,0:T(8,128)(2,1)S(1)}, u32[]{:S(2)}, u32[]{:S(2)}) collective-permute-start(bf16[128,128]{1,0:T(8,128)(2,1)S(1)} %bitcast.140), channel_id=1, source_target_pairs={{0,6},{1,7},{2,8},{3,9},{4,10},{5,11},{6,12},{7,13},{8,14},{9,15},... | collective-permute-start | bytes 98312 | tf_op jit(solution)/shard_map/ppermute | solution.py:219
  103.6 2.7 %collective-permute-start.19 = (bf16[128,128]{1,0:T(8,128)(2,1)S(1)}, bf16[128,128]{1,0:T(8,128)(2,1)S(1)}, u32[]{:S(2)}, u32[]{:S(2)}) collective-permute-start(bf16[128,128]{1,0:T(8,128)(2,1)S(1)} %bitcast.138), channel_id=1, source_target_pairs={{0,5},{1,6},{2,7},{3,8},{4,9},{5,10},{6,11},{7,12},{8,13},{9,14},{... | collective-permute-start | bytes 98312 | tf_op jit(solution)/shard_map/ppermute | solution.py:219
  106.3 2.3 %collective-permute-done.18 = bf16[128,128]{1,0:T(8,128)(2,1)S(1)} collective-permute-done((bf16[128,128]{1,0:T(8,128)(2,1)S(1)}, bf16[128,128]{1,0:T(8,128)(2,1)S(1)}, u32[]{:S(2)}, u32[]{:S(2)}) %collective-permute-start.18) | collective-permute-done | bytes 32800 | tf_op jit(solution)/shard_map/ppermute | solution.py:219
  108.9 5.4 %collective-permute-done.20 = bf16[128,128]{1,0:T(8,128)(2,1)S(1)} collective-permute-done((bf16[128,128]{1,0:T(8,128)(2,1)S(1)}, bf16[128,128]{1,0:T(8,128)(2,1)S(1)}, u32[]{:S(2)}, u32[]{:S(2)}) %collective-permute-start.20) | collective-permute-done | bytes 32800 | tf_op jit(solution)/shard_map/ppermute | solution.py:219
  (92 shorter events, 19.5 us)
Async XLA Ops:
  0.6 59.1 %copy-start = (bf16[1,64,128,128]{3,2,1,0:T(8,128)(2,1)S(1)}, bf16[1,64,128,128]{3,2,1,0:T(8,128)(2,1)}, u32[]{:S(2)}) copy-start(bf16[1,64,128,128]{3,2,1,0:T(8,128)(2,1)} %param.11) | copy-start | bytes 6291460
  0.6 16.3 %collective-permute-start.1 = (bf16[16,6,64,128]{3,2,1,0:T(8,128)(2,1)}, bf16[16,6,64,128]{3,2,1,0:T(8,128)(2,1)}, u32[]{:S(2)}, u32[]{:S(2)}) collective-permute-start(bf16[16,6,64,128]{3,2,1,0:T(8,128)(2,1)} %mine.3), channel_id=1, source_target_pairs={{0,1},{1,0},{2,3},{3,2},{4,5},{5,4},{6,7},{7,6},{8,9},{9,8},{10,11... | collective-permute-start | bytes 4718600 | tf_op jit(solution)/shard_map/ppermute | solution.py:184
  2.0 14.9 %collective-permute-start = (s32[16,6]{1,0:T(8,128)S(1)}, s32[16,6]{1,0:T(8,128)S(1)}, u32[]{:S(2)}, u32[]{:S(2)}) collective-permute-start(s32[16,6]{1,0:T(8,128)S(1)} %copy.42.mine_ids), channel_id=1, source_target_pairs={{0,1},{1,0},{2,3},{3,2},{4,5},{5,4},{6,7},{7,6},{8,9},{9,8},{10,11... | collective-permute-start | bytes 1160 | tf_op jit(solution)/shard_map/ppermute | solution.py:185
  4.8 1.3 %collective-permute-start.24 = (f32[64]{0:T(128)S(1)}, f32[64]{0:T(128)S(1)}, u32[]{:S(2)}, u32[]{:S(2)}) collective-permute-start(f32[64]{0:T(128)S(1)} %convolution_bitcast_fusion), channel_id=1, source_target_pairs={{0,1},{1,0},{2,3},{3,2},{4,5},{5,4},{6,7},{7,6},{8,9},{9,8},{10,11... | collective-permute-start | bytes 776 | tf_op jit(solution)/shard_map/ppermute | solution.py:191
  6.1 4.2 %collective-permute-start.25 = (f32[64]{0:T(128)S(1)}, f32[64]{0:T(128)S(1)}, u32[]{:S(2)}, u32[]{:S(2)}) collective-permute-start(f32[64]{0:T(128)S(1)} %add.117), channel_id=1, source_target_pairs={{0,2},{1,3},{2,0},{3,1},{4,6},{5,7},{6,4},{7,5},{8,10},{9,11},{10,... | collective-permute-start | bytes 776 | tf_op jit(solution)/shard_map/ppermute | solution.py:191
  10.3 3.6 %collective-permute-start.26 = (f32[64]{0:T(128)S(1)}, f32[64]{0:T(128)S(1)}, u32[]{:S(2)}, u32[]{:S(2)}) collective-permute-start(f32[64]{0:T(128)S(1)} %add.118), channel_id=1, source_target_pairs={{0,4},{1,5},{2,6},{3,7},{4,0},{5,1},{6,2},{7,3},{8,12},{9,13},{10,... | collective-permute-start | bytes 776 | tf_op jit(solution)/shard_map/ppermute | solution.py:191
  13.9 32.8 %collective-permute-start.27 = (f32[64]{0:T(128)S(1)}, f32[64]{0:T(128)S(1)}, u32[]{:S(2)}, u32[]{:S(2)}) collective-permute-start(f32[64]{0:T(128)S(1)} %add.119), channel_id=1, source_target_pairs={{0,8},{1,9},{2,10},{3,11},{4,12},{5,13},{6,14},{7,15},{8,0},{9,1},... | collective-permute-start | bytes 776 | tf_op jit(solution)/shard_map/ppermute | solution.py:191
  17.0 1.4 %copy-start.1 = (bf16[16,6,64,128]{3,2,1,0:T(8,128)(2,1)S(1)}, bf16[16,6,64,128]{3,2,1,0:T(8,128)(2,1)}, u32[]{:S(2)}) copy-start(bf16[16,6,64,128]{3,2,1,0:T(8,128)(2,1)} %mine.3) | copy-start | bytes 4718596
  27.5 20.0 %collective-permute-start.11 = (f32[2,128,384]{2,1,0:T(8,128)S(1)}, f32[2,128,384]{2,1,0:T(8,128)S(1)}, u32[]{:S(2)}, u32[]{:S(2)}) collective-permute-start(f32[2,128,384]{2,1,0:T(8,128)S(1)} %slice_bitcast_fusion), channel_id=1, source_target_pairs={{0,4},{1,5},{2,6},{3,7},{12,8},{13,9},{14,10},{15,11},{16,20},{17,... | collective-permute-start | bytes 1179656 | tf_op jit(solution)/shard_map/ppermute | solution.py:170
  42.9 3.9 %copy-start.3 = (f32[64,64]{1,0:T(8,128)S(1)}, f32[64,64]{1,0:T(8,128)}, u32[]{:S(2)}) copy-start(f32[64,64]{1,0:T(8,128)} %param.10) | copy-start | bytes 49156
  45.3 12.1 %collective-permute-start.5 = (f32[128,768]{1,0:T(8,128)S(1)}, f32[128,768]{1,0:T(8,128)S(1)}, u32[]{:S(2)}, u32[]{:S(2)}) collective-permute-start(f32[128,768]{1,0:T(8,128)S(1)} %get-tuple-element.16), channel_id=1, source_target_pairs={{0,2},{1,3},{2,0},{3,1},{4,6},{5,7},{6,4},{7,5},{8,10},{9,11},{10,... | collective-permute-start | bytes 1179656 | tf_op jit(solution)/shard_map/ppermute | solution.py:202
  46.9 14.6 %copy-start.4 = (f32[1,64]{1,0:T(1,128)}, f32[1,64]{1,0:T(1,128)S(1)}, u32[]{:S(2)}) copy-start(f32[1,64]{1,0:T(1,128)S(1)} %fusion.17) | copy-start | bytes 772
  46.9 18.9 %collective-permute-start.3 = (f32[128,768]{1,0:T(8,128)S(1)}, f32[128,768]{1,0:T(8,128)S(1)}, u32[]{:S(2)}, u32[]{:S(2)}) collective-permute-start(f32[128,768]{1,0:T(8,128)S(1)} %get-tuple-element.15), channel_id=1, source_target_pairs={{0,2},{1,3},{2,0},{3,1},{4,6},{5,7},{6,4},{7,5},{8,10},{9,11},{10,... | collective-permute-start | bytes 1179656 | tf_op jit(solution)/shard_map/ppermute | solution.py:202
  47.6 15.5 %collective-permute-start.12 = (f32[2,128,384]{2,1,0:T(8,128)S(1)}, f32[2,128,384]{2,1,0:T(8,128)S(1)}, u32[]{:S(2)}, u32[]{:S(2)}) collective-permute-start(f32[2,128,384]{2,1,0:T(8,128)S(1)} %select_add_fusion.1), channel_id=1, source_target_pairs={{0,4},{1,5},{2,6},{3,7},{4,8},{5,9},{6,10},{7,11},{16,20},{17,21},... | collective-permute-start | bytes 1179656 | tf_op jit(solution)/shard_map/ppermute | solution.py:172
  48.9 14.2 %collective-permute-start.14 = (f32[2,128,384]{2,1,0:T(8,128)S(1)}, f32[2,128,384]{2,1,0:T(8,128)S(1)}, u32[]{:S(2)}, u32[]{:S(2)}) collective-permute-start(f32[2,128,384]{2,1,0:T(8,128)S(1)} %select_add_fusion.1), channel_id=1, source_target_pairs={{8,4},{9,5},{10,6},{11,7},{12,8},{13,9},{14,10},{15,11},{24,20},{2... | collective-permute-start | bytes 1179656 | tf_op jit(solution)/shard_map/ppermute | solution.py:173
  58.4 10.5 %collective-permute-start.6 = (f32[128,768]{1,0:T(8,128)S(1)}, f32[128,768]{1,0:T(8,128)S(1)}, u32[]{:S(2)}, u32[]{:S(2)}) collective-permute-start(f32[128,768]{1,0:T(8,128)S(1)} %fusion.4), channel_id=1, source_target_pairs={{0,4},{1,5},{2,6},{3,7},{12,8},{13,9},{14,10},{15,11},{16,20},{17,... | collective-permute-start | bytes 1179656 | tf_op jit(solution)/shard_map/ppermute | solution.py:170
  61.5 19.4 %collective-permute-start.4 = (f32[128,768]{1,0:T(8,128)}, f32[128,768]{1,0:T(8,128)S(1)}, u32[]{:S(2)}, u32[]{:S(2)}) collective-permute-start(f32[128,768]{1,0:T(8,128)} %get-tuple-element.14), channel_id=1, source_target_pairs={{0,2},{1,3},{2,0},{3,1},{4,6},{5,7},{6,4},{7,5},{8,10},{9,11},{10,... | collective-permute-start | bytes 1179656 | tf_op jit(solution)/shard_map/ppermute | solution.py:202
  63.2 14.7 %collective-permute-start.13 = (f32[2,128,384]{2,1,0:T(8,128)S(1)}, f32[2,128,384]{2,1,0:T(8,128)S(1)}, u32[]{:S(2)}, u32[]{:S(2)}) collective-permute-start(f32[2,128,384]{2,1,0:T(8,128)S(1)} %get-tuple-element.17), channel_id=1, source_target_pairs={{0,4},{1,5},{2,6},{3,7},{4,8},{5,9},{6,10},{7,11},{8,12},{9,13},{1... | collective-permute-start | bytes 1179656 | tf_op jit(solution)/shard_map/ppermute | solution.py:174
  64.5 14.9 %collective-permute-start.15 = (f32[2,128,384]{2,1,0:T(8,128)S(1)}, f32[2,128,384]{2,1,0:T(8,128)S(1)}, u32[]{:S(2)}, u32[]{:S(2)}) collective-permute-start(f32[2,128,384]{2,1,0:T(8,128)S(1)} %get-tuple-element.18), channel_id=1, source_target_pairs={{4,0},{5,1},{6,2},{7,3},{8,4},{9,5},{10,6},{11,7},{12,8},{13,9},{1... | collective-permute-start | bytes 1179656 | tf_op jit(solution)/shard_map/ppermute | solution.py:175
  70.7 10.3 %collective-permute-start.7 = (f32[128,768]{1,0:T(8,128)}, f32[128,768]{1,0:T(8,128)}, u32[]{:S(2)}, u32[]{:S(2)}) collective-permute-start(f32[128,768]{1,0:T(8,128)} %get-tuple-element.9), channel_id=1, source_target_pairs={{0,4},{1,5},{2,6},{3,7},{4,8},{5,9},{6,10},{7,11},{16,20},{17,21},... | collective-permute-start | bytes 1179656 | tf_op jit(solution)/shard_map/ppermute | solution.py:172
  75.8 5.1 %collective-permute-start.9 = (f32[128,768]{1,0:T(8,128)}, f32[128,768]{1,0:T(8,128)}, u32[]{:S(2)}, u32[]{:S(2)}) collective-permute-start(f32[128,768]{1,0:T(8,128)} %get-tuple-element.9), channel_id=1, source_target_pairs={{8,4},{9,5},{10,6},{11,7},{12,8},{13,9},{14,10},{15,11},{24,20},{2... | collective-permute-start | bytes 1179656 | tf_op jit(solution)/shard_map/ppermute | solution.py:173
  77.8 17.0 %collective-permute-start.2 = (f32[128,768]{1,0:T(8,128)}, f32[128,768]{1,0:T(8,128)}, u32[]{:S(2)}, u32[]{:S(2)}) collective-permute-start(f32[128,768]{1,0:T(8,128)} %get-tuple-element.13), channel_id=1, source_target_pairs={{0,2},{1,3},{2,0},{3,1},{4,6},{5,7},{6,4},{7,5},{8,10},{9,11},{10,... | collective-permute-start | bytes 1179656 | tf_op jit(solution)/shard_map/ppermute | solution.py:202
  80.3 10.9 %collective-permute-start.16 = (f32[128,384]{0,1:T(8,128)}, f32[128,384]{0,1:T(8,128)}, u32[]{:S(2)}, u32[]{:S(2)}) collective-permute-start(f32[128,384]{0,1:T(8,128)} %copy.44), channel_id=1, source_target_pairs={{0,2},{1,3},{2,0},{3,1},{4,6},{5,7},{6,4},{7,5},{8,10},{9,11},{10,... | collective-permute-start | bytes 589832 | tf_op jit(solution)/shard_map/ppermute | solution.py:206
  83.2 13.4 %collective-permute-start.10 = (f32[128,768]{1,0:T(8,128)}, f32[128,768]{1,0:T(8,128)S(1)}, u32[]{:S(2)}, u32[]{:S(2)}) collective-permute-start(f32[128,768]{1,0:T(8,128)} %get-tuple-element.12), channel_id=1, source_target_pairs={{4,0},{5,1},{6,2},{7,3},{8,4},{9,5},{10,6},{11,7},{12,8},{13,9},{1... | collective-permute-start | bytes 1179656 | tf_op jit(solution)/shard_map/ppermute | solution.py:175
  84.5 12.6 %collective-permute-start.8 = (f32[128,768]{1,0:T(8,128)}, f32[128,768]{1,0:T(8,128)S(1)}, u32[]{:S(2)}, u32[]{:S(2)}) collective-permute-start(f32[128,768]{1,0:T(8,128)} %get-tuple-element.11), channel_id=1, source_target_pairs={{0,4},{1,5},{2,6},{3,7},{4,8},{5,9},{6,10},{7,11},{8,12},{9,13},{1... | collective-permute-start | bytes 1179656 | tf_op jit(solution)/shard_map/ppermute | solution.py:174
  93.1 21.2 %collective-permute-start.21 = (bf16[128,128]{1,0:T(8,128)(2,1)}, bf16[128,128]{1,0:T(8,128)(2,1)}, u32[]{:S(2)}, u32[]{:S(2)}) collective-permute-start(bf16[128,128]{1,0:T(8,128)(2,1)} %get-tuple-element.27), channel_id=1, source_target_pairs={{0,3},{1,4},{2,5},{3,6},{4,7},{5,8},{6,9},{7,10},{8,11},{9,12},{10... | collective-permute-start | bytes 98312 | tf_op jit(solution)/shard_map/ppermute | solution.py:219
  93.2 21.9 %collective-permute-start.22 = (bf16[128,128]{1,0:T(8,128)(2,1)S(1)}, bf16[128,128]{1,0:T(8,128)(2,1)}, u32[]{:S(2)}, u32[]{:S(2)}) collective-permute-start(bf16[128,128]{1,0:T(8,128)(2,1)S(1)} %get-tuple-element.26), channel_id=1, source_target_pairs={{0,2},{1,3},{2,4},{3,5},{4,6},{5,7},{6,8},{7,9},{8,10},{9,11},{10,... | collective-permute-start | bytes 98312 | tf_op jit(solution)/shard_map/ppermute | solution.py:219
  94.8 21.0 %collective-permute-start.23 = (bf16[128,128]{1,0:T(8,128)(2,1)S(1)}, bf16[128,128]{1,0:T(8,128)(2,1)}, u32[]{:S(2)}, u32[]{:S(2)}) collective-permute-start(bf16[128,128]{1,0:T(8,128)(2,1)S(1)} %get-tuple-element.25), channel_id=1, source_target_pairs={{0,1},{1,2},{2,3},{3,4},{4,5},{5,6},{6,7},{7,8},{8,9},{9,10},{10,1... | collective-permute-start | bytes 98312 | tf_op jit(solution)/shard_map/ppermute | solution.py:219
  99.3 4.3 %collective-permute-start.17 = (bf16[128,128]{1,0:T(8,128)(2,1)S(1)}, bf16[128,128]{1,0:T(8,128)(2,1)S(1)}, u32[]{:S(2)}, u32[]{:S(2)}) collective-permute-start(bf16[128,128]{1,0:T(8,128)(2,1)S(1)} %bitcast.142), channel_id=1, source_target_pairs={{0,7},{1,8},{2,9},{3,10},{4,11},{5,12},{6,13},{7,14},{8,15},{9,0},... | collective-permute-start | bytes 98312 | tf_op jit(solution)/shard_map/ppermute | solution.py:219
  99.9 8.7 %collective-permute-start.18 = (bf16[128,128]{1,0:T(8,128)(2,1)S(1)}, bf16[128,128]{1,0:T(8,128)(2,1)S(1)}, u32[]{:S(2)}, u32[]{:S(2)}) collective-permute-start(bf16[128,128]{1,0:T(8,128)(2,1)S(1)} %bitcast.140), channel_id=1, source_target_pairs={{0,6},{1,7},{2,8},{3,9},{4,10},{5,11},{6,12},{7,13},{8,14},{9,15},... | collective-permute-start | bytes 98312 | tf_op jit(solution)/shard_map/ppermute | solution.py:219
  103.6 5.3 %collective-permute-start.19 = (bf16[128,128]{1,0:T(8,128)(2,1)S(1)}, bf16[128,128]{1,0:T(8,128)(2,1)S(1)}, u32[]{:S(2)}, u32[]{:S(2)}) collective-permute-start(bf16[128,128]{1,0:T(8,128)(2,1)S(1)} %bitcast.138), channel_id=1, source_target_pairs={{0,5},{1,6},{2,7},{3,8},{4,9},{5,10},{6,11},{7,12},{8,13},{9,14},{... | collective-permute-start | bytes 98312 | tf_op jit(solution)/shard_map/ppermute | solution.py:219
  108.6 5.7 %collective-permute-start.20 = (bf16[128,128]{1,0:T(8,128)(2,1)S(1)}, bf16[128,128]{1,0:T(8,128)(2,1)S(1)}, u32[]{:S(2)}, u32[]{:S(2)}) collective-permute-start(bf16[128,128]{1,0:T(8,128)(2,1)S(1)} %bitcast.136), channel_id=1, source_target_pairs={{0,4},{1,5},{2,6},{3,7},{4,8},{5,9},{6,10},{7,11},{8,12},{9,13},{1... | collective-permute-start | bytes 98312 | tf_op jit(solution)/shard_map/ppermute | solution.py:219
  (1 other events, 0.7 us)

commit v2 on v0

--- a/solution.py
+++ b/solution.py
@@ -1,6 +1,9 @@
+import functools
 import jax
 import jax.numpy as jnp
 from jax import lax
+from jax.experimental import pallas as pl
+from jax.experimental.pallas import tpu as pltpu
 from jax.sharding import PartitionSpec as P
 
 
@@ -28,7 +31,7 @@
     return total
 
 
-def per_device(panels, blocks, row_block, coeffs, metric_inv, three_index):
+def sent_panels(panels, blocks, row_block, coeffs, metric_inv, three_index):
     count = row_block.shape[0]
     orbits, slots, aux, width = panels.shape
     capacity = max(2, (orbits * slots + count - 1) // count)
@@ -71,6 +74,293 @@
     return (exchange, coulomb.astype(jnp.bfloat16), fitted)
 
 
+ROWS = 16
+CORE, Y, Z = 1, 2, (4, 8, 12)
+PLACES = 16
+Z_FIRST, Y_FIRST = (1, "extra"), (2, 3, 0)
+TAIL = 16
+TOP = 14.99
+
+
+def send(x, flip):
+    return lax.ppermute(x, "row", [(i, i ^ flip) for i in range(ROWS)])
+
+
+def swap_low(index):
+    return (index & 12) | ((index & 1) << 1) | ((index >> 1) & 1)
+
+
+def side_of(z, apart):
+    return (z >> 1) & 1 if apart == 2 else z & 1
+
+
+def first_place(row, region):
+    if region == 0:
+        return 0
+    if region == "extra":
+        return 2 + (row & 1)
+    return region * 4 + side_of(row >> 2, region) * 2
+
+
+def width_of(region):
+    return 1 if region == "extra" else 2
+
+
+def encode(out, sums):
+    height, columns = sums[0].shape
+    line = lax.broadcasted_iota(jnp.int32, (TAIL, columns), 0)
+    exponents = jnp.zeros((TAIL, columns), jnp.float32)
+    for j, x in enumerate(sums):
+        peak = jnp.maximum(jnp.max(jnp.abs(x), axis=0, keepdims=True), 2.0**-100)
+        exponent = jnp.ceil(jnp.log2(peak) * 8)
+        scaled = jnp.round(x * jnp.exp2(TOP - exponent * 0.125))
+        out[j * height : (j + 1) * height, :] = scaled.astype(jnp.int32).astype(jnp.int16)
+        exponents = jnp.where(line == j, exponent, exponents)
+    out[len(sums) * height :, :] = exponents.astype(jnp.int32).astype(jnp.int16)
+
+
+def decode(codes, j, height):
+    count = (codes.shape[0] - TAIL) // height
+    exponents = codes[count * height :, :].astype(jnp.int32).astype(jnp.float32)
+    scale = jnp.exp2(exponents[j : j + 1, :] * 0.125 - TOP)
+    return codes[j * height : (j + 1) * height, :].astype(jnp.int32).astype(jnp.float32) * scale
+
+
+def rows_kernel(group, flips, per_message, sides, *refs):
+    lists, ranks, panels = refs[:sides], refs[sides : 2 * sides], refs[2 * sides : 3 * sides]
+    outs, picks, spreads = refs[3 * sides : -4], refs[-4:-2], refs[-2:]
+    orbits, slots, aux, width = panels[0].shape
+    capacity = lists[0].shape[1]
+    me = lax.axis_index("row")
+    gathered = []
+
+    for j, flip in enumerate(flips):
+        row = me ^ flip
+        row_rank = swap_low(row)
+        picked, spread = picks[j % 2], spreads[j % 2]
+        spans = [
+            pl.ds(pl.multiple_of(first_place(row, region) * width, width), width_of(region) * width)
+            for region in group
+        ]
+        for span in spans:
+            spread[:, span] = jnp.zeros((spread.shape[0], span.size), jnp.bfloat16)
+        for side in range(sides):
+            for n in range(capacity):
+                code = lists[side][row, n]
+                orbit, slot = jnp.maximum(code, 0) >> 3, jnp.maximum(code, 0) & 7
+                at = pl.ds((side * capacity + n) * aux, aux)
+                chosen = panels[side][orbit, slot]
+                tiles = [panels[side][orbit, t] for t in range(slots)]
+                places = [ranks[side][orbit, t] ^ row_rank for t in range(slots)]
+                picked[at, :] = jnp.where(code >= 0, chosen, jnp.zeros_like(chosen))
+                for tile, place in zip(tiles, places):
+                    spread[at, pl.ds(pl.multiple_of(place * width, width), width)] = tile
+        sums = [
+            lax.dot_general(
+                picked[...],
+                spread[:, span],
+                (((0,), (0,)), ((), ())),
+                preferred_element_type=jnp.float32,
+            )
+            for span in spans
+        ]
+        if per_message:
+            gathered.append(jnp.concatenate(sums, axis=1))
+            if len(gathered) == per_message:
+                encode(outs[j // per_message], gathered)
+                gathered = []
+        else:
+            at = 0
+            for x in sums:
+                outs[0][j, :, at : at + x.shape[1]] = x
+                at += x.shape[1]
+
+
+def partial_rows(group, flips, per_message, lists, ranks, panels):
+    orbits, slots, aux, width = panels[0].shape
+    capacity, sides = lists[0].shape[1], len(panels)
+    columns = sum(width_of(region) for region in group) * width
+    depth = sides * capacity * aux
+    if per_message:
+        message = jax.ShapeDtypeStruct((per_message * width + TAIL, columns), jnp.int16)
+        shapes = [message] * (len(flips) // per_message)
+    else:
+        shapes = [jax.ShapeDtypeStruct((len(flips), width, columns), jnp.float32)]
+    scalars = pl.BlockSpec(memory_space=pltpu.SMEM)
+    whole = pl.BlockSpec(memory_space=pltpu.VMEM)
+    return pl.pallas_call(
+        functools.partial(rows_kernel, group, flips, per_message, sides),
+        in_specs=[scalars] * (2 * sides) + [whole] * sides,
+        out_specs=[whole] * len(shapes),
+        out_shape=shapes,
+        scratch_shapes=[pltpu.VMEM((depth, width), jnp.bfloat16)] * 2
+        + [pltpu.VMEM((depth, PLACES * width), jnp.bfloat16)] * 2,
+        compiler_params=pltpu.CompilerParams(vmem_limit_bytes=32 << 20),
+        cost_estimate=pl.CostEstimate(
+            flops=8 * len(flips) * width * columns * depth,
+            bytes_accessed=4 * len(flips) * width * columns,
+            transcendentals=0,
+        ),
+    )(*lists, *ranks, *panels)
+
+
+def turn_y_kernel(stay, along_z, message, own, *codes):
+    height = own.shape[0]
+    rows = [stay[j] + sum(decode(c, j, height) for c in codes) for j in range(2)]
+    encode(message, rows[:1])
+    own[...] = rows[1]
+
+
+def turn_y(stay, codes):
+    height, columns = stay.shape[1:]
+    return pl.pallas_call(
+        lambda stay, *refs: turn_y_kernel(stay, None, refs[-2], refs[-1], *refs[:-2]),
+        out_shape=[
+            jax.ShapeDtypeStruct((height + TAIL, columns), jnp.int16),
+            jax.ShapeDtypeStruct((height, columns), jnp.float32),
+        ],
+        compiler_params=pltpu.CompilerParams(vmem_limit_bytes=32 << 20),
+    )(stay, *codes)
+
+
+def turn_z_kernel(stay, code, *outs):
+    height = stay.shape[1]
+    for j in range(1, len(outs)):
+        encode(outs[j], [stay[j] + decode(code, j, height)])
+    outs[0][...] = stay[0] + decode(code, 0, height)
+
+
+def turn_z(stay, code):
+    count, height, columns = stay.shape
+    message = jax.ShapeDtypeStruct((height + TAIL, columns), jnp.int16)
+    return pl.pallas_call(
+        turn_z_kernel,
+        out_shape=[jax.ShapeDtypeStruct((height, columns), jnp.float32)] + [message] * (count - 1),
+        compiler_params=pltpu.CompilerParams(vmem_limit_bytes=32 << 20),
+    )(stay, code)
+
+
+def finish_kernel(backs, own, *refs):
+    codes, done, back = refs[: -backs - 1], refs[-backs - 1], refs[len(refs) - backs :]
+    height = own.shape[0]
+    total = own[...] + sum(decode(c, 0, height) for c in codes)
+    done[...] = total.astype(jnp.bfloat16)
+    for b, out in enumerate(back):
+        out[...] = total[:, b * height : (b + 1) * height].T.astype(jnp.bfloat16)
+
+
+def finish(own, codes, backs):
+    height, columns = own.shape
+    return pl.pallas_call(
+        functools.partial(finish_kernel, backs),
+        out_shape=[jax.ShapeDtypeStruct((height, columns), jnp.bfloat16)]
+        + [jax.ShapeDtypeStruct((height, height), jnp.bfloat16)] * backs,
+        compiler_params=pltpu.CompilerParams(vmem_limit_bytes=32 << 20),
+    )(own, *codes)
+
+
+def give_back(block, region, b):
+    def holder(i):
+        return i ^ swap_low(first_place(i, region) + b)
+
+    return lax.ppermute(block, "row", [(i, holder(i)) for i in range(ROWS)])
+
+
+def assemble_kernel(holders, early, late, *refs):
+    came, out = refs[:-1], refs[-1]
+    width = early.shape[0]
+    me = lax.axis_index("row")
+    rank = swap_low(me)
+
+    def put(place, block):
+        column = holders[swap_low(place ^ rank)]
+        out[0, :, pl.ds(pl.multiple_of(column * width, width), width)] = block
+
+    k = 0
+    for group, rows in ((Z_FIRST, early), (Y_FIRST, late)):
+        at = 0
+        for region in group:
+            start = first_place(me, region)
+            for b in range(width_of(region)):
+                put(start + b, rows[:, at * width : (at + 1) * width])
+                at += 1
+                if region == 0:
+                    continue
+                other = 5 - start if region == "extra" else region * 8 + 2 - start + b
+                put(other, came[k][...])
+                k += 1
+
+
+def assemble(row_block, early, late, came):
+    width = early.shape[0]
+    vmem = pl.BlockSpec(memory_space=pltpu.VMEM)
+    return pl.pallas_call(
+        assemble_kernel,
+        in_specs=[pl.BlockSpec(memory_space=pltpu.SMEM)] + [vmem] * (2 + len(came)),
+        out_shape=jax.ShapeDtypeStruct((1, width, ROWS * width), jnp.bfloat16),
+    )(row_block, early, late, *came)
+
+
+def naming(blocks, row_block, capacity):
+    orbits, slots = blocks.shape
+    holders = jnp.arange(ROWS, dtype=jnp.int32)
+    hits = (blocks[:, :, None] == row_block[None, None, :]).astype(jnp.int32)
+    rank = jnp.sum(hits * swap_low(holders), axis=2)
+    named = jnp.sum(hits, axis=1)
+    code = jnp.arange(orbits, dtype=jnp.int32)[:, None] * 8 + jnp.sum(
+        hits * jnp.arange(slots, dtype=jnp.int32)[None, :, None], axis=1
+    )
+    earlier = (jnp.arange(orbits)[None, :] < jnp.arange(orbits)[:, None]).astype(jnp.int32)
+    before = jnp.sum(earlier[:, :, None] * named[None, :, :], axis=1)
+    here = (before[:, :, None] == jnp.arange(capacity)) & (named[:, :, None] > 0)
+    listed = jnp.sum(jnp.where(here, code[:, :, None] + 1, 0), axis=0) - 1
+    return listed, rank
+
+
+def summed_rows(panels, blocks, row_block, coeffs, metric_inv, three_index):
+    orbits, slots, aux, width = panels.shape
+    capacity = orbits * slots // ROWS
+
+    other = send(panels, CORE)
+    listed, rank = naming(blocks, row_block, capacity)
+    listed_other, rank_other = send(listed, CORE), send(rank, CORE)
+    rest = ((listed, listed_other), (rank, rank_other), (panels, other))
+    gamma = jnp.einsum(
+        "ispm,ism->p", panels.astype(jnp.float32), coeffs, precision=lax.Precision.HIGHEST
+    )
+    gamma = gamma + send(gamma, CORE)
+
+    early_go = partial_rows(Z_FIRST, [z | y for z in Z for y in (Y, 0)], 2, *rest)
+    *early_go, gamma = lax.optimization_barrier((*early_go, gamma))
+    near, far, across = [send(gamma, z) for z in Z]
+    gamma = (gamma + near) + (far + across)
+    early_codes = [send(x, z) for x, z in zip(early_go, Z)]
+    (late_go,) = partial_rows(Y_FIRST, [Y] + [z | Y for z in Z], 4, *rest)
+    late_go, gamma = lax.optimization_barrier((late_go, gamma))
+    gamma = gamma + send(gamma, Y)
+    late_code = send(late_go, Y)
+    (early_stay,) = partial_rows(Z_FIRST, [Y, 0], 0, *rest)
+    (late_stay,) = partial_rows(Y_FIRST, [0, *Z], 0, *rest)
+
+    late_own, *late_turn = turn_z(late_stay, late_code)
+    late_codes = [send(x, z) for x, z in zip(late_turn, Z)]
+    early_turn, early_own = turn_y(early_stay, early_codes)
+    early, *early_back = finish(early_own, [send(early_turn, Y)], 3)
+    early_came = [
+        give_back(early_back[0], 1, 0),
+        give_back(early_back[1], 1, 1),
+        give_back(early_back[2], "extra", 0),
+    ]
+    fitted = jnp.dot(metric_inv, gamma, precision=lax.Precision.HIGHEST)
+    coulomb = jnp.einsum(
+        "p,rpmn->rmn", fitted, three_index.astype(jnp.float32), precision=lax.Precision.HIGHEST
+    )
+    late, *late_back = finish(late_own, late_codes, 4)
+    late_came = [give_back(late_back[2 * k + b], 2 + k, b) for k in range(2) for b in range(2)]
+    exchange = assemble(row_block, early, late, early_came + late_came)
+    return (exchange, coulomb.astype(jnp.bfloat16), fitted)
+
+
 def solution(mesh):
     placed = (
         P(("groups", "row"), None, None, None),
@@ -81,7 +371,7 @@
         P(("groups", "row"), None, None, None),
     )
     return jax.shard_map(
-        per_device,
+        summed_rows if mesh.shape["row"] == ROWS else sent_panels,
         mesh=mesh,
         in_specs=placed,
         out_specs=(P(("groups", "row"), None, None), P(("groups", "row"), None, None), P("groups")),

time: 444 us -> 90.4 us (0.20)
  the two profiles are of different devices: /device:TPU:18 before, /device:TPU:0 now
where the time goes in v2:
time: 90.4 us; the launch traced here: 90.1 us
  starting transfers between devices  32.9 us (36%)
  waiting for transfers between devices  27.2 us (30%)
  Pallas kernels  19.9 us (22%)
  matrix products  4.7 us (5%)
  local copies, waits for them, and re-layouts  3.5 us (4%)
  other arithmetic  1.12 us (1%)
    ppermute x16, waiting for transfers between devices, send(): return lax.ppermute(x, 'row', [(i, i ^ flip) for i in range(ROWS)])  23.6 us
    ppermute x16, starting transfers between devices, send(): return lax.ppermute(x, 'row', [(i, i ^ flip) for i in range(ROWS)])  18.2 us
    pallas_call x4, Pallas kernels, partial_rows(): pl.pallas_call(functools.partial(rows_kernel, group, flips, per_message,...  16.7 us
    ppermute x7, starting transfers between devices, give_back(): return lax.ppermute(block, 'row', [(i, holder(i)) for i in range(ROWS)])  14.7 us
    ppermute x7, waiting for transfers between devices, give_back(): return lax.ppermute(block, 'row', [(i, holder(i)) for i in range(ROWS)])  3.54 us
    unnamed x30, local copies, waits for them, and re-layouts  3.33 us
    dot_general x1, matrix products, summed_rows(): jnp.einsum('ispm,ism->p', panels.astype(jnp.float32), coeffs, precision=l...  2.75 us
    pallas_call x1, Pallas kernels, assemble(): pl.pallas_call(assemble_kernel, in_specs=[pl.BlockSpec(memory_space=pltpu...  2.04 us
  transfers between devices with their start and end apart: 23, of which 9 were waited for; matrix products, arithmetic and copies ran while one was open for 7% of the time, Pallas kernels for 14%

profile of v2, /device:TPU:0, one launch (start us, length us, event | category | flops | bytes accessed | tf_op | source)
XLA Modules:
  0.0 90.1 jit_solution(10946620610370976372)
XLA Ops:
  0.7 0.5 collective-permute-start.2
  1.2 2.8 %convolution_bitcast_fusion = f32[64]{0:T(128)S(1)} fusion(bf16[16,6,64,128]{3,2,1,0:T(8,128)(2,1)} %refs_4_.7, f32[16,6,128,1]{2,0,1,3:T(8,128)} %bitcast.23), kind=kOutput, calls=%fused_computation.2 | convolution fusion | flops 9437184 | bytes 1622272 | tf_op jit(solution)/shard_map/ispm,ism->p/dot_general | solution.py:328
  5.3 0.6 collective-permute-done.refs_1_
  6.4 1.4 %copy-done.1 = bf16[16,6,64,128]{3,2,1,0:T(8,128)(2,1)S(1)} copy-done((bf16[16,6,64,128]{3,2,1,0:T(8,128)(2,1)S(1)}, bf16[16,6,64,128]{3,2,1,0:T(8,128)(2,1)}, u32[]{:S(2)}) %copy-start.1) | copy-done | bytes 1572888
  7.8 5.2 %shard_map.86 = (s16[272,384]{1,0:T(8,128)(2,1)S(1)}, s16[272,384]{1,0:T(8,128)(2,1)S(1)}, s16[272,384]{1,0:T(8,128)(2,1)S(1)}) custom-call(s32[16,6]{1,0:T(8,128)S(1)} %broadcast_add_fusion.refs_0_, s32[16,6]{1,0:T(8,128)S(1)} %collective-permute-done.refs_1_, s32[16,6]{1,0:T(8,128)S(1)} %copy.12.refs_2_, s32[16,6]{1,0:T(8,128)S(1)} %collective-permute-done.1.refs_3_, ...), custom_call_target="tpu_custom_call" | custom-call | flops 1811939328 | bytes 1179648 | tf_op jit(solution)/shard_map/pallas_call | solution.py:191
  12.9 4.8 %collective-permute-start.10 = (f32[64]{0:T(128)S(1)}, f32[64]{0:T(128)S(1)}, u32[]{:S(2)}, u32[]{:S(2)}) collective-permute-start(f32[64]{0:T(128)S(1)} %add.43), channel_id=1, source_target_pairs={{0,12},{1,13},{2,14},{3,15},{4,8},{5,9},{6,10},{7,11},{8,4},{9,5},... | collective-permute-start | bytes 776 | tf_op jit(solution)/shard_map/ppermute | solution.py:86
  17.7 0.6 collective-permute-start.8
  18.4 4.5 %shard_map.90 = s16[528,768]{1,0:T(8,128)(2,1)S(1)} custom-call(s32[16,6]{1,0:T(8,128)S(1)} %broadcast_add_fusion.refs_0_, s32[16,6]{1,0:T(8,128)S(1)} %collective-permute-done.refs_1_, s32[16,6]{1,0:T(8,128)S(1)} %copy.12.refs_2_, s32[16,6]{1,0:T(8,128)S(1)} %collective-permute-done.1.refs_3_, bf16[16,6,64,128]{3,2,1,0:T(8,128)(2,1)S(1)} %copy-done.1, ...), custom_call_target="tpu_custom_call" | custom-call | flops 2415919104 | bytes 1572864 | tf_op jit(solution)/shard_map/pallas_call | solution.py:191
  22.9 1.7 %collective-permute-start.11 = (s16[528,768]{1,0:T(8,128)(2,1)S(1)}, s16[528,768]{1,0:T(8,128)(2,1)S(1)}, u32[]{:S(2)}, u32[]{:S(2)}) collective-permute-start(s16[528,768]{1,0:T(8,128)(2,1)S(1)} %shard_map.90), channel_id=1, source_target_pairs={{0,2},{1,3},{2,0},{3,1},{4,6},{5,7},{6,4},{7,5},{8,10},{9,11},{10,... | collective-permute-start | bytes 2433032 | tf_op jit(solution)/shard_map/ppermute | solution.py:86
  24.6 1.2 %collective-permute-start.4 = (s16[272,384]{1,0:T(8,128)(2,1)S(1)}, s16[272,384]{1,0:T(8,128)(2,1)S(1)}, u32[]{:S(2)}, u32[]{:S(2)}) collective-permute-start(s16[272,384]{1,0:T(8,128)(2,1)S(1)} %get-tuple-element.30), channel_id=1, source_target_pairs={{0,4},{1,5},{2,6},{3,7},{4,0},{5,1},{6,2},{7,3},{8,12},{9,13},{10,... | collective-permute-start | bytes 626696 | tf_op jit(solution)/shard_map/ppermute | solution.py:86
  25.8 2.9 %collective-permute-start.5 = (s16[272,384]{1,0:T(8,128)(2,1)S(1)}, s16[272,384]{1,0:T(8,128)(2,1)S(1)}, u32[]{:S(2)}, u32[]{:S(2)}) collective-permute-start(s16[272,384]{1,0:T(8,128)(2,1)S(1)} %get-tuple-element.31), channel_id=1, source_target_pairs={{0,8},{1,9},{2,10},{3,11},{4,12},{5,13},{6,14},{7,15},{8,0},{9,1},... | collective-permute-start | bytes 626696 | tf_op jit(solution)/shard_map/ppermute | solution.py:86
  29.0 2.7 %shard_map.85.stay = f32[2,128,384]{2,1,0:T(8,128)S(1)} custom-call(s32[16,6]{1,0:T(8,128)S(1)} %broadcast_add_fusion.refs_0_, s32[16,6]{1,0:T(8,128)S(1)} %collective-permute-done.refs_1_, s32[16,6]{1,0:T(8,128)S(1)} %copy.12.refs_2_, s32[16,6]{1,0:T(8,128)S(1)} %collective-permute-done.1.refs_3_, bf16[16,6,64,128]{3,2,1,0:T(8,128)(2,1)S(1)} %copy-done.1, ...), custom_call_target="tpu_custom_call" | custom-call | flops 603979776 | bytes 393216 | tf_op jit(solution)/shard_map/pallas_call | solution.py:191
  31.7 4.3 %shard_map.89.stay = f32[4,128,768]{2,1,0:T(8,128)S(1)} custom-call(s32[16,6]{1,0:T(8,128)S(1)} %broadcast_add_fusion.refs_0_, s32[16,6]{1,0:T(8,128)S(1)} %collective-permute-done.refs_1_, s32[16,6]{1,0:T(8,128)S(1)} %copy.12.refs_2_, s32[16,6]{1,0:T(8,128)S(1)} %collective-permute-done.1.refs_3_, bf16[16,6,64,128]{3,2,1,0:T(8,128)(2,1)S(1)} %copy-done.1, ...), custom_call_target="tpu_custom_call" | custom-call | flops 2415919104 | bytes 1572864 | tf_op jit(solution)/shard_map/pallas_call | solution.py:191
  36.1 0.4 collective-permute-start.22
  36.5 7.3 %collective-permute-done.5.refs_1_ = s16[272,384]{1,0:T(8,128)(2,1)S(1)} collective-permute-done((s16[272,384]{1,0:T(8,128)(2,1)S(1)}, s16[272,384]{1,0:T(8,128)(2,1)S(1)}, u32[]{:S(2)}, u32[]{:S(2)}) %collective-permute-start.5) | collective-permute-done | bytes 208928 | tf_op jit(solution)/shard_map/ppermute | solution.py:86
  44.2 0.6 collective-permute-start.7
  45.0 4.1 %collective-permute-done.7.refs_0_ = s16[144,384]{1,0:T(8,128)(2,1)S(1)} collective-permute-done((s16[144,384]{1,0:T(8,128)(2,1)S(1)}, s16[144,384]{1,0:T(8,128)(2,1)S(1)}, u32[]{:S(2)}, u32[]{:S(2)}) %collective-permute-start.7) | collective-permute-done | bytes 110624 | tf_op jit(solution)/shard_map/ppermute | solution.py:86
  49.2 0.6 copy-done.3
  49.8 3.3 %collective-permute-start.15 = (bf16[128,128]{1,0:T(8,128)(2,1)S(1)}, bf16[128,128]{1,0:T(8,128)(2,1)S(1)}, u32[]{:S(2)}, u32[]{:S(2)}) collective-permute-start(bf16[128,128]{1,0:T(8,128)(2,1)S(1)} %get-tuple-element.43), channel_id=1, source_target_pairs={{0,4},{1,5},{2,6},{3,7},{4,1},{5,0},{6,3},{7,2},{8,12},{9,13},{10,... | collective-permute-start | bytes 98312 | tf_op jit(solution)/shard_map/ppermute | solution.py:266
  53.6 1.0 %collective-permute-start.13 = (s16[144,768]{1,0:T(8,128)(2,1)S(1)}, s16[144,768]{1,0:T(8,128)(2,1)S(1)}, u32[]{:S(2)}, u32[]{:S(2)}) collective-permute-start(s16[144,768]{1,0:T(8,128)(2,1)S(1)} %get-tuple-element.40), channel_id=1, source_target_pairs={{0,8},{1,9},{2,10},{3,11},{4,12},{5,13},{6,14},{7,15},{8,0},{9,1},... | collective-permute-start | bytes 663560 | tf_op jit(solution)/shard_map/ppermute | solution.py:86
  54.6 3.4 %collective-permute-start.14 = (s16[144,768]{1,0:T(8,128)(2,1)S(1)}, s16[144,768]{1,0:T(8,128)(2,1)S(1)}, u32[]{:S(2)}, u32[]{:S(2)}) collective-permute-start(s16[144,768]{1,0:T(8,128)(2,1)S(1)} %get-tuple-element.41), channel_id=1, source_target_pairs={{0,12},{1,13},{2,14},{3,15},{4,8},{5,9},{6,10},{7,11},{8,4},{9,5},... | collective-permute-start | bytes 663560 | tf_op jit(solution)/shard_map/ppermute | solution.py:86
  58.0 1.8 %fusion = f32[1,128,128]{2,0,1:T(1,128)S(1)} fusion(bf16[64,128,128]{2,1,0:T(8,128)(2,1)S(1)} %bitcast.20, f32[1,64]{1,0:T(1,128)S(1)} %fusion.13), kind=kOutput, calls=%fused_computation | convolution fusion | flops 12582912 | bytes 2162944 | tf_op jit(solution)/shard_map/p,rpmn->rmn/dot_general | solution.py:355
  59.8 5.6 %collective-permute-done.12.refs_0_ = s16[144,768]{1,0:T(8,128)(2,1)S(1)} collective-permute-done((s16[144,768]{1,0:T(8,128)(2,1)S(1)}, s16[144,768]{1,0:T(8,128)(2,1)S(1)}, u32[]{:S(2)}, u32[]{:S(2)}) %collective-permute-start.12) | collective-permute-done | bytes 221216 | tf_op jit(solution)/shard_map/ppermute | solution.py:86
  65.4 5.7 %collective-permute-done.14.refs_2_ = s16[144,768]{1,0:T(8,128)(2,1)S(1)} collective-permute-done((s16[144,768]{1,0:T(8,128)(2,1)S(1)}, s16[144,768]{1,0:T(8,128)(2,1)S(1)}, u32[]{:S(2)}, u32[]{:S(2)}) %collective-permute-start.14) | collective-permute-done | bytes 221216 | tf_op jit(solution)/shard_map/ppermute | solution.py:86
  71.3 0.7 copy-done.2
  71.9 7.0 %collective-permute-start.18 = (bf16[128,128]{1,0:T(8,128)(2,1)S(1)}, bf16[128,128]{1,0:T(8,128)(2,1)S(1)}, u32[]{:S(2)}, u32[]{:S(2)}) collective-permute-start(bf16[128,128]{1,0:T(8,128)(2,1)S(1)} %get-tuple-element.46), channel_id=1, source_target_pairs={{0,8},{1,9},{2,10},{3,11},{4,12},{5,13},{6,14},{7,15},{8,1},{9,0},... | collective-permute-start | bytes 98312 | tf_op jit(solution)/shard_map/ppermute | solution.py:266
  79.0 2.3 %collective-permute-start.20 = (bf16[128,128]{1,0:T(8,128)(2,1)S(1)}, bf16[128,128]{1,0:T(8,128)(2,1)S(1)}, u32[]{:S(2)}, u32[]{:S(2)}) collective-permute-start(bf16[128,128]{1,0:T(8,128)(2,1)S(1)} %get-tuple-element.48), channel_id=1, source_target_pairs={{0,12},{1,13},{2,14},{3,15},{4,9},{5,8},{6,11},{7,10},{8,4},{9,5},... | collective-permute-start | bytes 98312 | tf_op jit(solution)/shard_map/ppermute | solution.py:266
  81.3 2.0 %collective-permute-start.21 = (bf16[128,128]{1,0:T(8,128)(2,1)S(1)}, bf16[128,128]{1,0:T(8,128)(2,1)S(1)}, u32[]{:S(2)}, u32[]{:S(2)}) collective-permute-start(bf16[128,128]{1,0:T(8,128)(2,1)S(1)} %get-tuple-element.49), channel_id=1, source_target_pairs={{0,14},{1,15},{2,12},{3,13},{4,11},{5,10},{6,9},{7,8},{8,6},{9,7},... | collective-permute-start | bytes 98312 | tf_op jit(solution)/shard_map/ppermute | solution.py:266
  83.3 0.6 convert_bitcast_fusion
  84.4 3.1 %collective-permute-done.21.refs_6_ = bf16[128,128]{1,0:T(8,128)(2,1)S(1)} collective-permute-done((bf16[128,128]{1,0:T(8,128)(2,1)S(1)}, bf16[128,128]{1,0:T(8,128)(2,1)S(1)}, u32[]{:S(2)}, u32[]{:S(2)}) %collective-permute-start.21) | collective-permute-done | bytes 32800 | tf_op jit(solution)/shard_map/ppermute | solution.py:266
  87.5 0.6 copy-done.11
  88.1 2.0 %shard_map.93 = bf16[1,128,2048]{2,1,0:T(8,128)(2,1)} custom-call(s32[16]{0:T(128)} %holders.1, bf16[128,384]{1,0:T(8,128)(2,1)} %copy-done.3, bf16[128,768]{1,0:T(8,128)(2,1)} %copy-done.2, bf16[128,128]{1,0:T(8,128)(2,1)} %copy-done.5, bf16[128,128]{1,0:T(8,128)(2,1)} %copy-done.6, bf16[128,128]{1,0:T(8,128)(2,1)} %copy-done.7, ...), custom_call_target="tpu_custom_call" | custom-call | tf_op jit(solution)/shard_map/pallas_call | solution.py:297
  (70 shorter events, 3.9 us)
Async XLA Ops:
  0.6 57.3 %copy-start = (bf16[1,64,128,128]{3,2,1,0:T(8,128)(2,1)S(1)}, bf16[1,64,128,128]{3,2,1,0:T(8,128)(2,1)}, u32[]{:S(2)}) copy-start(bf16[1,64,128,128]{3,2,1,0:T(8,128)(2,1)} %param.11) | copy-start | bytes 6291460
  0.6 3.5 %copy-start.14 = (s32[16]{0:T(128)S(1)}, s32[16]{0:T(128)}, u32[]{:S(2)}) copy-start(s32[16]{0:T(128)} %holders.1) | copy-start | bytes 196
  0.7 3.5 %copy-start.12 = (s32[16,6]{0,1:T(8,128)S(1)}, s32[16,6]{0,1:T(8,128)}, u32[]{:S(2)}) copy-start(s32[16,6]{0,1:T(8,128)} %param.7) | copy-start | bytes 1156
  0.7 5.7 %collective-permute-start.2 = (bf16[16,6,64,128]{3,2,1,0:T(8,128)(2,1)}, bf16[16,6,64,128]{3,2,1,0:T(8,128)(2,1)}, u32[]{:S(2)}, u32[]{:S(2)}) collective-permute-start(bf16[16,6,64,128]{3,2,1,0:T(8,128)(2,1)} %refs_4_.7), channel_id=1, source_target_pairs={{0,1},{1,0},{2,3},{3,2},{4,5},{5,4},{6,7},{7,6},{8,9},{9,8},{10,11... | collective-permute-start | bytes 4718600 | tf_op jit(solution)/shard_map/ppermute | solution.py:86
  3.9 1.4 %collective-permute-start.3 = (f32[64]{0:T(128)S(1)}, f32[64]{0:T(128)S(1)}, u32[]{:S(2)}, u32[]{:S(2)}) collective-permute-start(f32[64]{0:T(128)S(1)} %convolution_bitcast_fusion), channel_id=1, source_target_pairs={{0,1},{1,0},{2,3},{3,2},{4,5},{5,4},{6,7},{7,6},{8,9},{9,8},{10,11... | collective-permute-start | bytes 776 | tf_op jit(solution)/shard_map/ppermute | solution.py:86
  4.7 1.2 %collective-permute-start = (s32[16,6]{1,0:T(8,128)S(1)}, s32[16,6]{1,0:T(8,128)S(1)}, u32[]{:S(2)}, u32[]{:S(2)}) collective-permute-start(s32[16,6]{1,0:T(8,128)S(1)} %broadcast_add_fusion.refs_0_), channel_id=1, source_target_pairs={{0,1},{1,0},{2,3},{3,2},{4,5},{5,4},{6,7},{7,6},{8,9},{9,8},{10,11... | collective-permute-start | bytes 1160 | tf_op jit(solution)/shard_map/ppermute | solution.py:86
  5.2 1.2 %collective-permute-start.1 = (s32[16,6]{1,0:T(8,128)S(1)}, s32[16,6]{1,0:T(8,128)S(1)}, u32[]{:S(2)}, u32[]{:S(2)}) collective-permute-start(s32[16,6]{1,0:T(8,128)S(1)} %copy.12.refs_2_), channel_id=1, source_target_pairs={{0,1},{1,0},{2,3},{3,2},{4,5},{5,4},{6,7},{7,6},{8,9},{9,8},{10,11... | collective-permute-start | bytes 1160 | tf_op jit(solution)/shard_map/ppermute | solution.py:86
  12.9 9.9 %collective-permute-start.10 = (f32[64]{0:T(128)S(1)}, f32[64]{0:T(128)S(1)}, u32[]{:S(2)}, u32[]{:S(2)}) collective-permute-start(f32[64]{0:T(128)S(1)} %add.43), channel_id=1, source_target_pairs={{0,12},{1,13},{2,14},{3,15},{4,8},{5,9},{6,10},{7,11},{8,4},{9,5},... | collective-permute-start | bytes 776 | tf_op jit(solution)/shard_map/ppermute | solution.py:86
  17.7 5.1 %collective-permute-start.9 = (f32[64]{0:T(128)S(1)}, f32[64]{0:T(128)S(1)}, u32[]{:S(2)}, u32[]{:S(2)}) collective-permute-start(f32[64]{0:T(128)S(1)} %add.43), channel_id=1, source_target_pairs={{0,8},{1,9},{2,10},{3,11},{4,12},{5,13},{6,14},{7,15},{8,0},{9,1},... | collective-permute-start | bytes 776 | tf_op jit(solution)/shard_map/ppermute | solution.py:86
  17.7 5.1 %collective-permute-start.8 = (f32[64]{0:T(128)S(1)}, f32[64]{0:T(128)S(1)}, u32[]{:S(2)}, u32[]{:S(2)}) collective-permute-start(f32[64]{0:T(128)S(1)} %add.43), channel_id=1, source_target_pairs={{0,4},{1,5},{2,6},{3,7},{4,0},{5,1},{6,2},{7,3},{8,12},{9,13},{10,... | collective-permute-start | bytes 776 | tf_op jit(solution)/shard_map/ppermute | solution.py:86
  22.9 30.2 %collective-permute-start.11 = (s16[528,768]{1,0:T(8,128)(2,1)S(1)}, s16[528,768]{1,0:T(8,128)(2,1)S(1)}, u32[]{:S(2)}, u32[]{:S(2)}) collective-permute-start(s16[528,768]{1,0:T(8,128)(2,1)S(1)} %shard_map.90), channel_id=1, source_target_pairs={{0,2},{1,3},{2,0},{3,1},{4,6},{5,7},{6,4},{7,5},{8,10},{9,11},{10,... | collective-permute-start | bytes 2433032 | tf_op jit(solution)/shard_map/ppermute | solution.py:86
  24.6 11.9 %collective-permute-start.4 = (s16[272,384]{1,0:T(8,128)(2,1)S(1)}, s16[272,384]{1,0:T(8,128)(2,1)S(1)}, u32[]{:S(2)}, u32[]{:S(2)}) collective-permute-start(s16[272,384]{1,0:T(8,128)(2,1)S(1)} %get-tuple-element.30), channel_id=1, source_target_pairs={{0,4},{1,5},{2,6},{3,7},{4,0},{5,1},{6,2},{7,3},{8,12},{9,13},{10,... | collective-permute-start | bytes 626696 | tf_op jit(solution)/shard_map/ppermute | solution.py:86
  25.8 18.0 %collective-permute-start.5 = (s16[272,384]{1,0:T(8,128)(2,1)S(1)}, s16[272,384]{1,0:T(8,128)(2,1)S(1)}, u32[]{:S(2)}, u32[]{:S(2)}) collective-permute-start(s16[272,384]{1,0:T(8,128)(2,1)S(1)} %get-tuple-element.31), channel_id=1, source_target_pairs={{0,8},{1,9},{2,10},{3,11},{4,12},{5,13},{6,14},{7,15},{8,0},{9,1},... | collective-permute-start | bytes 626696 | tf_op jit(solution)/shard_map/ppermute | solution.py:86
  28.7 15.0 %collective-permute-start.6 = (s16[272,384]{1,0:T(8,128)(2,1)S(1)}, s16[272,384]{1,0:T(8,128)(2,1)S(1)}, u32[]{:S(2)}, u32[]{:S(2)}) collective-permute-start(s16[272,384]{1,0:T(8,128)(2,1)S(1)} %get-tuple-element.32), channel_id=1, source_target_pairs={{0,12},{1,13},{2,14},{3,15},{4,8},{5,9},{6,10},{7,11},{8,4},{9,5},... | collective-permute-start | bytes 626696 | tf_op jit(solution)/shard_map/ppermute | solution.py:86
  31.7 13.1 %copy-start.4 = (f32[64,64]{1,0:T(8,128)S(1)}, f32[64,64]{1,0:T(8,128)}, u32[]{:S(2)}) copy-start(f32[64,64]{1,0:T(8,128)} %param.10) | copy-start | bytes 49156
  36.1 8.8 %collective-permute-start.22 = (f32[64]{0:T(128)S(1)}, f32[64]{0:T(128)S(1)}, u32[]{:S(2)}, u32[]{:S(2)}) collective-permute-start(f32[64]{0:T(128)S(1)} %add_add_fusion.1), channel_id=1, source_target_pairs={{0,2},{1,3},{2,0},{3,1},{4,6},{5,7},{6,4},{7,5},{8,10},{9,11},{10,... | collective-permute-start | bytes 776 | tf_op jit(solution)/shard_map/ppermute | solution.py:86
  44.2 4.8 %collective-permute-start.7 = (s16[144,384]{1,0:T(8,128)(2,1)S(1)}, s16[144,384]{1,0:T(8,128)(2,1)S(1)}, u32[]{:S(2)}, u32[]{:S(2)}) collective-permute-start(s16[144,384]{1,0:T(8,128)(2,1)S(1)} %get-tuple-element.34), channel_id=1, source_target_pairs={{0,2},{1,3},{2,0},{3,1},{4,6},{5,7},{6,4},{7,5},{8,10},{9,11},{10,... | collective-permute-start | bytes 331784 | tf_op jit(solution)/shard_map/ppermute | solution.py:86
  45.0 14.8 %copy-start.13 = (f32[1,64]{1,0:T(1,128)}, f32[1,64]{1,0:T(1,128)S(1)}, u32[]{:S(2)}) copy-start(f32[1,64]{1,0:T(1,128)S(1)} %fusion.13) | copy-start | bytes 772
  49.8 29.2 %collective-permute-start.15 = (bf16[128,128]{1,0:T(8,128)(2,1)S(1)}, bf16[128,128]{1,0:T(8,128)(2,1)S(1)}, u32[]{:S(2)}, u32[]{:S(2)}) collective-permute-start(bf16[128,128]{1,0:T(8,128)(2,1)S(1)} %get-tuple-element.43), channel_id=1, source_target_pairs={{0,4},{1,5},{2,6},{3,7},{4,1},{5,0},{6,3},{7,2},{8,12},{9,13},{10,... | collective-permute-start | bytes 98312 | tf_op jit(solution)/shard_map/ppermute | solution.py:266
  53.1 28.2 %collective-permute-start.16 = (bf16[128,128]{1,0:T(8,128)(2,1)S(1)}, bf16[128,128]{1,0:T(8,128)(2,1)S(1)}, u32[]{:S(2)}, u32[]{:S(2)}) collective-permute-start(bf16[128,128]{1,0:T(8,128)(2,1)S(1)} %get-tuple-element.44), channel_id=1, source_target_pairs={{0,6},{1,7},{2,4},{3,5},{4,3},{5,2},{6,1},{7,0},{8,14},{9,15},{10,... | collective-permute-start | bytes 98312 | tf_op jit(solution)/shard_map/ppermute | solution.py:266
  53.5 11.8 %collective-permute-start.12 = (s16[144,768]{1,0:T(8,128)(2,1)S(1)}, s16[144,768]{1,0:T(8,128)(2,1)S(1)}, u32[]{:S(2)}, u32[]{:S(2)}) collective-permute-start(s16[144,768]{1,0:T(8,128)(2,1)S(1)} %get-tuple-element.39), channel_id=1, source_target_pairs={{0,4},{1,5},{2,6},{3,7},{4,0},{5,1},{6,2},{7,3},{8,12},{9,13},{10,... | collective-permute-start | bytes 663560 | tf_op jit(solution)/shard_map/ppermute | solution.py:86
  53.6 11.8 %collective-permute-start.13 = (s16[144,768]{1,0:T(8,128)(2,1)S(1)}, s16[144,768]{1,0:T(8,128)(2,1)S(1)}, u32[]{:S(2)}, u32[]{:S(2)}) collective-permute-start(s16[144,768]{1,0:T(8,128)(2,1)S(1)} %get-tuple-element.40), channel_id=1, source_target_pairs={{0,8},{1,9},{2,10},{3,11},{4,12},{5,13},{6,14},{7,15},{8,0},{9,1},... | collective-permute-start | bytes 663560 | tf_op jit(solution)/shard_map/ppermute | solution.py:86
  54.6 16.5 %collective-permute-start.14 = (s16[144,768]{1,0:T(8,128)(2,1)S(1)}, s16[144,768]{1,0:T(8,128)(2,1)S(1)}, u32[]{:S(2)}, u32[]{:S(2)}) collective-permute-start(s16[144,768]{1,0:T(8,128)(2,1)S(1)} %get-tuple-element.41), channel_id=1, source_target_pairs={{0,12},{1,13},{2,14},{3,15},{4,8},{5,9},{6,10},{7,11},{8,4},{9,5},... | collective-permute-start | bytes 663560 | tf_op jit(solution)/shard_map/ppermute | solution.py:86
  65.4 18.6 %collective-permute-start.17 = (bf16[128,128]{1,0:T(8,128)(2,1)S(1)}, bf16[128,128]{1,0:T(8,128)(2,1)S(1)}, u32[]{:S(2)}, u32[]{:S(2)}) collective-permute-start(bf16[128,128]{1,0:T(8,128)(2,1)S(1)} %get-tuple-element.45), channel_id=1, source_target_pairs={{0,1},{1,2},{2,3},{3,0},{4,5},{5,6},{6,7},{7,4},{8,9},{9,10},{10,1... | collective-permute-start | bytes 98312 | tf_op jit(solution)/shard_map/ppermute | solution.py:266
  71.9 12.0 %collective-permute-start.18 = (bf16[128,128]{1,0:T(8,128)(2,1)S(1)}, bf16[128,128]{1,0:T(8,128)(2,1)S(1)}, u32[]{:S(2)}, u32[]{:S(2)}) collective-permute-start(bf16[128,128]{1,0:T(8,128)(2,1)S(1)} %get-tuple-element.46), channel_id=1, source_target_pairs={{0,8},{1,9},{2,10},{3,11},{4,12},{5,13},{6,14},{7,15},{8,1},{9,0},... | collective-permute-start | bytes 98312 | tf_op jit(solution)/shard_map/ppermute | solution.py:266
  79.0 5.3 %collective-permute-start.19 = (bf16[128,128]{1,0:T(8,128)(2,1)S(1)}, bf16[128,128]{1,0:T(8,128)(2,1)S(1)}, u32[]{:S(2)}, u32[]{:S(2)}) collective-permute-start(bf16[128,128]{1,0:T(8,128)(2,1)S(1)} %get-tuple-element.47), channel_id=1, source_target_pairs={{0,10},{1,11},{2,8},{3,9},{4,14},{5,15},{6,12},{7,13},{8,3},{9,2},... | collective-permute-start | bytes 98312 | tf_op jit(solution)/shard_map/ppermute | solution.py:266
  79.0 8.5 %copy-start.5 = (bf16[128,128]{1,0:T(8,128)(2,1)}, bf16[128,128]{1,0:T(8,128)(2,1)S(1)}, u32[]{:S(2)}) copy-start(bf16[128,128]{1,0:T(8,128)(2,1)S(1)} %collective-permute-done.15.refs_0_) | copy-start | bytes 98308
  79.0 5.4 %collective-permute-start.20 = (bf16[128,128]{1,0:T(8,128)(2,1)S(1)}, bf16[128,128]{1,0:T(8,128)(2,1)S(1)}, u32[]{:S(2)}, u32[]{:S(2)}) collective-permute-start(bf16[128,128]{1,0:T(8,128)(2,1)S(1)} %get-tuple-element.48), channel_id=1, source_target_pairs={{0,12},{1,13},{2,14},{3,15},{4,9},{5,8},{6,11},{7,10},{8,4},{9,5},... | collective-permute-start | bytes 98312 | tf_op jit(solution)/shard_map/ppermute | solution.py:266
  81.3 6.2 %copy-start.6 = (bf16[128,128]{1,0:T(8,128)(2,1)}, bf16[128,128]{1,0:T(8,128)(2,1)S(1)}, u32[]{:S(2)}) copy-start(bf16[128,128]{1,0:T(8,128)(2,1)S(1)} %collective-permute-done.16.refs_1_) | copy-start | bytes 98308
  81.3 6.2 %collective-permute-start.21 = (bf16[128,128]{1,0:T(8,128)(2,1)S(1)}, bf16[128,128]{1,0:T(8,128)(2,1)S(1)}, u32[]{:S(2)}, u32[]{:S(2)}) collective-permute-start(bf16[128,128]{1,0:T(8,128)(2,1)S(1)} %get-tuple-element.49), channel_id=1, source_target_pairs={{0,14},{1,15},{2,12},{3,13},{4,11},{5,10},{6,9},{7,8},{8,6},{9,7},... | collective-permute-start | bytes 98312 | tf_op jit(solution)/shard_map/ppermute | solution.py:266
  83.9 3.6 %copy-start.7 = (bf16[128,128]{1,0:T(8,128)(2,1)}, bf16[128,128]{1,0:T(8,128)(2,1)S(1)}, u32[]{:S(2)}) copy-start(bf16[128,128]{1,0:T(8,128)(2,1)S(1)} %collective-permute-done.17.refs_2_) | copy-start | bytes 98308
  83.9 3.6 %copy-start.8 = (bf16[128,128]{1,0:T(8,128)(2,1)}, bf16[128,128]{1,0:T(8,128)(2,1)S(1)}, u32[]{:S(2)}) copy-start(bf16[128,128]{1,0:T(8,128)(2,1)S(1)} %collective-permute-done.18.refs_3_) | copy-start | bytes 98308
  (6 other events, 9.7 us)

commit v3 on v2

--- a/solution.py
+++ b/solution.py
@@ -77,9 +77,12 @@
 ROWS = 16
 CORE, Y, Z = 1, 2, (4, 8, 12)
 PLACES = 16
-Z_FIRST, Y_FIRST = (1, "extra"), (2, 3, 0)
+Z_FIRST, Y_FIRST = (3, "extra"), (1, 2, 0)
 TAIL = 16
 TOP = 14.99
+VECTOR = 8
+AHEAD = 6
+SHORT = pl.CostEstimate(flops=1024, bytes_accessed=1024, transcendentals=0)
 
 
 def send(x, flip):
@@ -106,17 +109,37 @@
     return 1 if region == "extra" else 2
 
 
-def encode(out, sums):
+def encode(out, sums, vector=()):
     height, columns = sums[0].shape
     line = lax.broadcasted_iota(jnp.int32, (TAIL, columns), 0)
-    exponents = jnp.zeros((TAIL, columns), jnp.float32)
+    tail = jnp.zeros((TAIL, columns), jnp.float32)
     for j, x in enumerate(sums):
         peak = jnp.maximum(jnp.max(jnp.abs(x), axis=0, keepdims=True), 2.0**-100)
         exponent = jnp.ceil(jnp.log2(peak) * 8)
         scaled = jnp.round(x * jnp.exp2(TOP - exponent * 0.125))
         out[j * height : (j + 1) * height, :] = scaled.astype(jnp.int32).astype(jnp.int16)
-        exponents = jnp.where(line == j, exponent, exponents)
-    out[len(sums) * height :, :] = exponents.astype(jnp.int32).astype(jnp.int16)
+        tail = jnp.where(line == j, exponent, tail)
+    for j, x in enumerate(vector):
+        rest = jnp.zeros((1, columns - x.shape[1]), jnp.float32)
+        tail = jnp.where(line == VECTOR + j, jnp.concatenate([x, rest], axis=1), tail)
+    out[len(sums) * height :, :] = tail.astype(jnp.int32).astype(jnp.int16)
+
+
+def encode_vector(x):
+    exponent = jnp.ceil(jnp.log2(jnp.maximum(jnp.abs(x), 2.0**-100)))
+    scaled = x * jnp.exp2(14 - exponent)
+    high = jnp.round(scaled)
+    low = jnp.round((scaled - high) * 2.0**15)
+    return (exponent, high, low), combine(exponent, high, low)
+
+
+def combine(exponent, high, low):
+    return (high + low * 2.0**-15) * jnp.exp2(exponent - 14)
+
+
+def decode_vector(codes, width):
+    tail = codes[codes.shape[0] - TAIL :, :width].astype(jnp.int32).astype(jnp.float32)
+    return combine(*(tail[VECTOR + j : VECTOR + j + 1, :] for j in range(3)))
 
 
 def decode(codes, j, height):
@@ -126,35 +149,61 @@
     return codes[j * height : (j + 1) * height, :].astype(jnp.int32).astype(jnp.float32) * scale
 
 
-def rows_kernel(group, flips, per_message, sides, *refs):
-    lists, ranks, panels = refs[:sides], refs[sides : 2 * sides], refs[2 * sides : 3 * sides]
-    outs, picks, spreads = refs[3 * sides : -4], refs[-4:-2], refs[-2:]
-    orbits, slots, aux, width = panels[0].shape
-    capacity = lists[0].shape[1]
+def rows_kernel(jobs, project, listed, ranks, listed_other, ranks_other, mine, other_far, *refs):
+    if project:
+        coeffs, refs = refs[0], refs[1:]
+    outs, (other, arrived), picks, spreads = refs[: -2 * AHEAD - 2], refs[-2:], refs[-2 * AHEAD - 2 : -AHEAD - 2], refs[-AHEAD - 2 : -2]
+    orbits, slots, aux, width = mine.shape
+    capacity = listed.shape[1]
     me = lax.axis_index("row")
-    gathered = []
-
-    for j, flip in enumerate(flips):
-        row = me ^ flip
-        row_rank = swap_low(row)
-        picked, spread = picks[j % 2], spreads[j % 2]
-        spans = [
-            pl.ds(pl.multiple_of(first_place(row, region) * width, width), width_of(region) * width)
+    copy = pltpu.make_async_copy(other_far, other, arrived)
+    copy.start()
+    todo = [(job, j) for job in range(len(jobs)) for j in range(len(jobs[job][1]))]
+
+    def spans_of(job, j):
+        group, flips, _ = jobs[job]
+        return [
+            pl.ds(pl.multiple_of(first_place(me ^ flips[j], region) * width, width), width_of(region) * width)
             for region in group
         ]
-        for span in spans:
-            spread[:, span] = jnp.zeros((spread.shape[0], span.size), jnp.bfloat16)
-        for side in range(sides):
-            for n in range(capacity):
-                code = lists[side][row, n]
-                orbit, slot = jnp.maximum(code, 0) >> 3, jnp.maximum(code, 0) & 7
-                at = pl.ds((side * capacity + n) * aux, aux)
-                chosen = panels[side][orbit, slot]
-                tiles = [panels[side][orbit, t] for t in range(slots)]
-                places = [ranks[side][orbit, t] ^ row_rank for t in range(slots)]
-                picked[at, :] = jnp.where(code >= 0, chosen, jnp.zeros_like(chosen))
-                for tile, place in zip(tiles, places):
-                    spread[at, pl.ds(pl.multiple_of(place * width, width), width)] = tile
+
+    def gather(step, side):
+        job, j = todo[step]
+        row = me ^ jobs[job][1][j]
+        row_rank = swap_low(row)
+        picked, spread = picks[step % AHEAD], spreads[step % AHEAD]
+        names, places_of, panels = ((listed, ranks, mine), (listed_other, ranks_other, other))[side]
+        half = capacity * aux
+        for span in spans_of(job, j):
+            spread[side * half : (side + 1) * half, span] = jnp.zeros((half, span.size), jnp.bfloat16)
+        for n in range(capacity):
+            code = names[row, n]
+            orbit, slot = jnp.maximum(code, 0) >> 3, jnp.maximum(code, 0) & 7
+            at = pl.ds((side * capacity + n) * aux, aux)
+            chosen = panels[orbit, slot]
+            tiles = [panels[orbit, t] for t in range(slots)]
+            places = [places_of[orbit, t] ^ row_rank for t in range(slots)]
+            picked[at, :] = jnp.where(code >= 0, chosen, jnp.zeros_like(chosen))
+            for tile, place in zip(tiles, places):
+                spread[at, pl.ds(pl.multiple_of(place * width, width), width)] = tile
+
+    for step in range(min(AHEAD, len(todo))):
+        gather(step, 0)
+    vector = ()
+    if project:
+        total = jnp.zeros((aux, width), jnp.float32)
+        for i in range(orbits):
+            for t in range(slots):
+                total = total + mine[i, t].astype(jnp.float32) * coeffs[i, t : t + 1, :]
+        total = jnp.sum(total.T, axis=0, keepdims=True)
+        total = jnp.concatenate([total, jnp.zeros((1, width - aux), jnp.float32)], axis=1)
+        vector, kept = encode_vector(total)
+        outs[-1][...] = jnp.broadcast_to(kept, outs[-1].shape)
+    copy.wait()
+    first, gathered = 0, []
+    for step, (job, j) in enumerate(todo):
+        gather(step, 1)
+        picked, spread = picks[step % AHEAD], spreads[step % AHEAD]
         sums = [
             lax.dot_general(
                 picked[...],
@@ -162,82 +211,102 @@
                 (((0,), (0,)), ((), ())),
                 preferred_element_type=jnp.float32,
             )
-            for span in spans
+            for span in spans_of(job, j)
         ]
+        if step + AHEAD < len(todo):
+            gather(step + AHEAD, 0)
+        group, flips, per_message = jobs[job]
         if per_message:
             gathered.append(jnp.concatenate(sums, axis=1))
             if len(gathered) == per_message:
-                encode(outs[j // per_message], gathered)
-                gathered = []
+                encode(outs[first], gathered, vector if job + 1 == len(jobs) else ())
+                first, gathered = first + 1, []
         else:
             at = 0
             for x in sums:
-                outs[0][j, :, at : at + x.shape[1]] = x
+                outs[first][j, :, at : at + x.shape[1]] = x
                 at += x.shape[1]
-
-
-def partial_rows(group, flips, per_message, lists, ranks, panels):
+            first += j + 1 == len(flips)
+
+
+def partial_rows(jobs, lists, ranks, panels, *coeffs):
     orbits, slots, aux, width = panels[0].shape
-    capacity, sides = lists[0].shape[1], len(panels)
-    columns = sum(width_of(region) for region in group) * width
-    depth = sides * capacity * aux
-    if per_message:
-        message = jax.ShapeDtypeStruct((per_message * width + TAIL, columns), jnp.int16)
-        shapes = [message] * (len(flips) // per_message)
-    else:
-        shapes = [jax.ShapeDtypeStruct((len(flips), width, columns), jnp.float32)]
+    depth = 2 * lists[0].shape[1] * aux
+    shapes = []
+    for group, flips, per_message in jobs:
+        columns = sum(width_of(region) for region in group) * width
+        if per_message:
+            message = jax.ShapeDtypeStruct((per_message * width + TAIL, columns), jnp.int16)
+            shapes += [message] * (len(flips) // per_message)
+        else:
+            shapes.append(jax.ShapeDtypeStruct((len(flips), width, columns), jnp.float32))
+    if coeffs:
+        shapes.append(jax.ShapeDtypeStruct((8, width), jnp.float32))
     scalars = pl.BlockSpec(memory_space=pltpu.SMEM)
     whole = pl.BlockSpec(memory_space=pltpu.VMEM)
     return pl.pallas_call(
-        functools.partial(rows_kernel, group, flips, per_message, sides),
-        in_specs=[scalars] * (2 * sides) + [whole] * sides,
+        functools.partial(rows_kernel, jobs, len(coeffs)),
+        in_specs=[scalars] * 4 + [whole, pl.BlockSpec(memory_space=pl.ANY)] + [whole] * len(coeffs),
         out_specs=[whole] * len(shapes),
         out_shape=shapes,
-        scratch_shapes=[pltpu.VMEM((depth, width), jnp.bfloat16)] * 2
-        + [pltpu.VMEM((depth, PLACES * width), jnp.bfloat16)] * 2,
+        scratch_shapes=[pltpu.VMEM((depth, width), jnp.bfloat16)] * AHEAD
+        + [pltpu.VMEM((depth, PLACES * width), jnp.bfloat16)] * AHEAD
+        + [pltpu.VMEM(panels[1].shape, jnp.bfloat16), pltpu.SemaphoreType.DMA],
+        compiler_params=pltpu.CompilerParams(vmem_limit_bytes=40 << 20),
+        cost_estimate=SHORT,
+    )(lists[0], ranks[0], lists[1], ranks[1], *panels, *coeffs)
+
+
+def turn_kernel(late_stay, late_code, early_stay, vector, *refs):
+    codes, (late_own, *late_turn), (early_own, early_turn, vector_out) = refs[:3], refs[3:7], refs[7:]
+    height = late_own.shape[0]
+    for j, out in enumerate(late_turn):
+        encode(out, [late_stay[j + 1] + decode(late_code, j + 1, height)])
+    near, far, across = [decode_vector(c, vector.shape[1]) for c in codes]
+    rows, kept = encode_vector((vector[0:1, :] + near) + (far + across))
+    vector_out[...] = jnp.broadcast_to(kept, vector_out.shape)
+    encode(early_turn, [early_stay[0] + sum(decode(c, 0, height) for c in codes)], rows)
+    late_own[...] = late_stay[0] + decode(late_code, 0, height)
+    early_own[...] = early_stay[1] + sum(decode(c, 1, height) for c in codes)
+
+
+def turn(late_stay, late_code, early_stay, vector, early_codes):
+    def shapes(stay):
+        height, columns = stay.shape[1:]
+        message = jax.ShapeDtypeStruct((height + TAIL, columns), jnp.int16)
+        return jax.ShapeDtypeStruct((height, columns), jnp.float32), message
+
+    late_own, late_turn = shapes(late_stay)
+    return pl.pallas_call(
+        turn_kernel,
+        out_shape=[late_own] + [late_turn] * 3 + [*shapes(early_stay), vector],
         compiler_params=pltpu.CompilerParams(vmem_limit_bytes=32 << 20),
-        cost_estimate=pl.CostEstimate(
-            flops=8 * len(flips) * width * columns * depth,
-            bytes_accessed=4 * len(flips) * width * columns,
-            transcendentals=0,
-        ),
-    )(*lists, *ranks, *panels)
-
-
-def turn_y_kernel(stay, along_z, message, own, *codes):
-    height = own.shape[0]
-    rows = [stay[j] + sum(decode(c, j, height) for c in codes) for j in range(2)]
-    encode(message, rows[:1])
-    own[...] = rows[1]
-
-
-def turn_y(stay, codes):
-    height, columns = stay.shape[1:]
-    return pl.pallas_call(
-        lambda stay, *refs: turn_y_kernel(stay, None, refs[-2], refs[-1], *refs[:-2]),
+        cost_estimate=SHORT,
+    )(late_stay, late_code, early_stay, vector, *early_codes)
+
+
+def coulomb_kernel(vector, vector_other, metric, tiles, fitted, out):
+    aux, height, width = tiles.shape[1:]
+    gamma = (vector[...] + vector_other[...])[0:1, :aux]
+    column = jnp.sum(metric[...] * gamma, axis=1, keepdims=True)
+    fitted[...] = jnp.broadcast_to(column, (aux, width)).T[0:1, :]
+    total = jnp.zeros((height, width), jnp.float32)
+    for p in range(aux):
+        total = total + column[p : p + 1, 0:1] * tiles[0, p].astype(jnp.float32)
+    out[0] = total.astype(jnp.bfloat16)
+
+
+def coulomb_tile(vector, vector_other, metric_inv, three_index):
+    aux, height, width = three_index.shape[1:]
+    return pl.pallas_call(
+        coulomb_kernel,
         out_shape=[
-            jax.ShapeDtypeStruct((height + TAIL, columns), jnp.int16),
-            jax.ShapeDtypeStruct((height, columns), jnp.float32),
+            jax.ShapeDtypeStruct((1, aux), jnp.float32),
+            jax.ShapeDtypeStruct((1, height, width), jnp.bfloat16),
         ],
         compiler_params=pltpu.CompilerParams(vmem_limit_bytes=32 << 20),
-    )(stay, *codes)
-
-
-def turn_z_kernel(stay, code, *outs):
-    height = stay.shape[1]
-    for j in range(1, len(outs)):
-        encode(outs[j], [stay[j] + decode(code, j, height)])
-    outs[0][...] = stay[0] + decode(code, 0, height)
-
-
-def turn_z(stay, code):
-    count, height, columns = stay.shape
-    message = jax.ShapeDtypeStruct((height + TAIL, columns), jnp.int16)
-    return pl.pallas_call(
-        turn_z_kernel,
-        out_shape=[jax.ShapeDtypeStruct((height, columns), jnp.float32)] + [message] * (count - 1),
-        compiler_params=pltpu.CompilerParams(vmem_limit_bytes=32 << 20),
-    )(stay, code)
+        cost_estimate=SHORT,
+    )(vector, vector_other, metric_inv, three_index)
 
 
 def finish_kernel(backs, own, *refs):
@@ -256,7 +325,26 @@
         out_shape=[jax.ShapeDtypeStruct((height, columns), jnp.bfloat16)]
         + [jax.ShapeDtypeStruct((height, height), jnp.bfloat16)] * backs,
         compiler_params=pltpu.CompilerParams(vmem_limit_bytes=32 << 20),
+        cost_estimate=SHORT,
     )(own, *codes)
+
+
+def finish_early_kernel(own, code, vector, *refs):
+    finish_kernel(len(refs) - 2, own, code, *refs[:-1])
+    refs[-1][...] = vector[...] + decode_vector(code, vector.shape[1])
+
+
+def finish_early(own, code, vector):
+    height, columns = own.shape
+    backs = columns // height
+    return pl.pallas_call(
+        finish_early_kernel,
+        out_shape=[jax.ShapeDtypeStruct((height, columns), jnp.bfloat16)]
+        + [jax.ShapeDtypeStruct((height, height), jnp.bfloat16)] * backs
+        + [jax.ShapeDtypeStruct(vector.shape, jnp.float32)],
+        compiler_params=pltpu.CompilerParams(vmem_limit_bytes=32 << 20),
+        cost_estimate=SHORT,
+    )(own, code, vector)
 
 
 def give_back(block, region, b):
@@ -264,6 +352,12 @@
         return i ^ swap_low(first_place(i, region) + b)
 
     return lax.ppermute(block, "row", [(i, holder(i)) for i in range(ROWS)])
+
+
+def return_blocks(finished, group):
+    row, *back = finished
+    named = [(region, b) for region in group if region != 0 for b in range(width_of(region))]
+    return row, [give_back(block, *name) for block, name in zip(back, named)]
 
 
 def assemble_kernel(holders, early, late, *refs):
@@ -298,6 +392,7 @@
         assemble_kernel,
         in_specs=[pl.BlockSpec(memory_space=pltpu.SMEM)] + [vmem] * (2 + len(came)),
         out_shape=jax.ShapeDtypeStruct((1, width, ROWS * width), jnp.bfloat16),
+        cost_estimate=SHORT,
     )(row_block, early, late, *came)
 
 
@@ -324,41 +419,29 @@
     other = send(panels, CORE)
     listed, rank = naming(blocks, row_block, capacity)
     listed_other, rank_other = send(listed, CORE), send(rank, CORE)
-    rest = ((listed, listed_other), (rank, rank_other), (panels, other))
-    gamma = jnp.einsum(
-        "ispm,ism->p", panels.astype(jnp.float32), coeffs, precision=lax.Precision.HIGHEST
-    )
-    gamma = gamma + send(gamma, CORE)
-
-    early_go = partial_rows(Z_FIRST, [z | y for z in Z for y in (Y, 0)], 2, *rest)
-    *early_go, gamma = lax.optimization_barrier((*early_go, gamma))
-    near, far, across = [send(gamma, z) for z in Z]
-    gamma = (gamma + near) + (far + across)
-    early_codes = [send(x, z) for x, z in zip(early_go, Z)]
-    (late_go,) = partial_rows(Y_FIRST, [Y] + [z | Y for z in Z], 4, *rest)
-    late_go, gamma = lax.optimization_barrier((late_go, gamma))
-    gamma = gamma + send(gamma, Y)
+    ranks, sides = (rank, rank_other), (panels, other)
+
+    jobs = (Y_FIRST, [Y] + [z | Y for z in Z], 4), (Z_FIRST, [z | y for z in Z for y in (Y, 0)], 2)
+    late_go, *early_go, vector = partial_rows(jobs, (listed, listed_other), ranks, sides, coeffs)
+    across, far = send(early_go[2], Z[2]), send(early_go[1], Z[1])
     late_code = send(late_go, Y)
-    (early_stay,) = partial_rows(Z_FIRST, [Y, 0], 0, *rest)
-    (late_stay,) = partial_rows(Y_FIRST, [0, *Z], 0, *rest)
-
-    late_own, *late_turn = turn_z(late_stay, late_code)
-    late_codes = [send(x, z) for x, z in zip(late_turn, Z)]
-    early_turn, early_own = turn_y(early_stay, early_codes)
-    early, *early_back = finish(early_own, [send(early_turn, Y)], 3)
-    early_came = [
-        give_back(early_back[0], 1, 0),
-        give_back(early_back[1], 1, 1),
-        give_back(early_back[2], "extra", 0),
-    ]
-    fitted = jnp.dot(metric_inv, gamma, precision=lax.Precision.HIGHEST)
-    coulomb = jnp.einsum(
-        "p,rpmn->rmn", fitted, three_index.astype(jnp.float32), precision=lax.Precision.HIGHEST
-    )
-    late, *late_back = finish(late_own, late_codes, 4)
-    late_came = [give_back(late_back[2 * k + b], 2 + k, b) for k in range(2) for b in range(2)]
+    early_codes = [send(early_go[0], Z[0]), far, across]
+
+    listed, *_ = lax.optimization_barrier((listed, late_go, *early_go))
+    jobs = (Y_FIRST, [0, *Z], 0), (Z_FIRST, [Y, 0], 0)
+    late_stay, early_stay = partial_rows(jobs, (listed, listed_other), ranks, sides)
+
+    late_own, *late_turn, early_own, early_turn, vector = turn(
+        late_stay, late_code, early_stay, vector, early_codes
+    )
+    across, far = send(late_turn[2], Z[2]), send(late_turn[1], Z[1])
+    late_codes = [send(late_turn[0], Z[0]), far, across]
+    *early_out, vector = finish_early(early_own, send(early_turn, Y), vector)
+    early, early_came = return_blocks(early_out, Z_FIRST)
+    fitted, coulomb = coulomb_tile(vector, send(vector, CORE), metric_inv, three_index)
+    late, late_came = return_blocks(finish(late_own, late_codes, 4), Y_FIRST)
     exchange = assemble(row_block, early, late, early_came + late_came)
-    return (exchange, coulomb.astype(jnp.bfloat16), fitted)
+    return (exchange, coulomb, fitted[0])
 
 
 def solution(mesh):

time: 90.4 us -> 75 us (0.83)
  starting transfers between devices: 32.9 us -> 24 us
  matrix products: 4.7 us -> 0 us
  Pallas kernels: 19.9 us -> 16.5 us
  waiting for transfers between devices: 27.2 us -> 28.2 us
    ppermute x7, starting transfers between devices: 14.7 us -> 7.78 us  [give_back(): return lax.ppermute(block, 'row', [(i, holder(i)) for i in range(ROWS)])]
    dot_general x3 -> x0, matrix products: 4.7 us -> none  [the longest x1 2.75 us: summed_rows(): jnp.einsum('ispm,ism->p', panels.astype(jnp.float32), coeffs, precision=l...]
    pallas_call x6 -> x5, Pallas kernels: 17.5 us -> 14.2 us  [the longest x2 12.3 us: partial_rows(): pl.pallas_call(functools.partial(rows_kernel, jobs, len(coeffs)), in_spec...]
    ppermute x16 -> x12, starting transfers between devices: 18.2 us -> 16.2 us  [send(): return lax.ppermute(x, 'row', [(i, i ^ flip) for i in range(ROWS)])]
    ppermute x16 -> x12, waiting for transfers between devices: 23.6 us -> 24.1 us  [send(): return lax.ppermute(x, 'row', [(i, i ^ flip) for i in range(ROWS)])]
    unnamed x30 -> x25, local copies, waits for them, and re-layouts: 3.33 us -> 3.48 us
  transfers between devices with their start and end apart: 23 -> 19, of which waited for: 9 -> 9; matrix products, arithmetic and copies ran while one was open for 7% -> 3% of each run, Pallas kernels for 14% -> 8%
where the time goes in v3:
time: 75 us; the launch traced here: 74.3 us
  waiting for transfers between devices  28.2 us (38%)
  starting transfers between devices  24 us (32%)
  Pallas kernels  16.5 us (22%)
  local copies, waits for them, and re-layouts  3.65 us (5%)
  other arithmetic  1.19 us (2%)
  between operations  0.8 us (1%)
    ppermute x12, waiting for transfers between devices, send(): return lax.ppermute(x, 'row', [(i, i ^ flip) for i in range(ROWS)])  24.1 us
    ppermute x12, starting transfers between devices, send(): return lax.ppermute(x, 'row', [(i, i ^ flip) for i in range(ROWS)])  16.2 us
    pallas_call x2, Pallas kernels, partial_rows(): pl.pallas_call(functools.partial(rows_kernel, jobs, len(coeffs)), in_spec...  12.3 us
    ppermute x7, starting transfers between devices, give_back(): return lax.ppermute(block, 'row', [(i, holder(i)) for i in range(ROWS)])  7.78 us
    ppermute x7, waiting for transfers between devices, give_back(): return lax.ppermute(block, 'row', [(i, holder(i)) for i in range(ROWS)])  4.1 us
    unnamed x25, local copies, waits for them, and re-layouts  3.48 us
    pallas_call x1, Pallas kernels, assemble(): pl.pallas_call(assemble_kernel, in_specs=[pl.BlockSpec(memory_space=pltpu...  2.03 us
  transfers between devices with their start and end apart: 19, of which 9 were waited for; matrix products, arithmetic and copies ran while one was open for 3% of the time, Pallas kernels for 8%

profile of v3, /device:TPU:0, one launch (start us, length us, event | category | flops | bytes accessed | tf_op | source)
XLA Modules:
  0.0 74.3 jit_solution(13385583616135904537)
XLA Ops:
  0.6 0.5 collective-permute-start.2
  1.2 0.9 %fusion.2 = (s32[16,6]{0,1:T(8,128)S(1)}, s32[16,16]{1,0:T(8,128)S(1)}, s32[16,16]{1,0:T(8,128)S(1)}) fusion(s32[16]{0:T(128)S(1)} %fusion.6, s32[16]{0:T(128)} %holders.1, s32[16,6]{0,1:T(8,128)} %param.7), kind=kLoop, calls=%fused_computation.6 | loop fusion | flops 10144 | bytes 2944 | tf_op jit(solution)/shard_map/reduce_sum | solution.py:403
  2.6 0.5 collective-permute-start.1
  3.0 0.8 %copy.14.refs_0_ = f32[16,6,128]{2,1,0:T(8,128)S(1)} copy(f32[16,6,128]{2,0,1:T(8,128)} %param.9) | data formatting | bytes 98304 | tf_op args[3]
  3.9 0.3 collective-permute-done.listed_other
  4.4 1.4 %copy-done = bf16[16,6,64,128]{3,2,1,0:T(8,128)(2,1)S(1)} copy-done((bf16[16,6,64,128]{3,2,1,0:T(8,128)(2,1)S(1)}, bf16[16,6,64,128]{3,2,1,0:T(8,128)(2,1)}, u32[]{:S(2)}) %copy-start) | copy-done | bytes 1572888
  5.8 7.5 %shard_map.85 = (s16[528,768]{1,0:T(8,128)(2,1)S(1)}, s16[272,384]{1,0:T(8,128)(2,1)S(1)}, s16[272,384]{1,0:T(8,128)(2,1)S(1)}, s16[272,384]{1,0:T(8,128)(2,1)S(1)}, f32[8,128]{1,0:T(8,128)S(1)}) custom-call(s32[16,6]{1,0:T(8,128)S(1)} %broadcast_add_fusion.listed, s32[16,6]{1,0:T(8,128)S(1)} %copy.13.ranks, s32[16,6]{1,0:T(8,128)S(1)} %collective-permute-done.listed_other, ...), custom_call_target="tpu_custom_call" | custom-call | flops 1024 | bytes 1024 | tf_op jit(solution)/shard_map/pallas_call | solution.py:247
  13.3 3.0 %collective-permute-start.3 = (s16[528,768]{1,0:T(8,128)(2,1)S(1)}, s16[528,768]{1,0:T(8,128)(2,1)S(1)}, u32[]{:S(2)}, u32[]{:S(2)}) collective-permute-start(s16[528,768]{1,0:T(8,128)(2,1)S(1)} %get-tuple-element.30), channel_id=1, source_target_pairs={{0,2},{1,3},{2,0},{3,1},{4,6},{5,7},{6,4},{7,5},{8,10},{9,11},{10,... | collective-permute-start | bytes 2433032 | tf_op jit(solution)/shard_map/ppermute | solution.py:89
  16.3 1.6 %collective-permute-start.4 = (s16[272,384]{1,0:T(8,128)(2,1)S(1)}, s16[272,384]{1,0:T(8,128)(2,1)S(1)}, u32[]{:S(2)}, u32[]{:S(2)}) collective-permute-start(s16[272,384]{1,0:T(8,128)(2,1)S(1)} %get-tuple-element.31), channel_id=1, source_target_pairs={{0,4},{1,5},{2,6},{3,7},{4,0},{5,1},{6,2},{7,3},{8,12},{9,13},{10,... | collective-permute-start | bytes 626696 | tf_op jit(solution)/shard_map/ppermute | solution.py:89
  17.8 2.6 %collective-permute-start.5 = (s16[272,384]{1,0:T(8,128)(2,1)S(1)}, s16[272,384]{1,0:T(8,128)(2,1)S(1)}, u32[]{:S(2)}, u32[]{:S(2)}) collective-permute-start(s16[272,384]{1,0:T(8,128)(2,1)S(1)} %get-tuple-element.32), channel_id=1, source_target_pairs={{0,8},{1,9},{2,10},{3,11},{4,12},{5,13},{6,14},{7,15},{8,0},{9,1},... | collective-permute-start | bytes 626696 | tf_op jit(solution)/shard_map/ppermute | solution.py:89
  20.6 4.9 %shard_map.86 = (f32[4,128,768]{2,1,0:T(8,128)S(1)}, f32[2,128,384]{2,1,0:T(8,128)S(1)}) custom-call(s32[16,6]{1,0:T(8,128)S(1)} %broadcast_add_fusion.listed, s32[16,6]{1,0:T(8,128)S(1)} %copy.13.ranks, s32[16,6]{1,0:T(8,128)S(1)} %collective-permute-done.listed_other, s32[16,6]{1,0:T(8,128)S(1)} %collective-permute-done.1.ranks_other, ...), custom_call_target="tpu_custom_call" | custom-call | flops 1024 | bytes 1024 | tf_op jit(solution)/shard_map/pallas_call | solution.py:247
  25.5 1.4 %collective-permute-done.4.refs_0_ = s16[272,384]{1,0:T(8,128)(2,1)S(1)} collective-permute-done((s16[272,384]{1,0:T(8,128)(2,1)S(1)}, s16[272,384]{1,0:T(8,128)(2,1)S(1)}, u32[]{:S(2)}, u32[]{:S(2)}) %collective-permute-start.4) | collective-permute-done | bytes 208928 | tf_op jit(solution)/shard_map/ppermute | solution.py:89
  27.0 8.8 %collective-permute-done.5.refs_1_ = s16[272,384]{1,0:T(8,128)(2,1)S(1)} collective-permute-done((s16[272,384]{1,0:T(8,128)(2,1)S(1)}, s16[272,384]{1,0:T(8,128)(2,1)S(1)}, u32[]{:S(2)}, u32[]{:S(2)}) %collective-permute-start.5) | collective-permute-done | bytes 208928 | tf_op jit(solution)/shard_map/ppermute | solution.py:89
  35.8 0.7 shard_map.87
  36.5 3.7 %collective-permute-start.8 = (s16[144,768]{1,0:T(8,128)(2,1)S(1)}, s16[144,768]{1,0:T(8,128)(2,1)S(1)}, u32[]{:S(2)}, u32[]{:S(2)}) collective-permute-start(s16[144,768]{1,0:T(8,128)(2,1)S(1)} %get-tuple-element.43), channel_id=1, source_target_pairs={{0,4},{1,5},{2,6},{3,7},{4,0},{5,1},{6,2},{7,3},{8,12},{9,13},{10,... | collective-permute-start | bytes 663560 | tf_op jit(solution)/shard_map/ppermute | solution.py:89
  40.2 1.1 %collective-permute-start.9 = (s16[144,768]{1,0:T(8,128)(2,1)S(1)}, s16[144,768]{1,0:T(8,128)(2,1)S(1)}, u32[]{:S(2)}, u32[]{:S(2)}) collective-permute-start(s16[144,768]{1,0:T(8,128)(2,1)S(1)} %get-tuple-element.44), channel_id=1, source_target_pairs={{0,8},{1,9},{2,10},{3,11},{4,12},{5,13},{6,14},{7,15},{8,0},{9,1},... | collective-permute-start | bytes 663560 | tf_op jit(solution)/shard_map/ppermute | solution.py:89
  41.3 1.4 %collective-permute-start.10 = (s16[144,768]{1,0:T(8,128)(2,1)S(1)}, s16[144,768]{1,0:T(8,128)(2,1)S(1)}, u32[]{:S(2)}, u32[]{:S(2)}) collective-permute-start(s16[144,768]{1,0:T(8,128)(2,1)S(1)} %get-tuple-element.45), channel_id=1, source_target_pairs={{0,12},{1,13},{2,14},{3,15},{4,8},{5,9},{6,10},{7,11},{8,4},{9,5},... | collective-permute-start | bytes 663560 | tf_op jit(solution)/shard_map/ppermute | solution.py:89
  42.7 0.5 collective-permute-start.7
  43.2 4.3 %collective-permute-done.7.code = s16[144,384]{1,0:T(8,128)(2,1)S(1)} collective-permute-done((s16[144,384]{1,0:T(8,128)(2,1)S(1)}, s16[144,384]{1,0:T(8,128)(2,1)S(1)}, u32[]{:S(2)}, u32[]{:S(2)}) %collective-permute-start.7) | collective-permute-done | bytes 110624 | tf_op jit(solution)/shard_map/ppermute | solution.py:89
  47.6 2.5 %collective-permute-start.11 = (bf16[128,128]{1,0:T(8,128)(2,1)S(1)}, bf16[128,128]{1,0:T(8,128)(2,1)S(1)}, u32[]{:S(2)}, u32[]{:S(2)}) collective-permute-start(bf16[128,128]{1,0:T(8,128)(2,1)S(1)} %get-tuple-element.47), channel_id=1, source_target_pairs={{0,12},{1,13},{2,14},{3,15},{4,9},{5,8},{6,11},{7,10},{8,4},{9,5},... | collective-permute-start | bytes 98312 | tf_op jit(solution)/shard_map/ppermute | solution.py:354
  50.0 1.1 %collective-permute-start.18 = (f32[8,128]{1,0:T(8,128)S(1)}, f32[8,128]{1,0:T(8,128)S(1)}, u32[]{:S(2)}, u32[]{:S(2)}) collective-permute-start(f32[8,128]{1,0:T(8,128)S(1)} %get-tuple-element.54.vector), channel_id=1, source_target_pairs={{0,1},{1,0},{2,3},{3,2},{4,5},{5,4},{6,7},{7,6},{8,9},{9,8},{10,11... | collective-permute-start | bytes 12296 | tf_op jit(solution)/shard_map/ppermute | solution.py:89
  51.2 9.1 %collective-permute-done.9.refs_1_ = s16[144,768]{1,0:T(8,128)(2,1)S(1)} collective-permute-done((s16[144,768]{1,0:T(8,128)(2,1)S(1)}, s16[144,768]{1,0:T(8,128)(2,1)S(1)}, u32[]{:S(2)}, u32[]{:S(2)}) %collective-permute-start.9) | collective-permute-done | bytes 221216 | tf_op jit(solution)/shard_map/ppermute | solution.py:89
  60.5 0.7 copy-done.2
  61.1 3.6 %collective-permute-start.14 = (bf16[128,128]{1,0:T(8,128)(2,1)S(1)}, bf16[128,128]{1,0:T(8,128)(2,1)S(1)}, u32[]{:S(2)}, u32[]{:S(2)}) collective-permute-start(bf16[128,128]{1,0:T(8,128)(2,1)S(1)} %get-tuple-element.50), channel_id=1, source_target_pairs={{0,4},{1,5},{2,6},{3,7},{4,1},{5,0},{6,3},{7,2},{8,12},{9,13},{10,... | collective-permute-start | bytes 98312 | tf_op jit(solution)/shard_map/ppermute | solution.py:354
  64.7 1.1 %collective-permute-start.16 = (bf16[128,128]{1,0:T(8,128)(2,1)S(1)}, bf16[128,128]{1,0:T(8,128)(2,1)S(1)}, u32[]{:S(2)}, u32[]{:S(2)}) collective-permute-start(bf16[128,128]{1,0:T(8,128)(2,1)S(1)} %get-tuple-element.52), channel_id=1, source_target_pairs={{0,8},{1,9},{2,10},{3,11},{4,12},{5,13},{6,14},{7,15},{8,1},{9,0},... | collective-permute-start | bytes 98312 | tf_op jit(solution)/shard_map/ppermute | solution.py:354
  65.8 0.6 collective-permute-start.17
  66.4 1.1 %shard_map.91 = (f32[1,64]{1,0:T(1,128)}, bf16[1,128,128]{2,1,0:T(8,128)(2,1)}) custom-call(f32[8,128]{1,0:T(8,128)S(1)} %get-tuple-element.54.vector, f32[8,128]{1,0:T(8,128)S(1)} %collective-permute-done.18.vector_other, f32[64,64]{1,0:T(8,128)S(1)} %copy-done.4, bf16[1,64,128,128]{3,2,1,0:T(8,128)(2,1)S(1)} %copy-done.1), custom_call_target="tpu_custom_call" | custom-call | flops 1024 | bytes 1024 | tf_op jit(solution)/shard_map/pallas_call | solution.py:301
  67.6 1.3 %collective-permute-done.15.refs_4_ = bf16[128,128]{1,0:T(8,128)(2,1)S(1)} collective-permute-done((bf16[128,128]{1,0:T(8,128)(2,1)S(1)}, bf16[128,128]{1,0:T(8,128)(2,1)S(1)}, u32[]{:S(2)}, u32[]{:S(2)}) %collective-permute-start.15) | collective-permute-done | bytes 32800 | tf_op jit(solution)/shard_map/ppermute | solution.py:354
  68.9 0.4 collective-permute-done.16.refs_5_
  69.4 2.3 %collective-permute-done.17.refs_6_ = bf16[128,128]{1,0:T(8,128)(2,1)S(1)} collective-permute-done((bf16[128,128]{1,0:T(8,128)(2,1)S(1)}, bf16[128,128]{1,0:T(8,128)(2,1)S(1)}, u32[]{:S(2)}, u32[]{:S(2)}) %collective-permute-start.17) | collective-permute-done | bytes 32800 | tf_op jit(solution)/shard_map/ppermute | solution.py:354
  71.7 0.6 copy-done.11
  72.3 2.0 %shard_map.90 = bf16[1,128,2048]{2,1,0:T(8,128)(2,1)} custom-call(s32[16]{0:T(128)} %holders.1, bf16[128,384]{1,0:T(8,128)(2,1)} %copy-done.3, bf16[128,768]{1,0:T(8,128)(2,1)} %copy-done.2, bf16[128,128]{1,0:T(8,128)(2,1)} %copy-done.5, bf16[128,128]{1,0:T(8,128)(2,1)} %copy-done.6, bf16[128,128]{1,0:T(8,128)(2,1)} %copy-done.7, ...), custom_call_target="tpu_custom_call" | custom-call | flops 1024 | bytes 1024 | tf_op jit(solution)/shard_map/pallas_call | solution.py:391
  (49 shorter events, 1.3 us)
Async XLA Ops:
  0.6 3.8 %collective-permute-start.2 = (bf16[16,6,64,128]{3,2,1,0:T(8,128)(2,1)}, bf16[16,6,64,128]{3,2,1,0:T(8,128)(2,1)S(1)}, u32[]{:S(2)}, u32[]{:S(2)}) collective-permute-start(bf16[16,6,64,128]{3,2,1,0:T(8,128)(2,1)} %mine.3), channel_id=1, source_target_pairs={{0,1},{1,0},{2,3},{3,2},{4,5},{5,4},{6,7},{7,6},{8,9},{9,8},{10,11... | collective-permute-start | bytes 4718600 | tf_op jit(solution)/shard_map/ppermute | solution.py:89
  2.4 1.7 %collective-permute-start = (s32[16,6]{1,0:T(8,128)S(1)}, s32[16,6]{1,0:T(8,128)S(1)}, u32[]{:S(2)}, u32[]{:S(2)}) collective-permute-start(s32[16,6]{1,0:T(8,128)S(1)} %broadcast_add_fusion.listed), channel_id=1, source_target_pairs={{0,1},{1,0},{2,3},{3,2},{4,5},{5,4},{6,7},{7,6},{8,9},{9,8},{10,11... | collective-permute-start | bytes 1160 | tf_op jit(solution)/shard_map/ppermute | solution.py:89
  2.6 1.6 %collective-permute-start.1 = (s32[16,6]{1,0:T(8,128)S(1)}, s32[16,6]{1,0:T(8,128)S(1)}, u32[]{:S(2)}, u32[]{:S(2)}) collective-permute-start(s32[16,6]{1,0:T(8,128)S(1)} %copy.13.ranks), channel_id=1, source_target_pairs={{0,1},{1,0},{2,3},{3,2},{4,5},{5,4},{6,7},{7,6},{8,9},{9,8},{10,11... | collective-permute-start | bytes 1160 | tf_op jit(solution)/shard_map/ppermute | solution.py:89
  4.4 1.4 %copy-start = (bf16[16,6,64,128]{3,2,1,0:T(8,128)(2,1)S(1)}, bf16[16,6,64,128]{3,2,1,0:T(8,128)(2,1)}, u32[]{:S(2)}) copy-start(bf16[16,6,64,128]{3,2,1,0:T(8,128)(2,1)} %mine.3) | copy-start | bytes 4718596
  13.3 22.5 %collective-permute-start.3 = (s16[528,768]{1,0:T(8,128)(2,1)S(1)}, s16[528,768]{1,0:T(8,128)(2,1)S(1)}, u32[]{:S(2)}, u32[]{:S(2)}) collective-permute-start(s16[528,768]{1,0:T(8,128)(2,1)S(1)} %get-tuple-element.30), channel_id=1, source_target_pairs={{0,2},{1,3},{2,0},{3,1},{4,6},{5,7},{6,4},{7,5},{8,10},{9,11},{10,... | collective-permute-start | bytes 2433032 | tf_op jit(solution)/shard_map/ppermute | solution.py:89
  16.3 10.7 %collective-permute-start.4 = (s16[272,384]{1,0:T(8,128)(2,1)S(1)}, s16[272,384]{1,0:T(8,128)(2,1)S(1)}, u32[]{:S(2)}, u32[]{:S(2)}) collective-permute-start(s16[272,384]{1,0:T(8,128)(2,1)S(1)} %get-tuple-element.31), channel_id=1, source_target_pairs={{0,4},{1,5},{2,6},{3,7},{4,0},{5,1},{6,2},{7,3},{8,12},{9,13},{10,... | collective-permute-start | bytes 626696 | tf_op jit(solution)/shard_map/ppermute | solution.py:89
  17.8 17.9 %collective-permute-start.5 = (s16[272,384]{1,0:T(8,128)(2,1)S(1)}, s16[272,384]{1,0:T(8,128)(2,1)S(1)}, u32[]{:S(2)}, u32[]{:S(2)}) collective-permute-start(s16[272,384]{1,0:T(8,128)(2,1)S(1)} %get-tuple-element.32), channel_id=1, source_target_pairs={{0,8},{1,9},{2,10},{3,11},{4,12},{5,13},{6,14},{7,15},{8,0},{9,1},... | collective-permute-start | bytes 626696 | tf_op jit(solution)/shard_map/ppermute | solution.py:89
  20.4 15.3 %collective-permute-start.6 = (s16[272,384]{1,0:T(8,128)(2,1)S(1)}, s16[272,384]{1,0:T(8,128)(2,1)S(1)}, u32[]{:S(2)}, u32[]{:S(2)}) collective-permute-start(s16[272,384]{1,0:T(8,128)(2,1)S(1)} %get-tuple-element.33), channel_id=1, source_target_pairs={{0,12},{1,13},{2,14},{3,15},{4,8},{5,9},{6,10},{7,11},{8,4},{9,5},... | collective-permute-start | bytes 626696 | tf_op jit(solution)/shard_map/ppermute | solution.py:89
  35.8 30.7 %copy-start.1 = (bf16[1,64,128,128]{3,2,1,0:T(8,128)(2,1)S(1)}, bf16[1,64,128,128]{3,2,1,0:T(8,128)(2,1)}, u32[]{:S(2)}) copy-start(bf16[1,64,128,128]{3,2,1,0:T(8,128)(2,1)} %tiles.1) | copy-start | bytes 6291460
  35.8 30.7 %copy-start.4 = (f32[64,64]{1,0:T(8,128)S(1)}, f32[64,64]{1,0:T(8,128)}, u32[]{:S(2)}) copy-start(f32[64,64]{1,0:T(8,128)} %metric.1) | copy-start | bytes 49156
  36.5 13.6 %collective-permute-start.8 = (s16[144,768]{1,0:T(8,128)(2,1)S(1)}, s16[144,768]{1,0:T(8,128)(2,1)S(1)}, u32[]{:S(2)}, u32[]{:S(2)}) collective-permute-start(s16[144,768]{1,0:T(8,128)(2,1)S(1)} %get-tuple-element.43), channel_id=1, source_target_pairs={{0,4},{1,5},{2,6},{3,7},{4,0},{5,1},{6,2},{7,3},{8,12},{9,13},{10,... | collective-permute-start | bytes 663560 | tf_op jit(solution)/shard_map/ppermute | solution.py:89
  40.2 20.1 %collective-permute-start.9 = (s16[144,768]{1,0:T(8,128)(2,1)S(1)}, s16[144,768]{1,0:T(8,128)(2,1)S(1)}, u32[]{:S(2)}, u32[]{:S(2)}) collective-permute-start(s16[144,768]{1,0:T(8,128)(2,1)S(1)} %get-tuple-element.44), channel_id=1, source_target_pairs={{0,8},{1,9},{2,10},{3,11},{4,12},{5,13},{6,14},{7,15},{8,0},{9,1},... | collective-permute-start | bytes 663560 | tf_op jit(solution)/shard_map/ppermute | solution.py:89
  41.3 19.0 %collective-permute-start.10 = (s16[144,768]{1,0:T(8,128)(2,1)S(1)}, s16[144,768]{1,0:T(8,128)(2,1)S(1)}, u32[]{:S(2)}, u32[]{:S(2)}) collective-permute-start(s16[144,768]{1,0:T(8,128)(2,1)S(1)} %get-tuple-element.45), channel_id=1, source_target_pairs={{0,12},{1,13},{2,14},{3,15},{4,8},{5,9},{6,10},{7,11},{8,4},{9,5},... | collective-permute-start | bytes 663560 | tf_op jit(solution)/shard_map/ppermute | solution.py:89
  42.7 4.7 %collective-permute-start.7 = (s16[144,384]{1,0:T(8,128)(2,1)S(1)}, s16[144,384]{1,0:T(8,128)(2,1)S(1)}, u32[]{:S(2)}, u32[]{:S(2)}) collective-permute-start(s16[144,384]{1,0:T(8,128)(2,1)S(1)} %get-tuple-element.39), channel_id=1, source_target_pairs={{0,2},{1,3},{2,0},{3,1},{4,6},{5,7},{6,4},{7,5},{8,10},{9,11},{10,... | collective-permute-start | bytes 331784 | tf_op jit(solution)/shard_map/ppermute | solution.py:89
  47.5 20.0 %copy-start.3 = (bf16[128,384]{1,0:T(8,128)(2,1)}, bf16[128,384]{1,0:T(8,128)(2,1)S(1)}, u32[]{:S(2)}) copy-start(bf16[128,384]{1,0:T(8,128)(2,1)S(1)} %get-tuple-element.41.early) | copy-start | bytes 294916
  47.6 17.1 %collective-permute-start.11 = (bf16[128,128]{1,0:T(8,128)(2,1)S(1)}, bf16[128,128]{1,0:T(8,128)(2,1)S(1)}, u32[]{:S(2)}, u32[]{:S(2)}) collective-permute-start(bf16[128,128]{1,0:T(8,128)(2,1)S(1)} %get-tuple-element.47), channel_id=1, source_target_pairs={{0,12},{1,13},{2,14},{3,15},{4,9},{5,8},{6,11},{7,10},{8,4},{9,5},... | collective-permute-start | bytes 98312 | tf_op jit(solution)/shard_map/ppermute | solution.py:354
  50.0 15.8 %collective-permute-start.12 = (bf16[128,128]{1,0:T(8,128)(2,1)S(1)}, bf16[128,128]{1,0:T(8,128)(2,1)S(1)}, u32[]{:S(2)}, u32[]{:S(2)}) collective-permute-start(bf16[128,128]{1,0:T(8,128)(2,1)S(1)} %get-tuple-element.48), channel_id=1, source_target_pairs={{0,14},{1,15},{2,12},{3,13},{4,11},{5,10},{6,9},{7,8},{8,6},{9,7},... | collective-permute-start | bytes 98312 | tf_op jit(solution)/shard_map/ppermute | solution.py:354
  50.0 14.6 %collective-permute-start.18 = (f32[8,128]{1,0:T(8,128)S(1)}, f32[8,128]{1,0:T(8,128)S(1)}, u32[]{:S(2)}, u32[]{:S(2)}) collective-permute-start(f32[8,128]{1,0:T(8,128)S(1)} %get-tuple-element.54.vector), channel_id=1, source_target_pairs={{0,1},{1,0},{2,3},{3,2},{4,5},{5,4},{6,7},{7,6},{8,9},{9,8},{10,11... | collective-permute-start | bytes 12296 | tf_op jit(solution)/shard_map/ppermute | solution.py:89
  60.2 7.3 %collective-permute-start.13 = (bf16[128,128]{1,0:T(8,128)(2,1)S(1)}, bf16[128,128]{1,0:T(8,128)(2,1)S(1)}, u32[]{:S(2)}, u32[]{:S(2)}) collective-permute-start(bf16[128,128]{1,0:T(8,128)(2,1)S(1)} %get-tuple-element.49), channel_id=1, source_target_pairs={{0,1},{1,2},{2,3},{3,0},{4,5},{5,6},{6,7},{7,4},{8,9},{9,10},{10,1... | collective-permute-start | bytes 98312 | tf_op jit(solution)/shard_map/ppermute | solution.py:354
  60.5 0.7 copy-start.2
  61.1 6.4 %collective-permute-start.14 = (bf16[128,128]{1,0:T(8,128)(2,1)S(1)}, bf16[128,128]{1,0:T(8,128)(2,1)S(1)}, u32[]{:S(2)}, u32[]{:S(2)}) collective-permute-start(bf16[128,128]{1,0:T(8,128)(2,1)S(1)} %get-tuple-element.50), channel_id=1, source_target_pairs={{0,4},{1,5},{2,6},{3,7},{4,1},{5,0},{6,3},{7,2},{8,12},{9,13},{10,... | collective-permute-start | bytes 98312 | tf_op jit(solution)/shard_map/ppermute | solution.py:354
  64.7 4.2 %collective-permute-start.15 = (bf16[128,128]{1,0:T(8,128)(2,1)S(1)}, bf16[128,128]{1,0:T(8,128)(2,1)S(1)}, u32[]{:S(2)}, u32[]{:S(2)}) collective-permute-start(bf16[128,128]{1,0:T(8,128)(2,1)S(1)} %get-tuple-element.51), channel_id=1, source_target_pairs={{0,6},{1,7},{2,4},{3,5},{4,3},{5,2},{6,1},{7,0},{8,14},{9,15},{10,... | collective-permute-start | bytes 98312 | tf_op jit(solution)/shard_map/ppermute | solution.py:354
  64.7 7.0 %copy-start.5 = (bf16[128,128]{1,0:T(8,128)(2,1)}, bf16[128,128]{1,0:T(8,128)(2,1)S(1)}, u32[]{:S(2)}) copy-start(bf16[128,128]{1,0:T(8,128)(2,1)S(1)} %collective-permute-done.11.refs_0_) | copy-start | bytes 98308
  64.7 4.6 %collective-permute-start.16 = (bf16[128,128]{1,0:T(8,128)(2,1)S(1)}, bf16[128,128]{1,0:T(8,128)(2,1)S(1)}, u32[]{:S(2)}, u32[]{:S(2)}) collective-permute-start(bf16[128,128]{1,0:T(8,128)(2,1)S(1)} %get-tuple-element.52), channel_id=1, source_target_pairs={{0,8},{1,9},{2,10},{3,11},{4,12},{5,13},{6,14},{7,15},{8,1},{9,0},... | collective-permute-start | bytes 98312 | tf_op jit(solution)/shard_map/ppermute | solution.py:354
  65.8 5.8 %copy-start.6 = (bf16[128,128]{1,0:T(8,128)(2,1)}, bf16[128,128]{1,0:T(8,128)(2,1)S(1)}, u32[]{:S(2)}) copy-start(bf16[128,128]{1,0:T(8,128)(2,1)S(1)} %collective-permute-done.12.refs_1_) | copy-start | bytes 98308
  65.8 5.8 %collective-permute-start.17 = (bf16[128,128]{1,0:T(8,128)(2,1)S(1)}, bf16[128,128]{1,0:T(8,128)(2,1)S(1)}, u32[]{:S(2)}, u32[]{:S(2)}) collective-permute-start(bf16[128,128]{1,0:T(8,128)(2,1)S(1)} %get-tuple-element.53), channel_id=1, source_target_pairs={{0,10},{1,11},{2,8},{3,9},{4,14},{5,15},{6,12},{7,13},{8,3},{9,2},... | collective-permute-start | bytes 98312 | tf_op jit(solution)/shard_map/ppermute | solution.py:354
  67.6 4.1 %copy-start.7 = (bf16[128,128]{1,0:T(8,128)(2,1)}, bf16[128,128]{1,0:T(8,128)(2,1)S(1)}, u32[]{:S(2)}) copy-start(bf16[128,128]{1,0:T(8,128)(2,1)S(1)} %collective-permute-done.13.refs_2_) | copy-start | bytes 98308
  67.6 4.1 %copy-start.8 = (bf16[128,128]{1,0:T(8,128)(2,1)}, bf16[128,128]{1,0:T(8,128)(2,1)S(1)}, u32[]{:S(2)}) copy-start(bf16[128,128]{1,0:T(8,128)(2,1)S(1)} %collective-permute-done.14.refs_3_) | copy-start | bytes 98308
  68.9 2.8 %copy-start.9 = (bf16[128,128]{1,0:T(8,128)(2,1)}, bf16[128,128]{1,0:T(8,128)(2,1)S(1)}, u32[]{:S(2)}) copy-start(bf16[128,128]{1,0:T(8,128)(2,1)S(1)} %collective-permute-done.15.refs_4_) | copy-start | bytes 98308
  69.4 2.4 %copy-start.10 = (bf16[128,128]{1,0:T(8,128)(2,1)}, bf16[128,128]{1,0:T(8,128)(2,1)S(1)}, u32[]{:S(2)}) copy-start(bf16[128,128]{1,0:T(8,128)(2,1)S(1)} %collective-permute-done.16.refs_5_) | copy-start | bytes 98308
  71.7 0.6 copy-start.11

commit v4 on v3

v4 whole, which is shorter than its diff:
```python
import functools
import jax
import jax.numpy as jnp
from jax import lax
from jax.experimental import pallas as pl
from jax.experimental.pallas import tpu as pltpu
from jax.sharding import PartitionSpec as P


def row_terms(rows_in, row_ids, owned, count):
    total_rows = rows_in.shape[0]
    group = 32
    slots = rows_in.shape[1]
    width = rows_in.shape[3]
    grouped = rows_in.reshape((total_rows // group, group) + rows_in.shape[1:])
    grouped_ids = row_ids.reshape(total_rows // group, group, slots)

    def step(total, item):
        block_rows, block_ids = item
        chosen = (block_ids == owned).astype(jnp.bfloat16)
        picked = jnp.einsum(
            "gs,gspk->gpk", chosen, block_rows, preferred_element_type=jnp.float32
        ).astype(jnp.bfloat16)
        prods = jnp.einsum("gpk,gspn->gskn", picked, block_rows, preferred_element_type=jnp.float32)
        target = jnp.maximum(block_ids, 0).reshape(-1)
        added = jax.ops.segment_sum(prods.reshape(-1, width, width), target, num_segments=count)
        return (total + added, None)

    start = jnp.zeros((count, width, width), jnp.float32)
    total, _ = lax.scan(step, start, (grouped, grouped_ids))
    return total


def sent_panels(panels, blocks, row_block, coeffs, metric_inv, three_index):
    count = row_block.shape[0]
    orbits, slots, aux, width = panels.shape
    capacity = max(2, (orbits * slots + count - 1) // count)
    here = lax.axis_index("row")
    owned = row_block[here]
    ranks = jnp.arange(count, dtype=jnp.int32)
    flat_ids = blocks.reshape(-1)
    matches = (row_block[None, :] == flat_ids[:, None]).astype(jnp.int32)
    target = jnp.sum(matches * ranks[None, :], axis=1)
    hits = (ranks[None, :] == target[:, None]).astype(jnp.int32)
    before = jnp.cumsum(hits, axis=0) - hits
    place = jnp.sum(before * hits, axis=1)
    source = jnp.repeat(panels, slots, axis=0)
    source_ids = jnp.repeat(blocks, slots, axis=0).astype(jnp.bfloat16)
    outgoing = (
        jnp.zeros((count, capacity, slots, aux, width), jnp.bfloat16).at[target, place].set(source)
    )
    outgoing_ids = (
        jnp.full((count, capacity, slots), -1.0, jnp.bfloat16).at[target, place].set(source_ids)
    )
    partial_terms = jnp.einsum(
        "ispm,ism->p", panels.astype(jnp.float32), coeffs, precision=lax.Precision.HIGHEST
    )
    gamma = lax.psum(partial_terms, "row")
    fitted = jnp.dot(metric_inv, gamma, precision=lax.Precision.HIGHEST)
    coulomb = jnp.einsum(
        "p,rpmn->rmn", fitted, three_index.astype(jnp.float32), precision=lax.Precision.HIGHEST
    )
    arrived, arrived_ids = (
        lax.all_to_all(outgoing, "row", split_axis=0, concat_axis=0, tiled=True),
        lax.all_to_all(outgoing_ids, "row", split_axis=0, concat_axis=0, tiled=True),
    )
    accum = row_terms(
        arrived.reshape(-1, slots, aux, width),
        arrived_ids.reshape(-1, slots).astype(jnp.int32),
        owned,
        count,
    )
    exchange = accum.transpose(1, 0, 2).reshape(width, count * width)[None].astype(jnp.bfloat16)
    return (exchange, coulomb.astype(jnp.bfloat16), fitted)


ROWS = 16
CORE, Y, Z = 1, 2, (4, 8, 12)
NEAR, FAR = 4, 12
PLACES = 16
Z_FIRST, SOONER, LATER = (3, "extra"), (1, 2), (0,)
TAIL = 8
TOP = 14.99
VECTOR = 4
AHEAD = 6
SHORT = pl.CostEstimate(flops=1024, bytes_accessed=1024, transcendentals=0)
LONG = pl.CostEstimate(flops=1 << 34, bytes_accessed=1024, transcendentals=0)


def send(x, flip):
    return lax.ppermute(x, "row", [(i, i ^ flip) for i in range(ROWS)])


def side_of(z, apart):
    return (z >> 1) & 1 if apart == 2 else z & 1


def first_place(row, region):
    if region == 0:
        return 0
    if region == "extra":
        return 2 + ((row >> 1) & 1)
    return region * 4 + side_of(row >> 2, region) * 2


def width_of(region):
    return 1 if region == "extra" else 2


def encode(out, sums, vector=()):
    height, columns = sums[0].shape
    line = lax.broadcasted_iota(jnp.int32, (TAIL, columns), 0)
    tail = jnp.zeros((TAIL, columns), jnp.float32)
    for j, x in enumerate(sums):
        peak = jnp.maximum(jnp.max(jnp.abs(x), axis=0, keepdims=True), 2.0**-100)
        exponent = jnp.ceil(jnp.log2(peak) * 8)
        scaled = jnp.round(x * jnp.exp2(TOP - exponent * 0.125))
        out[j * height : (j + 1) * height, :] = scaled.astype(jnp.int32).astype(jnp.int16)
        tail = jnp.where(line == j, exponent, tail)
    for j, x in enumerate(vector):
        rest = jnp.zeros((1, columns - x.shape[1]), jnp.float32)
        tail = jnp.where(line == VECTOR + j, jnp.concatenate([x, rest], axis=1), tail)
    out[len(sums) * height :, :] = tail.astype(jnp.int32).astype(jnp.int16)


def encode_vector(x):
    exponent = jnp.ceil(jnp.log2(jnp.maximum(jnp.abs(x), 2.0**-100)))
    scaled = x * jnp.exp2(14 - exponent)
    high = jnp.round(scaled)
    low = jnp.round((scaled - high) * 2.0**15)
    return (exponent, high, low), combine(exponent, high, low)


def combine(exponent, high, low):
    return (high + low * 2.0**-15) * jnp.exp2(exponent - 14)


def decode_vector(codes, width):
    tail = codes[codes.shape[0] - TAIL :, :width].astype(jnp.int32).astype(jnp.float32)
    return combine(*(tail[VECTOR + j : VECTOR + j + 1, :] for j in range(3)))


def decode(codes, j, height):
    count = (codes.shape[0] - TAIL) // height
    exponents = codes[count * height :, :].astype(jnp.int32).astype(jnp.float32)
    scale = jnp.exp2(exponents[j : j + 1, :] * 0.125 - TOP)
    return codes[j * height : (j + 1) * height, :].astype(jnp.int32).astype(jnp.float32) * scale


def bring_kernel(far, near, arrived):
    copy = pltpu.make_async_copy(far, near, arrived)
    copy.start()
    copy.wait()


def bring(panels):
    return pl.pallas_call(
        bring_kernel,
        in_specs=[pl.BlockSpec(memory_space=pltpu.HBM)],
        out_specs=pl.BlockSpec(memory_space=pltpu.VMEM),
        out_shape=jax.ShapeDtypeStruct(panels.shape, panels.dtype),
        scratch_shapes=[pltpu.SemaphoreType.DMA],
        compiler_params=pltpu.CompilerParams(vmem_limit_bytes=16 << 20),
        cost_estimate=SHORT,
    )(panels)


def density_of(panels, coeffs):
    orbits, slots, aux, width = panels.shape
    total = jnp.zeros((aux, width), jnp.float32)
    for i in range(orbits):
        for t in range(slots):
            total = total + panels[i, t].astype(jnp.float32) * coeffs[t, i : i + 1, :]
    return total


def rows_kernel(jobs, project, listed, ranks, listed_other, ranks_other, mine, other_far, *refs):
    if project:
        coeffs, coeffs_other, refs = refs[0], refs[1], refs[2:]
    outs, (other, arrived), picks, spreads = refs[: -2 * AHEAD - 2], refs[-2:], refs[-2 * AHEAD - 2 : -AHEAD - 2], refs[-AHEAD - 2 : -2]
    orbits, slots, aux, width = mine.shape
    capacity = listed.shape[1]
    me = lax.axis_index("row")
    copy = pltpu.make_async_copy(other_far, other, arrived)
    copy.start()
    todo = [(job, j) for job in range(len(jobs)) for j in range(len(jobs[job][1]))]

    def spans_of(job, j):
        groups, flips, _ = jobs[job]
        return [
            [
                pl.ds(pl.multiple_of(first_place(me ^ flips[j], region) * width, width), width_of(region) * width)
                for region in group
            ]
            for group in groups
        ]

    def gather(step, side):
        job, j = todo[step]
        row = me ^ jobs[job][1][j]
        picked, spread = picks[step % AHEAD], spreads[step % AHEAD]
        names, places_of, panels = ((listed, ranks, mine), (listed_other, ranks_other, other))[side]
        half = capacity * aux
        for span in sum(spans_of(job, j), []):
            spread[side * half : (side + 1) * half, span] = jnp.zeros((half, span.size), jnp.bfloat16)
        for n in range(capacity):
            code = names[row, n]
            orbit, slot = jnp.maximum(code, 0) >> 3, jnp.maximum(code, 0) & 7
            at = pl.ds((side * capacity + n) * aux, aux)
            chosen = panels[orbit, slot]
            tiles = [panels[orbit, t] for t in range(slots)]
            places = [places_of[t, orbit] ^ row for t in range(slots)]
            picked[at, :] = jnp.where(code >= 0, chosen, jnp.zeros_like(chosen))
            for tile, place in zip(tiles, places):
                spread[at, pl.ds(pl.multiple_of(place * width, width), width)] = tile

    for step in range(min(AHEAD, len(todo))):
        gather(step, 0)
    if project:
        total = density_of(mine, coeffs)
    copy.wait()
    vector = ()
    if project:
        total = jnp.sum((total + density_of(other, coeffs_other)).T, axis=0, keepdims=True)
        total = jnp.concatenate([total, jnp.zeros((1, width - aux), jnp.float32)], axis=1)
        vector, outs[-1][...] = encode_vector(total)
    first, gathered = 0, {}
    for step, (job, j) in enumerate(todo):
        gather(step, 1)
        picked, spread = picks[step % AHEAD], spreads[step % AHEAD]
        sums = [
            [
                lax.dot_general(
                    picked[...],
                    spread[:, span],
                    (((0,), (0,)), ((), ())),
                    preferred_element_type=jnp.float32,
                )
                for span in spans
            ]
            for spans in spans_of(job, j)
        ]
        if step + AHEAD < len(todo):
            gather(step + AHEAD, 0)
        groups, flips, coded = jobs[job]
        for k, parts in enumerate(sums):
            out = outs[first + k]
            row = jnp.concatenate(parts, axis=1) if len(parts) > 1 else parts[0]
            if not coded:
                out[j] = row
                continue
            gathered.setdefault((job, k), []).append(row)
            if j + 1 == len(flips):
                encode(out, gathered[job, k], vector if job + 1 == len(jobs) else ())
        if j + 1 == len(flips):
            first += len(groups)


def partial_rows(jobs, lists, ranks, panels, *coeffs):
    orbits, slots, aux, width = panels[0].shape
    depth = 2 * lists[0].shape[1] * aux
    shapes = []
    for groups, flips, coded in jobs:
        for group in groups:
            columns = sum(width_of(region) for region in group) * width
            if coded:
                shapes.append(message_of(len(flips) * width, columns))
            else:
                shapes.append(sums_of(len(flips), width, columns))
    if coeffs:
        shapes.append(jax.ShapeDtypeStruct((1, width), jnp.float32))
    scalars = pl.BlockSpec(memory_space=pltpu.SMEM)
    whole = pl.BlockSpec(memory_space=pltpu.VMEM)
    return pl.pallas_call(
        functools.partial(rows_kernel, jobs, len(coeffs)),
        in_specs=[scalars] * 4 + [whole, pl.BlockSpec(memory_space=pltpu.HBM)] + [whole] * len(coeffs),
        out_specs=[whole] * len(shapes),
        out_shape=shapes,
        scratch_shapes=[pltpu.VMEM((depth, width), jnp.bfloat16)] * AHEAD
        + [pltpu.VMEM((depth, PLACES * width), jnp.bfloat16)] * AHEAD
        + [pltpu.VMEM(panels[1].shape, jnp.bfloat16), pltpu.SemaphoreType.DMA],
        compiler_params=pltpu.CompilerParams(vmem_limit_bytes=28 << 20),
        cost_estimate=SHORT if coeffs else LONG,
    )(lists[0], ranks[0], lists[1], ranks[1], *panels, *coeffs)


def turn_y_kernel(stay, code, kept, message):
    height = stay.shape[1]
    encode(message, [stay[j] + decode(code, j, height) for j in (1, 2)])
    for k, j in enumerate((0, 3)):
        kept[k] = stay[j] + decode(code, j, height)


def turn_z_kernel(kept, code, own, message):
    height = own.shape[0]
    encode(message, [kept[1] + decode(code, 1, height)])
    own[...] = kept[0] + decode(code, 0, height)


def turn_near_kernel(stay, projected, code, kept, message, vector):
    height = kept.shape[1]
    rows, vector[...] = encode_vector(projected[...] + decode_vector(code, projected.shape[1]))
    encode(message, [stay[j] + decode(code, j, height) for j in (2, 3)], rows)
    for j in range(2):
        kept[j] = stay[j] + decode(code, j, height)


def turn_far_kernel(stay, projected, code, own, message, vector, extra):
    height, width = own.shape[0], extra.shape[1]
    rows, vector[...] = encode_vector(projected[...] + decode_vector(code, projected.shape[1]))
    theirs, mine = [stay[j] + decode(code, j, height) for j in range(2)]
    encode(message, [jnp.concatenate([theirs, mine[:, -width:]], axis=1)], rows)
    own[...] = mine
    extra[...] = theirs[:, -width:]


def message_of(rows, columns):
    return jax.ShapeDtypeStruct((rows + TAIL, columns), jnp.int16)


def small_call(kernel, shapes, *args):
    return pl.pallas_call(
        kernel,
        out_shape=shapes,
        compiler_params=pltpu.CompilerParams(vmem_limit_bytes=16 << 20),
        cost_estimate=SHORT,
    )(*args)


def sums_of(*shape):
    return jax.ShapeDtypeStruct(shape, jnp.float32)


def turn_y(stay, code):
    height, columns = stay.shape[1:]
    shapes = [sums_of(2, height, columns), message_of(2 * height, columns)]
    return small_call(turn_y_kernel, shapes, stay, code)


def turn_z(kept, code):
    height, columns = kept.shape[1:]
    shapes = [sums_of(height, columns), message_of(height, columns)]
    return small_call(turn_z_kernel, shapes, kept, code)


def turn_near(stay, projected, code):
    height, columns = stay.shape[1:]
    shapes = [sums_of(2, height, columns), message_of(2 * height, columns), sums_of(1, projected.shape[1])]
    return small_call(turn_near_kernel, shapes, stay, projected, code)


def turn_far(stay, projected, code):
    height, columns = stay.shape[1:]
    shapes = [sums_of(height, columns), message_of(height, columns + height), sums_of(*projected.shape)]
    shapes.append(sums_of(height, height))
    return small_call(turn_far_kernel, shapes, stay, projected, code)


def coulomb_kernel(vector, metric, tiles, fitted, out):
    aux, height, width = tiles.shape[1:]
    column = jnp.sum(metric[...] * vector[0:1, :aux], axis=1, keepdims=True)
    fitted[...] = jnp.broadcast_to(column, (aux, width)).T[0:1, :]
    total = jnp.zeros((height, width), jnp.float32)
    for p in range(aux):
        total = total + column[p : p + 1, 0:1] * tiles[0, p].astype(jnp.float32)
    out[0] = total.astype(jnp.bfloat16)


def coulomb_tile(vector, metric_inv, three_index):
    aux, height, width = three_index.shape[1:]
    return pl.pallas_call(
        coulomb_kernel,
        out_shape=[
            jax.ShapeDtypeStruct((1, aux), jnp.float32),
            jax.ShapeDtypeStruct((1, height, width), jnp.bfloat16),
        ],
        compiler_params=pltpu.CompilerParams(vmem_limit_bytes=16 << 20),
        cost_estimate=SHORT,
    )(vector, metric_inv, three_index)


def finish_row(total, done, *backs):
    height = total.shape[0]
    done[...] = total.astype(jnp.bfloat16)
    for k, out in enumerate(backs):
        for b in range(2):
            at = (2 * k + b) * height
            out[b] = total[:, at : at + height].T.astype(jnp.bfloat16)


def blocks_of(count, height):
    return jax.ShapeDtypeStruct((count, height, height), jnp.bfloat16)


def finish_early_kernel(own, vector, extra, code, done, back, other_extra, vector_out):
    height, columns = own.shape
    came = decode(code, 0, height)
    finish_row(own[...] + came[:, :columns], done, back)
    other_extra[...] = (extra[...] + came[:, columns:]).T.astype(jnp.bfloat16)
    vector_out[...] = vector[...] + decode_vector(code, vector.shape[1])


def finish_early(own, vector, extra, code):
    height = own.shape[0]
    shapes = [jax.ShapeDtypeStruct(own.shape, jnp.bfloat16), blocks_of(2, height)]
    shapes += [jax.ShapeDtypeStruct((height, height), jnp.bfloat16), sums_of(*vector.shape)]
    return small_call(finish_early_kernel, shapes, own, vector, extra, code)


def finish_late_kernel(own, code, done, *backs):
    finish_row(own[...] + decode(code, 0, own.shape[0]), done, *backs)


def finish_late(own, code):
    backs = [blocks_of(2, own.shape[0])] * len(SOONER)
    return small_call(finish_late_kernel, [jax.ShapeDtypeStruct(own.shape, jnp.bfloat16)] + backs, own, code)


def give_back(blocks, region):
    came = lax.ppermute(blocks, "row", [(i, i ^ first_place(i, region)) for i in range(ROWS)])
    return came, send(came, CORE)


def assemble_kernel(holders, early, late, later, code, extra, extra_core, *refs):
    came, out = refs[:-1], refs[-1]
    width = early.shape[0]
    me = lax.axis_index("row")

    def put(place, block):
        where = pl.ds(pl.multiple_of(holders[place ^ me] * width, width), width)
        out[0, :, where] = block

    base = (later[...] + decode(code, 0, width)).astype(jnp.bfloat16)
    for group, rows in ((Z_FIRST, early), (SOONER, late), (LATER, base)):
        at = 0
        for region in group:
            start = first_place(me, region)
            for b in range(width_of(region)):
                put(start + b, rows[:, at * width : (at + 1) * width])
                at += 1
    put(5 - first_place(me, "extra"), jnp.where((me >> 1) & 1 == 0, extra_core[...], extra[...]))
    for k, region in enumerate((Z_FIRST[0], *SOONER)):
        start = region * 8 + 2 - first_place(me, region)
        put(start, came[2 * k][0])
        put(start + 1, came[2 * k + 1][1])


def assemble(row_block, early, *rest):
    width = early.shape[0]
    vmem = pl.BlockSpec(memory_space=pltpu.VMEM)
    return pl.pallas_call(
        assemble_kernel,
        in_specs=[pl.BlockSpec(memory_space=pltpu.SMEM)] + [vmem] * (1 + len(rest)),
        out_shape=jax.ShapeDtypeStruct((1, width, ROWS * width), jnp.bfloat16),
        compiler_params=pltpu.CompilerParams(vmem_limit_bytes=16 << 20),
        cost_estimate=SHORT,
    )(row_block, early, *rest)


def naming(blocks, row_block, capacity):
    slots, orbits = blocks.shape
    holders = jnp.arange(ROWS, dtype=jnp.int32)
    hits = (blocks[:, :, None] == row_block[None, None, :]).astype(jnp.int32)
    rank = jnp.sum(hits * holders, axis=2)
    named = jnp.sum(hits, axis=0)
    code = jnp.arange(orbits, dtype=jnp.int32)[:, None] * 8 + jnp.sum(
        hits * jnp.arange(slots, dtype=jnp.int32)[:, None, None], axis=0
    )
    earlier = (jnp.arange(orbits)[None, :] < jnp.arange(orbits)[:, None]).astype(jnp.int32)
    before = jnp.sum(earlier[:, :, None] * named[None, :, :], axis=1)
    here = (before[:, :, None] == jnp.arange(capacity)) & (named[:, :, None] > 0)
    listed = jnp.sum(jnp.where(here, code[:, :, None] + 1, 0), axis=0) - 1
    return listed, rank


def summed_rows(panels, blocks, row_block, coeffs, metric_inv, three_index):
    orbits, slots, aux, width = panels.shape
    capacity = orbits * slots // ROWS

    other = send(panels, CORE)
    coeffs = coeffs.transpose(1, 0, 2)
    coeffs_other = send(coeffs, CORE)
    listed, rank = naming(blocks.T, row_block, capacity)
    listed_other, rank_other = send(listed, CORE), send(rank, CORE)
    listed, rank, panels = lax.optimization_barrier((listed, rank, panels))
    mine = bring(panels)
    ranks, sides = (rank, rank_other), (mine, other)

    jobs = ((SOONER, LATER), [Y] + [z | Y for z in Z], True), ((Z_FIRST,), [4 | Y, 4, 8 | Y, 8], True)
    late_go, later_go, early_go, vector = partial_rows(
        jobs, (listed, listed_other), ranks, sides, coeffs, coeffs_other
    )
    late_code = send(late_go, Y)
    early_code = send(early_go, NEAR)
    later_code = send(later_go, Y)

    listed, *_ = lax.optimization_barrier((listed, late_go, early_go, later_go))
    jobs = ((Z_FIRST,), [Y, 0, 12 | Y, 12], False), ((SOONER, LATER), [0, *Z], False)
    early_stay, late_stay, later_stay = partial_rows(jobs, (listed, listed_other), ranks, sides)

    early_stay, early_turn, vector = turn_near(early_stay, vector, early_code)
    early_code = send(early_turn, FAR)
    late, late_turn = turn_y(late_stay, late_code)
    late, late_turn = turn_z(late, send(late_turn, NEAR))
    late_code = send(late_turn, FAR)
    later, later_turn = turn_y(later_stay, later_code)
    later, later_turn = turn_z(later, send(later_turn, NEAR))
    later_code = send(later_turn, FAR)

    early_stay, *_ = lax.optimization_barrier((early_stay, late_turn))
    early_own, early_turn, vector, extra = turn_far(early_stay, vector, early_code)
    early, early_back, extra, vector = finish_early(early_own, vector, extra, send(early_turn, Y))
    came = give_back(early_back, Z_FIRST[0])
    extra_core = send(extra, CORE)
    fitted, coulomb = coulomb_tile(vector, metric_inv, three_index)

    late, *_ = lax.optimization_barrier((late, coulomb))
    late, *late_back = finish_late(late, late_code)
    for blocks, region in zip(late_back, SOONER):
        came += give_back(blocks, region)
    exchange = assemble(row_block, early, late, later, later_code, extra, extra_core, *came)
    return (exchange, coulomb, fitted[0])


def solution(mesh):
    placed = (
        P(("groups", "row"), None, None, None),
        P(("groups", "row"), None),
        P("groups"),
        P(("groups", "row"), None, None),
        P("groups", None),
        P(("groups", "row"), None, None, None),
    )
    return jax.shard_map(
        summed_rows if mesh.shape["row"] == ROWS else sent_panels,
        mesh=mesh,
        in_specs=placed,
        out_specs=(P(("groups", "row"), None, None), P(("groups", "row"), None, None), P("groups")),
        check_vma=False,
    )
```

time: 75 us -> 63.3 us (0.84)
  waiting for transfers between devices: 28.2 us -> 21.9 us
  starting transfers between devices: 24 us -> 20.1 us
  local copies, waits for them, and re-layouts: 3.65 us -> 2.14 us
    ppermute x7 -> x3, starting transfers between devices: 7.78 us -> 3.71 us  [give_back(): lax.ppermute(blocks, 'row', [(i, i ^ first_place(i, region)) for i in ran...]
    ppermute x12 -> x17, waiting for transfers between devices: 24.1 us -> 20.8 us  [send(): return lax.ppermute(x, 'row', [(i, i ^ flip) for i in range(ROWS)])]
    ppermute x7 -> x3, waiting for transfers between devices: 4.1 us -> 1.05 us  [give_back(): lax.ppermute(blocks, 'row', [(i, i ^ first_place(i, region)) for i in ran...]
    unnamed x25 -> x10, local copies, waits for them, and re-layouts: 3.48 us -> 2.06 us
    ppermute x12 -> x17, starting transfers between devices: 16.2 us -> 16.4 us  [send(): return lax.ppermute(x, 'row', [(i, i ^ flip) for i in range(ROWS)])]
  transfers between devices with their start and end apart: 19 -> 20, of which waited for: 9 -> 7; matrix products, arithmetic and copies ran while one was open for 3% -> 2% of each run, Pallas kernels for 8% -> 13%
where the time goes in v4:
time: 63.3 us; the launch traced here: 63 us
  waiting for transfers between devices  21.9 us (35%)
  starting transfers between devices  20.1 us (32%)
  Pallas kernels  16.8 us (27%)
  local copies, waits for them, and re-layouts  2.14 us (3%)
  other arithmetic  1.18 us (2%)
  between operations  0.84 us (1%)
    ppermute x17, waiting for transfers between devices, send(): return lax.ppermute(x, 'row', [(i, i ^ flip) for i in range(ROWS)])  20.8 us
    ppermute x17, starting transfers between devices, send(): return lax.ppermute(x, 'row', [(i, i ^ flip) for i in range(ROWS)])  16.4 us
    pallas_call x2, Pallas kernels, partial_rows(): pl.pallas_call(functools.partial(rows_kernel, jobs, len(coeffs)), in_spec...  13 us
    ppermute x3, starting transfers between devices, give_back(): lax.ppermute(blocks, 'row', [(i, i ^ first_place(i, region)) for i in ran...  3.71 us
    unnamed x10, local copies, waits for them, and re-layouts  2.06 us
    pallas_call x1, Pallas kernels, assemble(): pl.pallas_call(assemble_kernel, in_specs=[pl.BlockSpec(memory_space=pltpu...  1.51 us
  transfers between devices with their start and end apart: 20, of which 7 were waited for; matrix products, arithmetic and copies ran while one was open for 2% of the time, Pallas kernels for 13%

profile of v4, /device:TPU:0, one launch (start us, length us, event | category | flops | bytes accessed | tf_op | source)
XLA Modules:
  0.0 63.0 jit_solution(13821886301726369876)
XLA Ops:
  0.6 0.5 collective-permute-start.2
  1.1 0.9 %fusion.2 = (s32[6,16]{1,0:T(8,128)S(1)}, s32[16,16]{1,0:T(8,128)S(1)}, s32[16,16]{1,0:T(8,128)S(1)}) fusion(s32[16]{0:T(128)} %holders.1, s32[6,16]{1,0:T(8,128)} %bitcast.5), kind=kLoop, calls=%fused_computation.6 | loop fusion | flops 10144 | bytes 2880 | tf_op jit(solution)/shard_map/reduce_sum | solution.py:464
  2.1 0.1 collective-permute-start.1
  2.2 0.5 collective-permute-start.3
  3.1 1.4 %copy-done.1 = bf16[16,6,64,128]{3,2,1,0:T(8,128)(2,1)S(1)} copy-done((bf16[16,6,64,128]{3,2,1,0:T(8,128)(2,1)S(1)}, bf16[16,6,64,128]{3,2,1,0:T(8,128)(2,1)}, u32[]{:S(2)}) %copy-start.1) | copy-done | bytes 1572888
  4.7 0.6 %copy-done.2 = f32[16,6,128]{2,0,1:T(8,128)S(1)} copy-done((f32[16,6,128]{2,0,1:T(8,128)S(1)}, f32[16,6,128]{2,0,1:T(8,128)}, u32[]{:S(2)}) %copy-start.2) | copy-done | bytes 49176
  5.3 6.9 %shard_map.86 = (s16[520,512]{1,0:T(8,128)(2,1)S(1)}, s16[520,256]{1,0:T(8,128)(2,1)S(1)}, s16[520,384]{1,0:T(8,128)(2,1)S(1)}, f32[1,128]{1,0:T(1,128)S(1)}) custom-call(s32[16,6]{1,0:T(8,128)S(1)} %broadcast_add_fusion.listed, s32[6,16]{1,0:T(8,128)S(1)} %get-tuple-element.41.ranks, s32[16,6]{1,0:T(8,128)S(1)} %collective-permute-done.listed_other, ...), custom_call_target="tpu_custom_call" | custom-call | flops 1024 | bytes 1024 | tf_op jit(solution)/shard_map/pallas_call | solution.py:274
  12.2 3.1 %collective-permute-start.4 = (s16[520,384]{1,0:T(8,128)(2,1)S(1)}, s16[520,384]{1,0:T(8,128)(2,1)S(1)}, u32[]{:S(2)}, u32[]{:S(2)}) collective-permute-start(s16[520,384]{1,0:T(8,128)(2,1)S(1)} %get-tuple-element.44), channel_id=1, source_target_pairs={{0,4},{1,5},{2,6},{3,7},{4,0},{5,1},{6,2},{7,3},{8,12},{9,13},{10,... | collective-permute-start | bytes 1198088 | tf_op jit(solution)/shard_map/ppermute | solution.py:91
  15.2 1.5 %collective-permute-start.5 = (s16[520,512]{1,0:T(8,128)(2,1)S(1)}, s16[520,512]{1,0:T(8,128)(2,1)S(1)}, u32[]{:S(2)}, u32[]{:S(2)}) collective-permute-start(s16[520,512]{1,0:T(8,128)(2,1)S(1)} %get-tuple-element.43), channel_id=1, source_target_pairs={{0,2},{1,3},{2,0},{3,1},{4,6},{5,7},{6,4},{7,5},{8,10},{9,11},{10,... | collective-permute-start | bytes 1597448 | tf_op jit(solution)/shard_map/ppermute | solution.py:91
  16.7 6.1 %shard_map.87 = (f32[4,128,384]{2,1,0:T(8,128)S(1)}, f32[4,128,512]{2,1,0:T(8,128)S(1)}, f32[4,128,256]{2,1,0:T(8,128)S(1)}) custom-call(s32[16,6]{1,0:T(8,128)S(1)} %broadcast_add_fusion.listed, s32[6,16]{1,0:T(8,128)S(1)} %get-tuple-element.41.ranks, s32[16,6]{1,0:T(8,128)S(1)} %collective-permute-done.listed_other, ...), custom_call_target="tpu_custom_call" | custom-call | flops 17179869184 | bytes 1024 | tf_op jit(solution)/shard_map/pallas_call | solution.py:274
  22.9 6.2 %collective-permute-done.5.code = s16[520,512]{1,0:T(8,128)(2,1)S(1)} collective-permute-done((s16[520,512]{1,0:T(8,128)(2,1)S(1)}, s16[520,512]{1,0:T(8,128)(2,1)S(1)}, u32[]{:S(2)}, u32[]{:S(2)}) %collective-permute-start.5) | collective-permute-done | bytes 532512 | tf_op jit(solution)/shard_map/ppermute | solution.py:91
  29.0 0.3 shard_map.89
  29.3 0.4 collective-permute-start.6
  29.7 0.2 shard_map.88
  29.9 3.8 %collective-permute-start.7 = (s16[264,384]{1,0:T(8,128)(2,1)S(1)}, s16[264,384]{1,0:T(8,128)(2,1)S(1)}, u32[]{:S(2)}, u32[]{:S(2)}) collective-permute-start(s16[264,384]{1,0:T(8,128)(2,1)S(1)} %get-tuple-element.56), channel_id=1, source_target_pairs={{0,12},{1,13},{2,14},{3,15},{4,8},{5,9},{6,10},{7,11},{8,4},{9,5},... | collective-permute-start | bytes 608264 | tf_op jit(solution)/shard_map/ppermute | solution.py:91
  33.7 1.5 %collective-permute-start.10 = (s16[520,256]{1,0:T(8,128)(2,1)S(1)}, s16[520,256]{1,0:T(8,128)(2,1)S(1)}, u32[]{:S(2)}, u32[]{:S(2)}) collective-permute-start(s16[520,256]{1,0:T(8,128)(2,1)S(1)} %get-tuple-element.45), channel_id=1, source_target_pairs={{0,2},{1,3},{2,0},{3,1},{4,6},{5,7},{6,4},{7,5},{8,10},{9,11},{10,... | collective-permute-start | bytes 798728 | tf_op jit(solution)/shard_map/ppermute | solution.py:91
  35.2 1.5 %collective-permute-done.6.code = s16[264,512]{1,0:T(8,128)(2,1)S(1)} collective-permute-done((s16[264,512]{1,0:T(8,128)(2,1)S(1)}, s16[264,512]{1,0:T(8,128)(2,1)S(1)}, u32[]{:S(2)}, u32[]{:S(2)}) %collective-permute-start.6) | collective-permute-done | bytes 270368 | tf_op jit(solution)/shard_map/ppermute | solution.py:91
  36.7 0.1 shard_map.90
  36.8 6.3 %collective-permute-done.7.code = s16[264,384]{1,0:T(8,128)(2,1)S(1)} collective-permute-done((s16[264,384]{1,0:T(8,128)(2,1)S(1)}, s16[264,384]{1,0:T(8,128)(2,1)S(1)}, u32[]{:S(2)}, u32[]{:S(2)}) %collective-permute-start.7) | collective-permute-done | bytes 202784 | tf_op jit(solution)/shard_map/ppermute | solution.py:91
  43.3 1.6 %collective-permute-start.8 = (s16[136,512]{1,0:T(8,128)(2,1)S(1)}, s16[136,512]{1,0:T(8,128)(2,1)S(1)}, u32[]{:S(2)}, u32[]{:S(2)}) collective-permute-start(s16[136,512]{1,0:T(8,128)(2,1)S(1)} %get-tuple-element.60), channel_id=1, source_target_pairs={{0,2},{1,3},{2,0},{3,1},{4,6},{5,7},{6,4},{7,5},{8,10},{9,11},{10,... | collective-permute-start | bytes 417800 | tf_op jit(solution)/shard_map/ppermute | solution.py:91
  44.8 0.6 collective-permute-start.9
  45.7 2.8 %collective-permute-done.8.code = s16[136,512]{1,0:T(8,128)(2,1)S(1)} collective-permute-done((s16[136,512]{1,0:T(8,128)(2,1)S(1)}, s16[136,512]{1,0:T(8,128)(2,1)S(1)}, u32[]{:S(2)}, u32[]{:S(2)}) %collective-permute-start.8) | collective-permute-done | bytes 139296 | tf_op jit(solution)/shard_map/ppermute | solution.py:91
  48.6 1.1 %shard_map.93 = (f32[1,64]{1,0:T(1,128)}, bf16[1,128,128]{2,1,0:T(8,128)(2,1)}) custom-call(f32[1,128]{1,0:T(1,128)S(1)} %get-tuple-element.63.vector, f32[64,64]{1,0:T(8,128)S(1)} %copy-done.3, bf16[1,64,128,128]{3,2,1,0:T(8,128)(2,1)S(1)} %copy-done), custom_call_target="tpu_custom_call" | custom-call | flops 1024 | bytes 1024 | tf_op jit(solution)/shard_map/pallas_call | solution.py:371
  49.7 0.5 collective-permute-start.14
  50.2 1.6 %collective-permute-done.9.code = s16[136,512]{1,0:T(8,128)(2,1)S(1)} collective-permute-done((s16[136,512]{1,0:T(8,128)(2,1)S(1)}, s16[136,512]{1,0:T(8,128)(2,1)S(1)}, u32[]{:S(2)}, u32[]{:S(2)}) %collective-permute-start.9) | collective-permute-done | bytes 139296 | tf_op jit(solution)/shard_map/ppermute | solution.py:91
  51.8 0.1 shard_map.94
  52.0 3.2 %collective-permute-start.18 = (bf16[2,128,128]{2,1,0:T(8,128)(2,1)S(1)}, bf16[2,128,128]{2,1,0:T(8,128)(2,1)S(1)}, u32[]{:S(2)}, u32[]{:S(2)}) collective-permute-start(bf16[2,128,128]{2,1,0:T(8,128)(2,1)S(1)} %get-tuple-element.75), channel_id=1, source_target_pairs={{0,8},{1,9},{2,10},{3,11},{4,12},{5,13},{6,14},{7,15},{8,2},{9,3},... | collective-permute-start | bytes 196616 | tf_op jit(solution)/shard_map/ppermute | solution.py:420
  55.3 2.2 %collective-permute-start.12 = (s16[136,256]{1,0:T(8,128)(2,1)S(1)}, s16[136,256]{1,0:T(8,128)(2,1)S(1)}, u32[]{:S(2)}, u32[]{:S(2)}) collective-permute-start(s16[136,256]{1,0:T(8,128)(2,1)S(1)} %get-tuple-element.71), channel_id=1, source_target_pairs={{0,12},{1,13},{2,14},{3,15},{4,8},{5,9},{6,10},{7,11},{8,4},{9,5},... | collective-permute-start | bytes 208904 | tf_op jit(solution)/shard_map/ppermute | solution.py:91
  57.4 1.0 %collective-permute-done.16.refs_2_ = bf16[2,128,128]{2,1,0:T(8,128)(2,1)S(1)} collective-permute-done((bf16[2,128,128]{2,1,0:T(8,128)(2,1)S(1)}, bf16[2,128,128]{2,1,0:T(8,128)(2,1)S(1)}, u32[]{:S(2)}, u32[]{:S(2)}) %collective-permute-start.16) | collective-permute-done | bytes 65568 | tf_op jit(solution)/shard_map/ppermute | solution.py:420
  58.5 0.5 collective-permute-start.19
  59.0 2.4 %collective-permute-done.12.code = s16[136,256]{1,0:T(8,128)(2,1)S(1)} collective-permute-done((s16[136,256]{1,0:T(8,128)(2,1)S(1)}, s16[136,256]{1,0:T(8,128)(2,1)S(1)}, u32[]{:S(2)}, u32[]{:S(2)}) %collective-permute-start.12) | collective-permute-done | bytes 69664 | tf_op jit(solution)/shard_map/ppermute | solution.py:91
  61.5 1.5 %shard_map.97 = bf16[1,128,2048]{2,1,0:T(8,128)(2,1)} custom-call(s32[16]{0:T(128)S(1)} %copy-done.4, bf16[128,384]{1,0:T(8,128)(2,1)S(1)} %get-tuple-element.61.early, bf16[128,512]{1,0:T(8,128)(2,1)S(1)} %get-tuple-element.66.late, f32[128,256]{1,0:T(8,128)S(1)} %get-tuple-element.70.later, s16[136,256]{1,0:T(8,128)(2,1)S(1)} %collective-permute-done.12.code, ...), custom_call_target="tpu_custom_call" | custom-call | flops 1024 | bytes 1024 | tf_op jit(solution)/shard_map/pallas_call | solution.py:451
  (40 shorter events, 1.1 us)
Async XLA Ops:
  0.6 4.0 %collective-permute-start.2 = (bf16[16,6,64,128]{3,2,1,0:T(8,128)(2,1)}, bf16[16,6,64,128]{3,2,1,0:T(8,128)(2,1)S(1)}, u32[]{:S(2)}, u32[]{:S(2)}) collective-permute-start(bf16[16,6,64,128]{3,2,1,0:T(8,128)(2,1)} %far), channel_id=1, source_target_pairs={{0,1},{1,0},{2,3},{3,2},{4,5},{5,4},{6,7},{7,6},{8,9},{9,8},{10,11... | collective-permute-start | bytes 4718600 | tf_op jit(solution)/shard_map/ppermute | solution.py:91
  2.1 2.5 %collective-permute-start.1 = (s32[6,16]{1,0:T(8,128)S(1)}, s32[6,16]{1,0:T(8,128)S(1)}, u32[]{:S(2)}, u32[]{:S(2)}) collective-permute-start(s32[6,16]{1,0:T(8,128)S(1)} %get-tuple-element.41.ranks), channel_id=1, source_target_pairs={{0,1},{1,0},{2,3},{3,2},{4,5},{5,4},{6,7},{7,6},{8,9},{9,8},{10,11... | collective-permute-start | bytes 1160 | tf_op jit(solution)/shard_map/ppermute | solution.py:91
  2.2 2.4 %collective-permute-start.3 = (f32[6,16,128]{2,1,0:T(8,128)}, f32[6,16,128]{2,1,0:T(8,128)S(1)}, u32[]{:S(2)}, u32[]{:S(2)}) collective-permute-start(f32[6,16,128]{2,1,0:T(8,128)} %bitcast.3), channel_id=1, source_target_pairs={{0,1},{1,0},{2,3},{3,2},{4,5},{5,4},{6,7},{7,6},{8,9},{9,8},{10,11... | collective-permute-start | bytes 147464 | tf_op jit(solution)/shard_map/ppermute | solution.py:91
  3.0 1.6 %collective-permute-start = (s32[16,6]{1,0:T(8,128)S(1)}, s32[16,6]{1,0:T(8,128)S(1)}, u32[]{:S(2)}, u32[]{:S(2)}) collective-permute-start(s32[16,6]{1,0:T(8,128)S(1)} %broadcast_add_fusion.listed), channel_id=1, source_target_pairs={{0,1},{1,0},{2,3},{3,2},{4,5},{5,4},{6,7},{7,6},{8,9},{9,8},{10,11... | collective-permute-start | bytes 1160 | tf_op jit(solution)/shard_map/ppermute | solution.py:91
  3.1 1.4 %copy-start.1 = (bf16[16,6,64,128]{3,2,1,0:T(8,128)(2,1)S(1)}, bf16[16,6,64,128]{3,2,1,0:T(8,128)(2,1)}, u32[]{:S(2)}) copy-start(bf16[16,6,64,128]{3,2,1,0:T(8,128)(2,1)} %far) | copy-start | bytes 4718596
  4.5 0.8 %copy-start.2 = (f32[16,6,128]{2,0,1:T(8,128)S(1)}, f32[16,6,128]{2,0,1:T(8,128)}, u32[]{:S(2)}) copy-start(f32[16,6,128]{2,0,1:T(8,128)} %param.9) | copy-start | bytes 147460
  12.2 17.6 %collective-permute-start.4 = (s16[520,384]{1,0:T(8,128)(2,1)S(1)}, s16[520,384]{1,0:T(8,128)(2,1)S(1)}, u32[]{:S(2)}, u32[]{:S(2)}) collective-permute-start(s16[520,384]{1,0:T(8,128)(2,1)S(1)} %get-tuple-element.44), channel_id=1, source_target_pairs={{0,4},{1,5},{2,6},{3,7},{4,0},{5,1},{6,2},{7,3},{8,12},{9,13},{10,... | collective-permute-start | bytes 1198088 | tf_op jit(solution)/shard_map/ppermute | solution.py:91
  15.2 13.8 %collective-permute-start.5 = (s16[520,512]{1,0:T(8,128)(2,1)S(1)}, s16[520,512]{1,0:T(8,128)(2,1)S(1)}, u32[]{:S(2)}, u32[]{:S(2)}) collective-permute-start(s16[520,512]{1,0:T(8,128)(2,1)S(1)} %get-tuple-element.43), channel_id=1, source_target_pairs={{0,2},{1,3},{2,0},{3,1},{4,6},{5,7},{6,4},{7,5},{8,10},{9,11},{10,... | collective-permute-start | bytes 1597448 | tf_op jit(solution)/shard_map/ppermute | solution.py:91
  29.3 7.4 %collective-permute-start.6 = (s16[264,512]{1,0:T(8,128)(2,1)S(1)}, s16[264,512]{1,0:T(8,128)(2,1)S(1)}, u32[]{:S(2)}, u32[]{:S(2)}) collective-permute-start(s16[264,512]{1,0:T(8,128)(2,1)S(1)} %get-tuple-element.52), channel_id=1, source_target_pairs={{0,4},{1,5},{2,6},{3,7},{4,0},{5,1},{6,2},{7,3},{8,12},{9,13},{10,... | collective-permute-start | bytes 811016 | tf_op jit(solution)/shard_map/ppermute | solution.py:91
  29.9 18.6 %copy-start = (bf16[1,64,128,128]{3,2,1,0:T(8,128)(2,1)S(1)}, bf16[1,64,128,128]{3,2,1,0:T(8,128)(2,1)}, u32[]{:S(2)}) copy-start(bf16[1,64,128,128]{3,2,1,0:T(8,128)(2,1)} %tiles.1) | copy-start | bytes 6291460
  29.9 18.6 %copy-start.3 = (f32[64,64]{1,0:T(8,128)S(1)}, f32[64,64]{1,0:T(8,128)}, u32[]{:S(2)}) copy-start(f32[64,64]{1,0:T(8,128)} %metric.1) | copy-start | bytes 49156
  29.9 13.2 %collective-permute-start.7 = (s16[264,384]{1,0:T(8,128)(2,1)S(1)}, s16[264,384]{1,0:T(8,128)(2,1)S(1)}, u32[]{:S(2)}, u32[]{:S(2)}) collective-permute-start(s16[264,384]{1,0:T(8,128)(2,1)S(1)} %get-tuple-element.56), channel_id=1, source_target_pairs={{0,12},{1,13},{2,14},{3,15},{4,8},{5,9},{6,10},{7,11},{8,4},{9,5},... | collective-permute-start | bytes 608264 | tf_op jit(solution)/shard_map/ppermute | solution.py:91
  33.7 11.8 %collective-permute-start.10 = (s16[520,256]{1,0:T(8,128)(2,1)S(1)}, s16[520,256]{1,0:T(8,128)(2,1)S(1)}, u32[]{:S(2)}, u32[]{:S(2)}) collective-permute-start(s16[520,256]{1,0:T(8,128)(2,1)S(1)} %get-tuple-element.45), channel_id=1, source_target_pairs={{0,2},{1,3},{2,0},{3,1},{4,6},{5,7},{6,4},{7,5},{8,10},{9,11},{10,... | collective-permute-start | bytes 798728 | tf_op jit(solution)/shard_map/ppermute | solution.py:91
  43.3 5.1 %collective-permute-start.8 = (s16[136,512]{1,0:T(8,128)(2,1)S(1)}, s16[136,512]{1,0:T(8,128)(2,1)S(1)}, u32[]{:S(2)}, u32[]{:S(2)}) collective-permute-start(s16[136,512]{1,0:T(8,128)(2,1)S(1)} %get-tuple-element.60), channel_id=1, source_target_pairs={{0,2},{1,3},{2,0},{3,1},{4,6},{5,7},{6,4},{7,5},{8,10},{9,11},{10,... | collective-permute-start | bytes 417800 | tf_op jit(solution)/shard_map/ppermute | solution.py:91
  44.8 7.0 %collective-permute-start.9 = (s16[136,512]{1,0:T(8,128)(2,1)S(1)}, s16[136,512]{1,0:T(8,128)(2,1)S(1)}, u32[]{:S(2)}, u32[]{:S(2)}) collective-permute-start(s16[136,512]{1,0:T(8,128)(2,1)S(1)} %get-tuple-element.53), channel_id=1, source_target_pairs={{0,12},{1,13},{2,14},{3,15},{4,8},{5,9},{6,10},{7,11},{8,4},{9,5},... | collective-permute-start | bytes 417800 | tf_op jit(solution)/shard_map/ppermute | solution.py:91
  45.6 9.6 %collective-permute-start.11 = (s16[264,256]{1,0:T(8,128)(2,1)S(1)}, s16[264,256]{1,0:T(8,128)(2,1)S(1)}, u32[]{:S(2)}, u32[]{:S(2)}) collective-permute-start(s16[264,256]{1,0:T(8,128)(2,1)S(1)} %get-tuple-element.69), channel_id=1, source_target_pairs={{0,4},{1,5},{2,6},{3,7},{4,0},{5,1},{6,2},{7,3},{8,12},{9,13},{10,... | collective-permute-start | bytes 405512 | tf_op jit(solution)/shard_map/ppermute | solution.py:91
  48.5 12.9 %copy-start.4 = (s32[16]{0:T(128)S(1)}, s32[16]{0:T(128)}, u32[]{:S(2)}) copy-start(s32[16]{0:T(128)} %holders.1) | copy-start | bytes 196
  49.7 7.8 %collective-permute-start.14 = (bf16[2,128,128]{2,1,0:T(8,128)(2,1)S(1)}, bf16[2,128,128]{2,1,0:T(8,128)(2,1)S(1)}, u32[]{:S(2)}, u32[]{:S(2)}) collective-permute-start(bf16[2,128,128]{2,1,0:T(8,128)(2,1)S(1)} %get-tuple-element.73), channel_id=1, source_target_pairs={{0,12},{1,13},{2,14},{3,15},{4,10},{5,11},{6,8},{7,9},{8,4},{9,5},... | collective-permute-start | bytes 196616 | tf_op jit(solution)/shard_map/ppermute | solution.py:420
  51.9 6.5 %collective-permute-start.16 = (bf16[2,128,128]{2,1,0:T(8,128)(2,1)S(1)}, bf16[2,128,128]{2,1,0:T(8,128)(2,1)S(1)}, u32[]{:S(2)}, u32[]{:S(2)}) collective-permute-start(bf16[2,128,128]{2,1,0:T(8,128)(2,1)S(1)} %get-tuple-element.74), channel_id=1, source_target_pairs={{0,4},{1,5},{2,6},{3,7},{4,2},{5,3},{6,0},{7,1},{8,12},{9,13},{10,... | collective-permute-start | bytes 196616 | tf_op jit(solution)/shard_map/ppermute | solution.py:420
  52.0 6.5 %collective-permute-start.18 = (bf16[2,128,128]{2,1,0:T(8,128)(2,1)S(1)}, bf16[2,128,128]{2,1,0:T(8,128)(2,1)S(1)}, u32[]{:S(2)}, u32[]{:S(2)}) collective-permute-start(bf16[2,128,128]{2,1,0:T(8,128)(2,1)S(1)} %get-tuple-element.75), channel_id=1, source_target_pairs={{0,8},{1,9},{2,10},{3,11},{4,12},{5,13},{6,14},{7,15},{8,2},{9,3},... | collective-permute-start | bytes 196616 | tf_op jit(solution)/shard_map/ppermute | solution.py:420
  55.3 6.2 %collective-permute-start.12 = (s16[136,256]{1,0:T(8,128)(2,1)S(1)}, s16[136,256]{1,0:T(8,128)(2,1)S(1)}, u32[]{:S(2)}, u32[]{:S(2)}) collective-permute-start(s16[136,256]{1,0:T(8,128)(2,1)S(1)} %get-tuple-element.71), channel_id=1, source_target_pairs={{0,12},{1,13},{2,14},{3,15},{4,8},{5,9},{6,10},{7,11},{8,4},{9,5},... | collective-permute-start | bytes 208904 | tf_op jit(solution)/shard_map/ppermute | solution.py:91
  57.4 4.0 %collective-permute-start.15 = (bf16[2,128,128]{2,1,0:T(8,128)(2,1)S(1)}, bf16[2,128,128]{2,1,0:T(8,128)(2,1)S(1)}, u32[]{:S(2)}, u32[]{:S(2)}) collective-permute-start(bf16[2,128,128]{2,1,0:T(8,128)(2,1)S(1)} %collective-permute-done.14.refs_0_), channel_id=1, source_target_pairs={{0,1},{1,0},{2,3},{3,2},{4,5},{5,4},{6,7},{7,6},{8,9},{9,8},{10,11... | collective-permute-start | bytes 196616 | tf_op jit(solution)/shard_map/ppermute | solution.py:91
  58.5 3.0 %collective-permute-start.17 = (bf16[2,128,128]{2,1,0:T(8,128)(2,1)S(1)}, bf16[2,128,128]{2,1,0:T(8,128)(2,1)S(1)}, u32[]{:S(2)}, u32[]{:S(2)}) collective-permute-start(bf16[2,128,128]{2,1,0:T(8,128)(2,1)S(1)} %collective-permute-done.16.refs_2_), channel_id=1, source_target_pairs={{0,1},{1,0},{2,3},{3,2},{4,5},{5,4},{6,7},{7,6},{8,9},{9,8},{10,11... | collective-permute-start | bytes 196616 | tf_op jit(solution)/shard_map/ppermute | solution.py:91
  58.5 3.0 %collective-permute-start.19 = (bf16[2,128,128]{2,1,0:T(8,128)(2,1)S(1)}, bf16[2,128,128]{2,1,0:T(8,128)(2,1)S(1)}, u32[]{:S(2)}, u32[]{:S(2)}) collective-permute-start(bf16[2,128,128]{2,1,0:T(8,128)(2,1)S(1)} %collective-permute-done.18.refs_4_), channel_id=1, source_target_pairs={{0,1},{1,0},{2,3},{3,2},{4,5},{5,4},{6,7},{7,6},{8,9},{9,8},{10,11... | collective-permute-start | bytes 196616 | tf_op jit(solution)/shard_map/ppermute | solution.py:91
  59.0 2.4 %collective-permute-start.13 = (bf16[128,128]{1,0:T(8,128)(2,1)S(1)}, bf16[128,128]{1,0:T(8,128)(2,1)S(1)}, u32[]{:S(2)}, u32[]{:S(2)}) collective-permute-start(bf16[128,128]{1,0:T(8,128)(2,1)S(1)} %get-tuple-element.72.extra), channel_id=1, source_target_pairs={{0,1},{1,0},{2,3},{3,2},{4,5},{5,4},{6,7},{7,6},{8,9},{9,8},{10,11... | collective-permute-start | bytes 98312 | tf_op jit(solution)/shard_map/ppermute | solution.py:91

commit v5 on v4

--- a/solution.py
+++ b/solution.py
@@ -78,13 +78,14 @@
 CORE, Y, Z = 1, 2, (4, 8, 12)
 NEAR, FAR = 4, 12
 PLACES = 16
-Z_FIRST, SOONER, LATER = (3, "extra"), (1, 2), (0,)
+Z_FIRST, SOONER, LATER = (3, "extra"), (1, "diagonal"), (2, "mate")
 TAIL = 8
 TOP = 14.99
+SPARE = 0
 VECTOR = 4
 AHEAD = 6
 SHORT = pl.CostEstimate(flops=1024, bytes_accessed=1024, transcendentals=0)
-LONG = pl.CostEstimate(flops=1 << 34, bytes_accessed=1024, transcendentals=0)
+LONG = pl.CostEstimate(flops=1 << 32, bytes_accessed=1024, transcendentals=0)
 
 
 def send(x, flip):
@@ -96,21 +97,30 @@
 
 
 def first_place(row, region):
-    if region == 0:
-        return 0
+    if region in ("diagonal", "mate"):
+        return int(region == "mate")
     if region == "extra":
         return 2 + ((row >> 1) & 1)
     return region * 4 + side_of(row >> 2, region) * 2
 
 
+def returned(group):
+    return [region for region in group if region in (1, 2, 3)]
+
+
+def spare_of(region):
+    return {Z_FIRST[0]: 32, SOONER[0]: 16, LATER[0]: 0}[region]
+
+
 def width_of(region):
-    return 1 if region == "extra" else 2
+    return 2 if region in (1, 2, 3) else 1
 
 
 def encode(out, sums, vector=()):
     height, columns = sums[0].shape
-    line = lax.broadcasted_iota(jnp.int32, (TAIL, columns), 0)
-    tail = jnp.zeros((TAIL, columns), jnp.float32)
+    rest = out.shape[0] - len(sums) * height
+    line = lax.broadcasted_iota(jnp.int32, (rest, columns), 0)
+    tail = jnp.zeros((rest, columns), jnp.float32)
     for j, x in enumerate(sums):
         peak = jnp.maximum(jnp.max(jnp.abs(x), axis=0, keepdims=True), 2.0**-100)
         exponent = jnp.ceil(jnp.log2(peak) * 8)
@@ -118,8 +128,8 @@
         out[j * height : (j + 1) * height, :] = scaled.astype(jnp.int32).astype(jnp.int16)
         tail = jnp.where(line == j, exponent, tail)
     for j, x in enumerate(vector):
-        rest = jnp.zeros((1, columns - x.shape[1]), jnp.float32)
-        tail = jnp.where(line == VECTOR + j, jnp.concatenate([x, rest], axis=1), tail)
+        beside = jnp.zeros((1, columns - x.shape[1]), jnp.float32)
+        tail = jnp.where(line == VECTOR + j, jnp.concatenate([x, beside], axis=1), tail)
     out[len(sums) * height :, :] = tail.astype(jnp.int32).astype(jnp.int16)
 
 
@@ -264,7 +274,8 @@
         for group in groups:
             columns = sum(width_of(region) for region in group) * width
             if coded:
-                shapes.append(message_of(len(flips) * width, columns))
+                spare = SPARE if group == LATER else 0
+                shapes.append(message_of(len(flips) * width, columns, spare))
             else:
                 shapes.append(sums_of(len(flips), width, columns))
     if coeffs:
@@ -280,7 +291,7 @@
         + [pltpu.VMEM((depth, PLACES * width), jnp.bfloat16)] * AHEAD
         + [pltpu.VMEM(panels[1].shape, jnp.bfloat16), pltpu.SemaphoreType.DMA],
         compiler_params=pltpu.CompilerParams(vmem_limit_bytes=28 << 20),
-        cost_estimate=SHORT if coeffs else LONG,
+        cost_estimate=SHORT,
     )(lists[0], ranks[0], lists[1], ranks[1], *panels, *coeffs)
 
 
@@ -314,16 +325,16 @@
     extra[...] = theirs[:, -width:]
 
 
-def message_of(rows, columns):
-    return jax.ShapeDtypeStruct((rows + TAIL, columns), jnp.int16)
-
-
-def small_call(kernel, shapes, *args):
+def message_of(rows, columns, spare=0):
+    return jax.ShapeDtypeStruct((rows + TAIL + spare, columns), jnp.int16)
+
+
+def small_call(kernel, shapes, *args, cost=SHORT):
     return pl.pallas_call(
         kernel,
         out_shape=shapes,
         compiler_params=pltpu.CompilerParams(vmem_limit_bytes=16 << 20),
-        cost_estimate=SHORT,
+        cost_estimate=cost,
     )(*args)
 
 
@@ -331,15 +342,15 @@
     return jax.ShapeDtypeStruct(shape, jnp.float32)
 
 
-def turn_y(stay, code):
+def turn_y(stay, code, spare):
     height, columns = stay.shape[1:]
-    shapes = [sums_of(2, height, columns), message_of(2 * height, columns)]
+    shapes = [sums_of(2, height, columns), message_of(2 * height, columns, spare)]
     return small_call(turn_y_kernel, shapes, stay, code)
 
 
-def turn_z(kept, code):
+def turn_z(kept, code, spare):
     height, columns = kept.shape[1:]
-    shapes = [sums_of(height, columns), message_of(height, columns)]
+    shapes = [sums_of(height, columns), message_of(height, columns, spare)]
     return small_call(turn_z_kernel, shapes, kept, code)
 
 
@@ -385,24 +396,30 @@
     for k, out in enumerate(backs):
         for b in range(2):
             at = (2 * k + b) * height
-            out[b] = total[:, at : at + height].T.astype(jnp.bfloat16)
-
-
-def blocks_of(count, height):
-    return jax.ShapeDtypeStruct((count, height, height), jnp.bfloat16)
-
-
-def finish_early_kernel(own, vector, extra, code, done, back, other_extra, vector_out):
+            out[b * height : (b + 1) * height, :] = total[:, at : at + height].T.astype(jnp.bfloat16)
+        if out.shape[0] > 2 * height:
+            out[2 * height :, :] = jnp.zeros((out.shape[0] - 2 * height, height), jnp.bfloat16)
+
+
+def backs_of(group, height):
+    return [
+        jax.ShapeDtypeStruct((2 * height + spare_of(region), height), jnp.bfloat16)
+        for region in returned(group)
+    ]
+
+
+def finish_early_kernel(own, vector, extra, code, done, *refs):
     height, columns = own.shape
+    *backs, other_extra, vector_out = refs
     came = decode(code, 0, height)
-    finish_row(own[...] + came[:, :columns], done, back)
+    finish_row(own[...] + came[:, :columns], done, *backs)
     other_extra[...] = (extra[...] + came[:, columns:]).T.astype(jnp.bfloat16)
     vector_out[...] = vector[...] + decode_vector(code, vector.shape[1])
 
 
 def finish_early(own, vector, extra, code):
     height = own.shape[0]
-    shapes = [jax.ShapeDtypeStruct(own.shape, jnp.bfloat16), blocks_of(2, height)]
+    shapes = [jax.ShapeDtypeStruct(own.shape, jnp.bfloat16)] + backs_of(Z_FIRST, height)
     shapes += [jax.ShapeDtypeStruct((height, height), jnp.bfloat16), sums_of(*vector.shape)]
     return small_call(finish_early_kernel, shapes, own, vector, extra, code)
 
@@ -411,9 +428,9 @@
     finish_row(own[...] + decode(code, 0, own.shape[0]), done, *backs)
 
 
-def finish_late(own, code):
-    backs = [blocks_of(2, own.shape[0])] * len(SOONER)
-    return small_call(finish_late_kernel, [jax.ShapeDtypeStruct(own.shape, jnp.bfloat16)] + backs, own, code)
+def finish_late(own, code, group, cost=SHORT):
+    backs = backs_of(group, own.shape[0])
+    return small_call(finish_late_kernel, [jax.ShapeDtypeStruct(own.shape, jnp.bfloat16)] + backs, own, code, cost=cost)
 
 
 def give_back(blocks, region):
@@ -421,7 +438,11 @@
     return came, send(came, CORE)
 
 
-def assemble_kernel(holders, early, late, later, code, extra, extra_core, *refs):
+def return_all(backs, group):
+    return sum((give_back(blocks, region) for blocks, region in zip(backs, returned(group))), ())
+
+
+def assemble_kernel(holders, early, late, later, extra, extra_core, *refs):
     came, out = refs[:-1], refs[-1]
     width = early.shape[0]
     me = lax.axis_index("row")
@@ -430,19 +451,20 @@
         where = pl.ds(pl.multiple_of(holders[place ^ me] * width, width), width)
         out[0, :, where] = block
 
-    base = (later[...] + decode(code, 0, width)).astype(jnp.bfloat16)
-    for group, rows in ((Z_FIRST, early), (SOONER, late), (LATER, base)):
+    k = 0
+    for group, rows in ((Z_FIRST, early), (SOONER, late), (LATER, later)):
         at = 0
         for region in group:
             start = first_place(me, region)
             for b in range(width_of(region)):
                 put(start + b, rows[:, at * width : (at + 1) * width])
                 at += 1
+            if region in returned(group):
+                start = region * 8 + 2 - start
+                put(start, came[k][:width, :])
+                put(start + 1, came[k + 1][width : 2 * width, :])
+                k += 2
     put(5 - first_place(me, "extra"), jnp.where((me >> 1) & 1 == 0, extra_core[...], extra[...]))
-    for k, region in enumerate((Z_FIRST[0], *SOONER)):
-        start = region * 8 + 2 - first_place(me, region)
-        put(start, came[2 * k][0])
-        put(start + 1, came[2 * k + 1][1])
 
 
 def assemble(row_block, early, *rest):
@@ -500,25 +522,26 @@
 
     early_stay, early_turn, vector = turn_near(early_stay, vector, early_code)
     early_code = send(early_turn, FAR)
-    late, late_turn = turn_y(late_stay, late_code)
-    late, late_turn = turn_z(late, send(late_turn, NEAR))
+    late, late_turn = turn_y(late_stay, late_code, 8)
+    near_code = send(late_turn, NEAR)
+    later, later_turn = turn_y(later_stay, later_code, 0)
+    late, late_turn = turn_z(late, near_code, 8)
     late_code = send(late_turn, FAR)
-    later, later_turn = turn_y(later_stay, later_code)
-    later, later_turn = turn_z(later, send(later_turn, NEAR))
+    later, later_turn = turn_z(later, send(later_turn, NEAR), 0)
     later_code = send(later_turn, FAR)
 
-    early_stay, *_ = lax.optimization_barrier((early_stay, late_turn))
     early_own, early_turn, vector, extra = turn_far(early_stay, vector, early_code)
-    early, early_back, extra, vector = finish_early(early_own, vector, extra, send(early_turn, Y))
-    came = give_back(early_back, Z_FIRST[0])
+    early, *early_back, extra, vector = finish_early(early_own, vector, extra, send(early_turn, Y))
+    came = return_all(early_back, Z_FIRST)
     extra_core = send(extra, CORE)
     fitted, coulomb = coulomb_tile(vector, metric_inv, three_index)
 
-    late, *_ = lax.optimization_barrier((late, coulomb))
-    late, *late_back = finish_late(late, late_code)
-    for blocks, region in zip(late_back, SOONER):
-        came += give_back(blocks, region)
-    exchange = assemble(row_block, early, late, later, later_code, extra, extra_core, *came)
+    late, coulomb = lax.optimization_barrier((late, coulomb))
+    late, *back = finish_late(late, late_code, SOONER)
+    came += return_all(back, SOONER)
+    later, *back = finish_late(later, later_code, LATER)
+    came += return_all(back, LATER)
+    exchange = assemble(row_block, early, late, later, extra, extra_core, *came)
     return (exchange, coulomb, fitted[0])
 
 

time: 63.3 us -> 61.8 us (0.976)
  waiting for transfers between devices: 21.9 us -> 14.1 us
  starting transfers between devices: 20.1 us -> 25.1 us
  Pallas kernels: 16.8 us -> 17.8 us
    ppermute x17, waiting for transfers between devices: 20.8 us -> 10.7 us  [send(): return lax.ppermute(x, 'row', [(i, i ^ flip) for i in range(ROWS)])]
    ppermute x3, starting transfers between devices: 3.71 us -> 8.18 us  [give_back(): lax.ppermute(blocks, 'row', [(i, i ^ first_place(i, region)) for i in ran...]
    ppermute x3, waiting for transfers between devices: 1.05 us -> 3.4 us  [give_back(): lax.ppermute(blocks, 'row', [(i, i ^ first_place(i, region)) for i in ran...]
    pallas_call x2, Pallas kernels: 13 us -> 13.9 us  [partial_rows(): pl.pallas_call(functools.partial(rows_kernel, jobs, len(coeffs)), in_spec...]
  transfers between devices with their start and end apart: 20 -> 20, of which waited for: 7 -> 7; matrix products, arithmetic and copies ran while one was open for 2% -> 2% of each run, Pallas kernels for 13% -> 15%
where the time goes in v5:
time: 61.8 us; the launch traced here: 61.2 us
  starting transfers between devices  25.1 us (41%)
  Pallas kernels  17.8 us (29%)
  waiting for transfers between devices  14.1 us (23%)
  local copies, waits for them, and re-layouts  2.13 us (3%)
  other arithmetic  1.18 us (2%)
  between operations  0.8 us (1%)
    ppermute x17, starting transfers between devices, send(): return lax.ppermute(x, 'row', [(i, i ^ flip) for i in range(ROWS)])  16.9 us
    pallas_call x2, Pallas kernels, partial_rows(): pl.pallas_call(functools.partial(rows_kernel, jobs, len(coeffs)), in_spec...  13.9 us
    ppermute x17, waiting for transfers between devices, send(): return lax.ppermute(x, 'row', [(i, i ^ flip) for i in range(ROWS)])  10.7 us
    ppermute x3, starting transfers between devices, give_back(): lax.ppermute(blocks, 'row', [(i, i ^ first_place(i, region)) for i in ran...  8.18 us
    ppermute x3, waiting for transfers between devices, give_back(): lax.ppermute(blocks, 'row', [(i, i ^ first_place(i, region)) for i in ran...  3.4 us
    unnamed x10, local copies, waits for them, and re-layouts  2.05 us
    pallas_call x1, Pallas kernels, assemble(): pl.pallas_call(assemble_kernel, in_specs=[pl.BlockSpec(memory_space=pltpu...  1.49 us
  transfers between devices with their start and end apart: 20, of which 7 were waited for; matrix products, arithmetic and copies ran while one was open for 2% of the time, Pallas kernels for 15%

profile of v5, /device:TPU:0, one launch (start us, length us, event | category | flops | bytes accessed | tf_op | source)
XLA Modules:
  0.0 61.2 jit_solution(6425835559776576085)
XLA Ops:
  0.6 0.5 collective-permute-start.2
  1.1 0.9 %fusion.2 = (s32[6,16]{1,0:T(8,128)S(1)}, s32[16,16]{1,0:T(8,128)S(1)}, s32[16,16]{1,0:T(8,128)S(1)}) fusion(s32[16]{0:T(128)} %holders.1, s32[6,16]{1,0:T(8,128)} %bitcast.5), kind=kLoop, calls=%fused_computation.6 | loop fusion | flops 10144 | bytes 2880 | tf_op jit(solution)/shard_map/reduce_sum | solution.py:486
  2.1 0.1 collective-permute-start.1
  2.2 0.5 collective-permute-start.3
  3.1 1.4 %copy-done.1 = bf16[16,6,64,128]{3,2,1,0:T(8,128)(2,1)S(1)} copy-done((bf16[16,6,64,128]{3,2,1,0:T(8,128)(2,1)S(1)}, bf16[16,6,64,128]{3,2,1,0:T(8,128)(2,1)}, u32[]{:S(2)}) %copy-start.1) | copy-done | bytes 1572888
  4.7 0.6 %copy-done.2 = f32[16,6,128]{2,0,1:T(8,128)S(1)} copy-done((f32[16,6,128]{2,0,1:T(8,128)S(1)}, f32[16,6,128]{2,0,1:T(8,128)}, u32[]{:S(2)}) %copy-start.2) | copy-done | bytes 49176
  5.3 7.3 %shard_map.86 = (s16[520,384]{1,0:T(8,128)(2,1)S(1)}, s16[520,384]{1,0:T(8,128)(2,1)S(1)}, s16[520,384]{1,0:T(8,128)(2,1)S(1)}, f32[1,128]{1,0:T(1,128)S(1)}) custom-call(s32[16,6]{1,0:T(8,128)S(1)} %broadcast_add_fusion.listed, s32[6,16]{1,0:T(8,128)S(1)} %get-tuple-element.42.ranks, s32[16,6]{1,0:T(8,128)S(1)} %collective-permute-done.listed_other, ...), custom_call_target="tpu_custom_call" | custom-call | flops 1024 | bytes 1024 | tf_op jit(solution)/shard_map/pallas_call | solution.py:285
  12.6 3.1 %collective-permute-start.4 = (s16[520,384]{1,0:T(8,128)(2,1)S(1)}, s16[520,384]{1,0:T(8,128)(2,1)S(1)}, u32[]{:S(2)}, u32[]{:S(2)}) collective-permute-start(s16[520,384]{1,0:T(8,128)(2,1)S(1)} %get-tuple-element.45), channel_id=1, source_target_pairs={{0,4},{1,5},{2,6},{3,7},{4,0},{5,1},{6,2},{7,3},{8,12},{9,13},{10,... | collective-permute-start | bytes 1198088 | tf_op jit(solution)/shard_map/ppermute | solution.py:92
  15.7 1.5 %collective-permute-start.7 = (s16[520,384]{1,0:T(8,128)(2,1)S(1)}, s16[520,384]{1,0:T(8,128)(2,1)S(1)}, u32[]{:S(2)}, u32[]{:S(2)}) collective-permute-start(s16[520,384]{1,0:T(8,128)(2,1)S(1)} %get-tuple-element.44), channel_id=1, source_target_pairs={{0,2},{1,3},{2,0},{3,1},{4,6},{5,7},{6,4},{7,5},{8,10},{9,11},{10,... | collective-permute-start | bytes 1198088 | tf_op jit(solution)/shard_map/ppermute | solution.py:92
  17.3 0.5 collective-permute-start.10
  17.7 6.6 %shard_map.87 = (f32[4,128,384]{2,1,0:T(8,128)S(1)}, f32[4,128,384]{2,1,0:T(8,128)S(1)}, f32[4,128,384]{2,1,0:T(8,128)S(1)}) custom-call(s32[16,6]{1,0:T(8,128)S(1)} %broadcast_add_fusion.listed, s32[6,16]{1,0:T(8,128)S(1)} %get-tuple-element.42.ranks, s32[16,6]{1,0:T(8,128)S(1)} %collective-permute-done.listed_other, ...), custom_call_target="tpu_custom_call" | custom-call | flops 1024 | bytes 1024 | tf_op jit(solution)/shard_map/pallas_call | solution.py:285
  24.3 0.9 %collective-permute-done.4.code = s16[520,384]{1,0:T(8,128)(2,1)S(1)} collective-permute-done((s16[520,384]{1,0:T(8,128)(2,1)S(1)}, s16[520,384]{1,0:T(8,128)(2,1)S(1)}, u32[]{:S(2)}, u32[]{:S(2)}) %collective-permute-start.4) | collective-permute-done | bytes 399392 | tf_op jit(solution)/shard_map/ppermute | solution.py:92
  25.3 0.2 shard_map.88
  25.5 3.8 %collective-permute-start.5 = (s16[264,384]{1,0:T(8,128)(2,1)S(1)}, s16[264,384]{1,0:T(8,128)(2,1)S(1)}, u32[]{:S(2)}, u32[]{:S(2)}) collective-permute-start(s16[264,384]{1,0:T(8,128)(2,1)S(1)} %get-tuple-element.52), channel_id=1, source_target_pairs={{0,12},{1,13},{2,14},{3,15},{4,8},{5,9},{6,10},{7,11},{8,4},{9,5},... | collective-permute-start | bytes 608264 | tf_op jit(solution)/shard_map/ppermute | solution.py:92
  29.2 0.2 shard_map.91
  29.5 5.8 %collective-permute-done.10.code = s16[520,384]{1,0:T(8,128)(2,1)S(1)} collective-permute-done((s16[520,384]{1,0:T(8,128)(2,1)S(1)}, s16[520,384]{1,0:T(8,128)(2,1)S(1)}, u32[]{:S(2)}, u32[]{:S(2)}) %collective-permute-start.10) | collective-permute-done | bytes 399392 | tf_op jit(solution)/shard_map/ppermute | solution.py:92
  35.3 0.2 shard_map.95
  35.5 0.4 collective-permute-start.11
  36.0 1.6 %collective-permute-start.6 = (s16[136,512]{1,0:T(8,128)(2,1)S(1)}, s16[136,512]{1,0:T(8,128)(2,1)S(1)}, u32[]{:S(2)}, u32[]{:S(2)}) collective-permute-start(s16[136,512]{1,0:T(8,128)(2,1)S(1)} %get-tuple-element.56), channel_id=1, source_target_pairs={{0,2},{1,3},{2,0},{3,1},{4,6},{5,7},{6,4},{7,5},{8,10},{9,11},{10,... | collective-permute-start | bytes 417800 | tf_op jit(solution)/shard_map/ppermute | solution.py:92
  37.7 1.5 %collective-permute-done.8.code = s16[272,384]{1,0:T(8,128)(2,1)S(1)} collective-permute-done((s16[272,384]{1,0:T(8,128)(2,1)S(1)}, s16[272,384]{1,0:T(8,128)(2,1)S(1)}, u32[]{:S(2)}, u32[]{:S(2)}) %collective-permute-start.8) | collective-permute-done | bytes 208928 | tf_op jit(solution)/shard_map/ppermute | solution.py:92
  39.3 2.1 %collective-permute-start.9 = (s16[144,384]{1,0:T(8,128)(2,1)S(1)}, s16[144,384]{1,0:T(8,128)(2,1)S(1)}, u32[]{:S(2)}, u32[]{:S(2)}) collective-permute-start(s16[144,384]{1,0:T(8,128)(2,1)S(1)} %get-tuple-element.65), channel_id=1, source_target_pairs={{0,12},{1,13},{2,14},{3,15},{4,8},{5,9},{6,10},{7,11},{8,4},{9,5},... | collective-permute-start | bytes 331784 | tf_op jit(solution)/shard_map/ppermute | solution.py:92
  41.4 1.6 %collective-permute-done.11.code = s16[264,384]{1,0:T(8,128)(2,1)S(1)} collective-permute-done((s16[264,384]{1,0:T(8,128)(2,1)S(1)}, s16[264,384]{1,0:T(8,128)(2,1)S(1)}, u32[]{:S(2)}, u32[]{:S(2)}) %collective-permute-start.11) | collective-permute-done | bytes 202784 | tf_op jit(solution)/shard_map/ppermute | solution.py:92
  43.1 2.1 %collective-permute-start.12 = (s16[136,384]{1,0:T(8,128)(2,1)S(1)}, s16[136,384]{1,0:T(8,128)(2,1)S(1)}, u32[]{:S(2)}, u32[]{:S(2)}) collective-permute-start(s16[136,384]{1,0:T(8,128)(2,1)S(1)} %get-tuple-element.71), channel_id=1, source_target_pairs={{0,12},{1,13},{2,14},{3,15},{4,8},{5,9},{6,10},{7,11},{8,4},{9,5},... | collective-permute-start | bytes 313352 | tf_op jit(solution)/shard_map/ppermute | solution.py:92
  45.3 1.8 %collective-permute-start.14 = (bf16[288,128]{1,0:T(8,128)(2,1)S(1)}, bf16[288,128]{1,0:T(8,128)(2,1)S(1)}, u32[]{:S(2)}, u32[]{:S(2)}) collective-permute-start(bf16[288,128]{1,0:T(8,128)(2,1)S(1)} %get-tuple-element.74), channel_id=1, source_target_pairs={{0,12},{1,13},{2,14},{3,15},{4,10},{5,11},{6,8},{7,9},{8,4},{9,5},... | collective-permute-start | bytes 221192 | tf_op jit(solution)/shard_map/ppermute | solution.py:437
  47.2 1.1 %shard_map.93 = (f32[1,64]{1,0:T(1,128)}, bf16[1,128,128]{2,1,0:T(8,128)(2,1)}) custom-call(f32[1,128]{1,0:T(1,128)S(1)} %get-tuple-element.62.vector, f32[64,64]{1,0:T(8,128)S(1)} %copy-done.3, bf16[1,64,128,128]{3,2,1,0:T(8,128)(2,1)S(1)} %copy-done), custom_call_target="tpu_custom_call" | custom-call | flops 1024 | bytes 1024 | tf_op jit(solution)/shard_map/pallas_call | solution.py:382
  48.4 3.6 %collective-permute-start.16 = (bf16[272,128]{1,0:T(8,128)(2,1)S(1)}, bf16[272,128]{1,0:T(8,128)(2,1)S(1)}, u32[]{:S(2)}, u32[]{:S(2)}) collective-permute-start(bf16[272,128]{1,0:T(8,128)(2,1)S(1)} %get-tuple-element.75), channel_id=1, source_target_pairs={{0,4},{1,5},{2,6},{3,7},{4,2},{5,3},{6,0},{7,1},{8,12},{9,13},{10,... | collective-permute-start | bytes 208904 | tf_op jit(solution)/shard_map/ppermute | solution.py:437
  52.2 2.7 %collective-permute-start.18 = (bf16[256,128]{1,0:T(8,128)(2,1)S(1)}, bf16[256,128]{1,0:T(8,128)(2,1)S(1)}, u32[]{:S(2)}, u32[]{:S(2)}) collective-permute-start(bf16[256,128]{1,0:T(8,128)(2,1)S(1)} %get-tuple-element.76), channel_id=1, source_target_pairs={{0,8},{1,9},{2,10},{3,11},{4,12},{5,13},{6,14},{7,15},{8,2},{9,3},... | collective-permute-start | bytes 196616 | tf_op jit(solution)/shard_map/ppermute | solution.py:437
  54.9 1.5 %collective-permute-done.16.refs_2_ = bf16[272,128]{1,0:T(8,128)(2,1)S(1)} collective-permute-done((bf16[272,128]{1,0:T(8,128)(2,1)S(1)}, bf16[272,128]{1,0:T(8,128)(2,1)S(1)}, u32[]{:S(2)}, u32[]{:S(2)}) %collective-permute-start.16) | collective-permute-done | bytes 69664 | tf_op jit(solution)/shard_map/ppermute | solution.py:437
  56.4 1.9 %collective-permute-done.18.refs_4_ = bf16[256,128]{1,0:T(8,128)(2,1)S(1)} collective-permute-done((bf16[256,128]{1,0:T(8,128)(2,1)S(1)}, bf16[256,128]{1,0:T(8,128)(2,1)S(1)}, u32[]{:S(2)}, u32[]{:S(2)}) %collective-permute-start.18) | collective-permute-done | bytes 65568 | tf_op jit(solution)/shard_map/ppermute | solution.py:437
  58.3 0.5 collective-permute-start.13
  58.8 0.9 %collective-permute-done.13.extra_core = bf16[128,128]{1,0:T(8,128)(2,1)S(1)} collective-permute-done((bf16[128,128]{1,0:T(8,128)(2,1)S(1)}, bf16[128,128]{1,0:T(8,128)(2,1)S(1)}, u32[]{:S(2)}, u32[]{:S(2)}) %collective-permute-start.13) | collective-permute-done | bytes 32800 | tf_op jit(solution)/shard_map/ppermute | solution.py:92
  59.7 1.5 %shard_map.98 = bf16[1,128,2048]{2,1,0:T(8,128)(2,1)} custom-call(s32[16]{0:T(128)S(1)} %copy-done.4, bf16[128,384]{1,0:T(8,128)(2,1)S(1)} %get-tuple-element.57.early, bf16[128,384]{1,0:T(8,128)(2,1)S(1)} %get-tuple-element.66.late, bf16[128,384]{1,0:T(8,128)(2,1)S(1)} %get-tuple-element.72.later, bf16[128,128]{1,0:T(8,128)(2,1)S(1)} %get-tuple-element.73.extra, ...), custom_call_target="tpu_custom_call" | custom-call | flops 1024 | bytes 1024 | tf_op jit(solution)/shard_map/pallas_call | solution.py:473
  (41 shorter events, 1.3 us)
Async XLA Ops:
  0.6 4.0 %collective-permute-start.2 = (bf16[16,6,64,128]{3,2,1,0:T(8,128)(2,1)}, bf16[16,6,64,128]{3,2,1,0:T(8,128)(2,1)S(1)}, u32[]{:S(2)}, u32[]{:S(2)}) collective-permute-start(bf16[16,6,64,128]{3,2,1,0:T(8,128)(2,1)} %far), channel_id=1, source_target_pairs={{0,1},{1,0},{2,3},{3,2},{4,5},{5,4},{6,7},{7,6},{8,9},{9,8},{10,11... | collective-permute-start | bytes 4718600 | tf_op jit(solution)/shard_map/ppermute | solution.py:92
  2.1 2.5 %collective-permute-start.1 = (s32[6,16]{1,0:T(8,128)S(1)}, s32[6,16]{1,0:T(8,128)S(1)}, u32[]{:S(2)}, u32[]{:S(2)}) collective-permute-start(s32[6,16]{1,0:T(8,128)S(1)} %get-tuple-element.42.ranks), channel_id=1, source_target_pairs={{0,1},{1,0},{2,3},{3,2},{4,5},{5,4},{6,7},{7,6},{8,9},{9,8},{10,11... | collective-permute-start | bytes 1160 | tf_op jit(solution)/shard_map/ppermute | solution.py:92
  2.2 2.4 %collective-permute-start.3 = (f32[6,16,128]{2,1,0:T(8,128)}, f32[6,16,128]{2,1,0:T(8,128)S(1)}, u32[]{:S(2)}, u32[]{:S(2)}) collective-permute-start(f32[6,16,128]{2,1,0:T(8,128)} %bitcast.3), channel_id=1, source_target_pairs={{0,1},{1,0},{2,3},{3,2},{4,5},{5,4},{6,7},{7,6},{8,9},{9,8},{10,11... | collective-permute-start | bytes 147464 | tf_op jit(solution)/shard_map/ppermute | solution.py:92
  3.0 1.6 %collective-permute-start = (s32[16,6]{1,0:T(8,128)S(1)}, s32[16,6]{1,0:T(8,128)S(1)}, u32[]{:S(2)}, u32[]{:S(2)}) collective-permute-start(s32[16,6]{1,0:T(8,128)S(1)} %broadcast_add_fusion.listed), channel_id=1, source_target_pairs={{0,1},{1,0},{2,3},{3,2},{4,5},{5,4},{6,7},{7,6},{8,9},{9,8},{10,11... | collective-permute-start | bytes 1160 | tf_op jit(solution)/shard_map/ppermute | solution.py:92
  3.1 1.4 %copy-start.1 = (bf16[16,6,64,128]{3,2,1,0:T(8,128)(2,1)S(1)}, bf16[16,6,64,128]{3,2,1,0:T(8,128)(2,1)}, u32[]{:S(2)}) copy-start(bf16[16,6,64,128]{3,2,1,0:T(8,128)(2,1)} %far) | copy-start | bytes 4718596
  4.5 0.8 %copy-start.2 = (f32[16,6,128]{2,0,1:T(8,128)S(1)}, f32[16,6,128]{2,0,1:T(8,128)}, u32[]{:S(2)}) copy-start(f32[16,6,128]{2,0,1:T(8,128)} %param.9) | copy-start | bytes 147460
  12.6 12.6 %collective-permute-start.4 = (s16[520,384]{1,0:T(8,128)(2,1)S(1)}, s16[520,384]{1,0:T(8,128)(2,1)S(1)}, u32[]{:S(2)}, u32[]{:S(2)}) collective-permute-start(s16[520,384]{1,0:T(8,128)(2,1)S(1)} %get-tuple-element.45), channel_id=1, source_target_pairs={{0,4},{1,5},{2,6},{3,7},{4,0},{5,1},{6,2},{7,3},{8,12},{9,13},{10,... | collective-permute-start | bytes 1198088 | tf_op jit(solution)/shard_map/ppermute | solution.py:92
  15.7 13.5 %collective-permute-start.7 = (s16[520,384]{1,0:T(8,128)(2,1)S(1)}, s16[520,384]{1,0:T(8,128)(2,1)S(1)}, u32[]{:S(2)}, u32[]{:S(2)}) collective-permute-start(s16[520,384]{1,0:T(8,128)(2,1)S(1)} %get-tuple-element.44), channel_id=1, source_target_pairs={{0,2},{1,3},{2,0},{3,1},{4,6},{5,7},{6,4},{7,5},{8,10},{9,11},{10,... | collective-permute-start | bytes 1198088 | tf_op jit(solution)/shard_map/ppermute | solution.py:92
  17.3 18.0 %collective-permute-start.10 = (s16[520,384]{1,0:T(8,128)(2,1)S(1)}, s16[520,384]{1,0:T(8,128)(2,1)S(1)}, u32[]{:S(2)}, u32[]{:S(2)}) collective-permute-start(s16[520,384]{1,0:T(8,128)(2,1)S(1)} %get-tuple-element.46), channel_id=1, source_target_pairs={{0,2},{1,3},{2,0},{3,1},{4,6},{5,7},{6,4},{7,5},{8,10},{9,11},{10,... | collective-permute-start | bytes 1198088 | tf_op jit(solution)/shard_map/ppermute | solution.py:92
  25.5 10.4 %collective-permute-start.5 = (s16[264,384]{1,0:T(8,128)(2,1)S(1)}, s16[264,384]{1,0:T(8,128)(2,1)S(1)}, u32[]{:S(2)}, u32[]{:S(2)}) collective-permute-start(s16[264,384]{1,0:T(8,128)(2,1)S(1)} %get-tuple-element.52), channel_id=1, source_target_pairs={{0,12},{1,13},{2,14},{3,15},{4,8},{5,9},{6,10},{7,11},{8,4},{9,5},... | collective-permute-start | bytes 608264 | tf_op jit(solution)/shard_map/ppermute | solution.py:92
  29.4 9.8 %collective-permute-start.8 = (s16[272,384]{1,0:T(8,128)(2,1)S(1)}, s16[272,384]{1,0:T(8,128)(2,1)S(1)}, u32[]{:S(2)}, u32[]{:S(2)}) collective-permute-start(s16[272,384]{1,0:T(8,128)(2,1)S(1)} %get-tuple-element.60), channel_id=1, source_target_pairs={{0,4},{1,5},{2,6},{3,7},{4,0},{5,1},{6,2},{7,3},{8,12},{9,13},{10,... | collective-permute-start | bytes 626696 | tf_op jit(solution)/shard_map/ppermute | solution.py:92
  35.3 11.9 %copy-start = (bf16[1,64,128,128]{3,2,1,0:T(8,128)(2,1)S(1)}, bf16[1,64,128,128]{3,2,1,0:T(8,128)(2,1)}, u32[]{:S(2)}) copy-start(bf16[1,64,128,128]{3,2,1,0:T(8,128)(2,1)} %tiles.1) | copy-start | bytes 6291460
  35.3 11.9 %copy-start.3 = (f32[64,64]{1,0:T(8,128)S(1)}, f32[64,64]{1,0:T(8,128)}, u32[]{:S(2)}) copy-start(f32[64,64]{1,0:T(8,128)} %metric.1) | copy-start | bytes 49156
  35.5 7.5 %collective-permute-start.11 = (s16[264,384]{1,0:T(8,128)(2,1)S(1)}, s16[264,384]{1,0:T(8,128)(2,1)S(1)}, u32[]{:S(2)}, u32[]{:S(2)}) collective-permute-start(s16[264,384]{1,0:T(8,128)(2,1)S(1)} %get-tuple-element.69), channel_id=1, source_target_pairs={{0,4},{1,5},{2,6},{3,7},{4,0},{5,1},{6,2},{7,3},{8,12},{9,13},{10,... | collective-permute-start | bytes 608264 | tf_op jit(solution)/shard_map/ppermute | solution.py:92
  36.0 9.2 %collective-permute-start.6 = (s16[136,512]{1,0:T(8,128)(2,1)S(1)}, s16[136,512]{1,0:T(8,128)(2,1)S(1)}, u32[]{:S(2)}, u32[]{:S(2)}) collective-permute-start(s16[136,512]{1,0:T(8,128)(2,1)S(1)} %get-tuple-element.56), channel_id=1, source_target_pairs={{0,2},{1,3},{2,0},{3,1},{4,6},{5,7},{6,4},{7,5},{8,10},{9,11},{10,... | collective-permute-start | bytes 417800 | tf_op jit(solution)/shard_map/ppermute | solution.py:92
  39.3 9.0 %collective-permute-start.9 = (s16[144,384]{1,0:T(8,128)(2,1)S(1)}, s16[144,384]{1,0:T(8,128)(2,1)S(1)}, u32[]{:S(2)}, u32[]{:S(2)}) collective-permute-start(s16[144,384]{1,0:T(8,128)(2,1)S(1)} %get-tuple-element.65), channel_id=1, source_target_pairs={{0,12},{1,13},{2,14},{3,15},{4,8},{5,9},{6,10},{7,11},{8,4},{9,5},... | collective-permute-start | bytes 331784 | tf_op jit(solution)/shard_map/ppermute | solution.py:92
  43.1 8.9 %collective-permute-start.12 = (s16[136,384]{1,0:T(8,128)(2,1)S(1)}, s16[136,384]{1,0:T(8,128)(2,1)S(1)}, u32[]{:S(2)}, u32[]{:S(2)}) collective-permute-start(s16[136,384]{1,0:T(8,128)(2,1)S(1)} %get-tuple-element.71), channel_id=1, source_target_pairs={{0,12},{1,13},{2,14},{3,15},{4,8},{5,9},{6,10},{7,11},{8,4},{9,5},... | collective-permute-start | bytes 313352 | tf_op jit(solution)/shard_map/ppermute | solution.py:92
  45.2 14.5 %copy-start.4 = (s32[16]{0:T(128)S(1)}, s32[16]{0:T(128)}, u32[]{:S(2)}) copy-start(s32[16]{0:T(128)} %holders.1) | copy-start | bytes 196
  45.3 9.5 %collective-permute-start.14 = (bf16[288,128]{1,0:T(8,128)(2,1)S(1)}, bf16[288,128]{1,0:T(8,128)(2,1)S(1)}, u32[]{:S(2)}, u32[]{:S(2)}) collective-permute-start(bf16[288,128]{1,0:T(8,128)(2,1)S(1)} %get-tuple-element.74), channel_id=1, source_target_pairs={{0,12},{1,13},{2,14},{3,15},{4,10},{5,11},{6,8},{7,9},{8,4},{9,5},... | collective-permute-start | bytes 221192 | tf_op jit(solution)/shard_map/ppermute | solution.py:437
  48.4 8.0 %collective-permute-start.16 = (bf16[272,128]{1,0:T(8,128)(2,1)S(1)}, bf16[272,128]{1,0:T(8,128)(2,1)S(1)}, u32[]{:S(2)}, u32[]{:S(2)}) collective-permute-start(bf16[272,128]{1,0:T(8,128)(2,1)S(1)} %get-tuple-element.75), channel_id=1, source_target_pairs={{0,4},{1,5},{2,6},{3,7},{4,2},{5,3},{6,0},{7,1},{8,12},{9,13},{10,... | collective-permute-start | bytes 208904 | tf_op jit(solution)/shard_map/ppermute | solution.py:437
  52.2 6.1 %collective-permute-start.18 = (bf16[256,128]{1,0:T(8,128)(2,1)S(1)}, bf16[256,128]{1,0:T(8,128)(2,1)S(1)}, u32[]{:S(2)}, u32[]{:S(2)}) collective-permute-start(bf16[256,128]{1,0:T(8,128)(2,1)S(1)} %get-tuple-element.76), channel_id=1, source_target_pairs={{0,8},{1,9},{2,10},{3,11},{4,12},{5,13},{6,14},{7,15},{8,2},{9,3},... | collective-permute-start | bytes 196616 | tf_op jit(solution)/shard_map/ppermute | solution.py:437
  54.9 4.8 %collective-permute-start.15 = (bf16[288,128]{1,0:T(8,128)(2,1)S(1)}, bf16[288,128]{1,0:T(8,128)(2,1)S(1)}, u32[]{:S(2)}, u32[]{:S(2)}) collective-permute-start(bf16[288,128]{1,0:T(8,128)(2,1)S(1)} %collective-permute-done.14.refs_0_), channel_id=1, source_target_pairs={{0,1},{1,0},{2,3},{3,2},{4,5},{5,4},{6,7},{7,6},{8,9},{9,8},{10,11... | collective-permute-start | bytes 221192 | tf_op jit(solution)/shard_map/ppermute | solution.py:92
  56.4 3.3 %collective-permute-start.17 = (bf16[272,128]{1,0:T(8,128)(2,1)S(1)}, bf16[272,128]{1,0:T(8,128)(2,1)S(1)}, u32[]{:S(2)}, u32[]{:S(2)}) collective-permute-start(bf16[272,128]{1,0:T(8,128)(2,1)S(1)} %collective-permute-done.16.refs_2_), channel_id=1, source_target_pairs={{0,1},{1,0},{2,3},{3,2},{4,5},{5,4},{6,7},{7,6},{8,9},{9,8},{10,11... | collective-permute-start | bytes 208904 | tf_op jit(solution)/shard_map/ppermute | solution.py:92
  58.3 1.4 %collective-permute-start.19 = (bf16[256,128]{1,0:T(8,128)(2,1)S(1)}, bf16[256,128]{1,0:T(8,128)(2,1)S(1)}, u32[]{:S(2)}, u32[]{:S(2)}) collective-permute-start(bf16[256,128]{1,0:T(8,128)(2,1)S(1)} %collective-permute-done.18.refs_4_), channel_id=1, source_target_pairs={{0,1},{1,0},{2,3},{3,2},{4,5},{5,4},{6,7},{7,6},{8,9},{9,8},{10,11... | collective-permute-start | bytes 196616 | tf_op jit(solution)/shard_map/ppermute | solution.py:92
  58.3 1.4 %collective-permute-start.13 = (bf16[128,128]{1,0:T(8,128)(2,1)S(1)}, bf16[128,128]{1,0:T(8,128)(2,1)S(1)}, u32[]{:S(2)}, u32[]{:S(2)}) collective-permute-start(bf16[128,128]{1,0:T(8,128)(2,1)S(1)} %get-tuple-element.73.extra), channel_id=1, source_target_pairs={{0,1},{1,0},{2,3},{3,2},{4,5},{5,4},{6,7},{7,6},{8,9},{9,8},{10,11... | collective-permute-start | bytes 98312 | tf_op jit(solution)/shard_map/ppermute | solution.py:92

commit v6 on v5

--- a/solution.py
+++ b/solution.py
@@ -76,10 +76,11 @@
 
 ROWS = 16
 CORE, Y, Z = 1, 2, (4, 8, 12)
-NEAR, FAR = 4, 12
+NEAR = 4
+EARLY_FAR, LATE_FAR, LATER_FAR = 8, 12, 12
 PLACES = 16
 Z_FIRST, SOONER, LATER = (3, "extra"), (1, "diagonal"), (2, "mate")
-TAIL = 8
+TAIL = 16
 TOP = 14.99
 SPARE = 0
 VECTOR = 4
@@ -106,6 +107,9 @@
 
 def returned(group):
     return [region for region in group if region in (1, 2, 3)]
+
+
+EXTRA_SPARE = 48
 
 
 def spare_of(region):
@@ -295,10 +299,10 @@
     )(lists[0], ranks[0], lists[1], ranks[1], *panels, *coeffs)
 
 
-def turn_y_kernel(stay, code, kept, message):
+def turn_y_kernel(last, stay, code, kept, message):
     height = stay.shape[1]
-    encode(message, [stay[j] + decode(code, j, height) for j in (1, 2)])
-    for k, j in enumerate((0, 3)):
+    encode(message, [stay[j] + decode(code, j, height) for j in (1, 1 ^ last // 4)])
+    for k, j in enumerate((0, last // 4)):
         kept[k] = stay[j] + decode(code, j, height)
 
 
@@ -342,10 +346,10 @@
     return jax.ShapeDtypeStruct(shape, jnp.float32)
 
 
-def turn_y(stay, code, spare):
+def turn_y(stay, code, spare, last):
     height, columns = stay.shape[1:]
     shapes = [sums_of(2, height, columns), message_of(2 * height, columns, spare)]
-    return small_call(turn_y_kernel, shapes, stay, code)
+    return small_call(functools.partial(turn_y_kernel, last), shapes, stay, code)
 
 
 def turn_z(kept, code, spare):
@@ -413,14 +417,15 @@
     *backs, other_extra, vector_out = refs
     came = decode(code, 0, height)
     finish_row(own[...] + came[:, :columns], done, *backs)
-    other_extra[...] = (extra[...] + came[:, columns:]).T.astype(jnp.bfloat16)
+    other_extra[:height, :] = (extra[...] + came[:, columns:]).T.astype(jnp.bfloat16)
+    other_extra[height:, :] = jnp.zeros((other_extra.shape[0] - height, height), jnp.bfloat16)
     vector_out[...] = vector[...] + decode_vector(code, vector.shape[1])
 
 
 def finish_early(own, vector, extra, code):
     height = own.shape[0]
     shapes = [jax.ShapeDtypeStruct(own.shape, jnp.bfloat16)] + backs_of(Z_FIRST, height)
-    shapes += [jax.ShapeDtypeStruct((height, height), jnp.bfloat16), sums_of(*vector.shape)]
+    shapes += [jax.ShapeDtypeStruct((2 * height + EXTRA_SPARE, height), jnp.bfloat16), sums_of(*vector.shape)]
     return small_call(finish_early_kernel, shapes, own, vector, extra, code)
 
 
@@ -464,7 +469,7 @@
                 put(start, came[k][:width, :])
                 put(start + 1, came[k + 1][width : 2 * width, :])
                 k += 2
-    put(5 - first_place(me, "extra"), jnp.where((me >> 1) & 1 == 0, extra_core[...], extra[...]))
+    put(5 - first_place(me, "extra"), jnp.where((me >> 1) & 1 == 0, extra_core[:width, :], extra[:width, :]))
 
 
 def assemble(row_block, early, *rest):
@@ -508,7 +513,7 @@
     mine = bring(panels)
     ranks, sides = (rank, rank_other), (mine, other)
 
-    jobs = ((SOONER, LATER), [Y] + [z | Y for z in Z], True), ((Z_FIRST,), [4 | Y, 4, 8 | Y, 8], True)
+    jobs = ((SOONER, LATER), [Y] + [z | Y for z in Z], True), ((Z_FIRST,), [4 | Y, 4, (4 ^ EARLY_FAR) | Y, 4 ^ EARLY_FAR], True)
     late_go, later_go, early_go, vector = partial_rows(
         jobs, (listed, listed_other), ranks, sides, coeffs, coeffs_other
     )
@@ -517,18 +522,18 @@
     later_code = send(later_go, Y)
 
     listed, *_ = lax.optimization_barrier((listed, late_go, early_go, later_go))
-    jobs = ((Z_FIRST,), [Y, 0, 12 | Y, 12], False), ((SOONER, LATER), [0, *Z], False)
+    jobs = ((Z_FIRST,), [Y, 0, EARLY_FAR | Y, EARLY_FAR], False), ((SOONER, LATER), [0, *Z], False)
     early_stay, late_stay, later_stay = partial_rows(jobs, (listed, listed_other), ranks, sides)
 
     early_stay, early_turn, vector = turn_near(early_stay, vector, early_code)
-    early_code = send(early_turn, FAR)
-    late, late_turn = turn_y(late_stay, late_code, 8)
+    early_code = send(early_turn, EARLY_FAR)
+    late, late_turn = turn_y(late_stay, late_code, 16, LATE_FAR)
     near_code = send(late_turn, NEAR)
-    later, later_turn = turn_y(later_stay, later_code, 0)
-    late, late_turn = turn_z(late, near_code, 8)
-    late_code = send(late_turn, FAR)
+    later, later_turn = turn_y(later_stay, later_code, 0, LATER_FAR)
+    late, late_turn = turn_z(late, near_code, 0)
+    late_code = send(late_turn, LATE_FAR)
     later, later_turn = turn_z(later, send(later_turn, NEAR), 0)
-    later_code = send(later_turn, FAR)
+    later_code = send(later_turn, LATER_FAR)
 
     early_own, early_turn, vector, extra = turn_far(early_stay, vector, early_code)
     early, *early_back, extra, vector = finish_early(early_own, vector, extra, send(early_turn, Y))

time: 61.8 us -> 61.5 us (level)
  starting transfers between devices: 25.1 us -> 27.4 us
  waiting for transfers between devices: 14.1 us -> 11.9 us
    ppermute x17, starting transfers between devices: 16.9 us -> 19.4 us  [send(): return lax.ppermute(x, 'row', [(i, i ^ flip) for i in range(ROWS)])]
    ppermute x17, waiting for transfers between devices: 10.7 us -> 9.2 us  [send(): return lax.ppermute(x, 'row', [(i, i ^ flip) for i in range(ROWS)])]
    ppermute x3, waiting for transfers between devices: 3.4 us -> 2.75 us  [give_back(): lax.ppermute(blocks, 'row', [(i, i ^ first_place(i, region)) for i in ran...]
  transfers between devices with their start and end apart: 20 -> 20, of which waited for: 7 -> 5; matrix products, arithmetic and copies ran while one was open for 2% -> 2% of each run, Pallas kernels for 15% -> 15%
where the time goes in v6:
time: 61.5 us; the launch traced here: 61.3 us
  starting transfers between devices  27.4 us (45%)
  Pallas kernels  17.8 us (29%)
  waiting for transfers between devices  11.9 us (19%)
  local copies, waits for them, and re-layouts  2.13 us (3%)
  other arithmetic  1.18 us (2%)
  between operations  0.78 us (1%)
    ppermute x17, starting transfers between devices, send(): return lax.ppermute(x, 'row', [(i, i ^ flip) for i in range(ROWS)])  19.4 us
    pallas_call x2, Pallas kernels, partial_rows(): pl.pallas_call(functools.partial(rows_kernel, jobs, len(coeffs)), in_spec...  13.9 us
    ppermute x17, waiting for transfers between devices, send(): return lax.ppermute(x, 'row', [(i, i ^ flip) for i in range(ROWS)])  9.2 us
    ppermute x3, starting transfers between devices, give_back(): lax.ppermute(blocks, 'row', [(i, i ^ first_place(i, region)) for i in ran...  8.06 us
    ppermute x3, waiting for transfers between devices, give_back(): lax.ppermute(blocks, 'row', [(i, i ^ first_place(i, region)) for i in ran...  2.75 us
    unnamed x10, local copies, waits for them, and re-layouts  2.05 us
    pallas_call x1, Pallas kernels, assemble(): pl.pallas_call(assemble_kernel, in_specs=[pl.BlockSpec(memory_space=pltpu...  1.49 us
    pallas_call x9, Pallas kernels, small_call(): pl.pallas_call(kernel, out_shape=shapes, compiler_params=pltpu.CompilerPa...  1.24 us
  transfers between devices with their start and end apart: 20, of which 5 were waited for; matrix products, arithmetic and copies ran while one was open for 2% of the time, Pallas kernels for 15%

profile of v6, /device:TPU:0, one launch (start us, length us, event | category | flops | bytes accessed | tf_op | source)
XLA Modules:
  0.0 61.3 jit_solution(3754641995655738252)
XLA Ops:
  0.6 0.5 collective-permute-start.2
  1.1 0.9 %fusion.2 = (s32[6,16]{1,0:T(8,128)S(1)}, s32[16,16]{1,0:T(8,128)S(1)}, s32[16,16]{1,0:T(8,128)S(1)}) fusion(s32[16]{0:T(128)} %holders.1, s32[6,16]{1,0:T(8,128)} %bitcast.5), kind=kLoop, calls=%fused_computation.6 | loop fusion | flops 10144 | bytes 2880 | tf_op jit(solution)/shard_map/reduce_sum | solution.py:491
  2.1 0.1 collective-permute-start.1
  2.2 0.5 collective-permute-start.3
  3.1 1.4 %copy-done.1 = bf16[16,6,64,128]{3,2,1,0:T(8,128)(2,1)S(1)} copy-done((bf16[16,6,64,128]{3,2,1,0:T(8,128)(2,1)S(1)}, bf16[16,6,64,128]{3,2,1,0:T(8,128)(2,1)}, u32[]{:S(2)}) %copy-start.1) | copy-done | bytes 1572888
  4.7 0.6 %copy-done.2 = f32[16,6,128]{2,0,1:T(8,128)S(1)} copy-done((f32[16,6,128]{2,0,1:T(8,128)S(1)}, f32[16,6,128]{2,0,1:T(8,128)}, u32[]{:S(2)}) %copy-start.2) | copy-done | bytes 49176
  5.3 7.3 %shard_map.86 = (s16[528,384]{1,0:T(8,128)(2,1)S(1)}, s16[528,384]{1,0:T(8,128)(2,1)S(1)}, s16[528,384]{1,0:T(8,128)(2,1)S(1)}, f32[1,128]{1,0:T(1,128)S(1)}) custom-call(s32[16,6]{1,0:T(8,128)S(1)} %broadcast_add_fusion.listed, s32[6,16]{1,0:T(8,128)S(1)} %get-tuple-element.42.ranks, s32[16,6]{1,0:T(8,128)S(1)} %collective-permute-done.listed_other, ...), custom_call_target="tpu_custom_call" | custom-call | flops 1024 | bytes 1024 | tf_op jit(solution)/shard_map/pallas_call | solution.py:289
  12.6 3.1 %collective-permute-start.4 = (s16[528,384]{1,0:T(8,128)(2,1)S(1)}, s16[528,384]{1,0:T(8,128)(2,1)S(1)}, u32[]{:S(2)}, u32[]{:S(2)}) collective-permute-start(s16[528,384]{1,0:T(8,128)(2,1)S(1)} %get-tuple-element.45), channel_id=1, source_target_pairs={{0,4},{1,5},{2,6},{3,7},{4,0},{5,1},{6,2},{7,3},{8,12},{9,13},{10,... | collective-permute-start | bytes 1216520 | tf_op jit(solution)/shard_map/ppermute | solution.py:93
  15.7 1.5 %collective-permute-start.7 = (s16[528,384]{1,0:T(8,128)(2,1)S(1)}, s16[528,384]{1,0:T(8,128)(2,1)S(1)}, u32[]{:S(2)}, u32[]{:S(2)}) collective-permute-start(s16[528,384]{1,0:T(8,128)(2,1)S(1)} %get-tuple-element.44), channel_id=1, source_target_pairs={{0,2},{1,3},{2,0},{3,1},{4,6},{5,7},{6,4},{7,5},{8,10},{9,11},{10,... | collective-permute-start | bytes 1216520 | tf_op jit(solution)/shard_map/ppermute | solution.py:93
  17.2 0.5 collective-permute-start.10
  17.7 6.6 %shard_map.87 = (f32[4,128,384]{2,1,0:T(8,128)S(1)}, f32[4,128,384]{2,1,0:T(8,128)S(1)}, f32[4,128,384]{2,1,0:T(8,128)S(1)}) custom-call(s32[16,6]{1,0:T(8,128)S(1)} %broadcast_add_fusion.listed, s32[6,16]{1,0:T(8,128)S(1)} %get-tuple-element.42.ranks, s32[16,6]{1,0:T(8,128)S(1)} %collective-permute-done.listed_other, ...), custom_call_target="tpu_custom_call" | custom-call | flops 1024 | bytes 1024 | tf_op jit(solution)/shard_map/pallas_call | solution.py:289
  24.3 1.0 %collective-permute-done.4.code = s16[528,384]{1,0:T(8,128)(2,1)S(1)} collective-permute-done((s16[528,384]{1,0:T(8,128)(2,1)S(1)}, s16[528,384]{1,0:T(8,128)(2,1)S(1)}, u32[]{:S(2)}, u32[]{:S(2)}) %collective-permute-start.4) | collective-permute-done | bytes 405536 | tf_op jit(solution)/shard_map/ppermute | solution.py:93
  25.3 0.2 shard_map.88
  25.5 2.8 %collective-permute-start.5 = (s16[272,384]{1,0:T(8,128)(2,1)S(1)}, s16[272,384]{1,0:T(8,128)(2,1)S(1)}, u32[]{:S(2)}, u32[]{:S(2)}) collective-permute-start(s16[272,384]{1,0:T(8,128)(2,1)S(1)} %get-tuple-element.52), channel_id=1, source_target_pairs={{0,8},{1,9},{2,10},{3,11},{4,12},{5,13},{6,14},{7,15},{8,0},{9,1},... | collective-permute-start | bytes 626696 | tf_op jit(solution)/shard_map/ppermute | solution.py:93
  28.3 0.2 shard_map.91
  28.5 1.6 %collective-permute-start.8 = (s16[288,384]{1,0:T(8,128)(2,1)S(1)}, s16[288,384]{1,0:T(8,128)(2,1)S(1)}, u32[]{:S(2)}, u32[]{:S(2)}) collective-permute-start(s16[288,384]{1,0:T(8,128)(2,1)S(1)} %get-tuple-element.60), channel_id=1, source_target_pairs={{0,4},{1,5},{2,6},{3,7},{4,0},{5,1},{6,2},{7,3},{8,12},{9,13},{10,... | collective-permute-start | bytes 663560 | tf_op jit(solution)/shard_map/ppermute | solution.py:93
  30.1 5.3 %collective-permute-done.10.code = s16[528,384]{1,0:T(8,128)(2,1)S(1)} collective-permute-done((s16[528,384]{1,0:T(8,128)(2,1)S(1)}, s16[528,384]{1,0:T(8,128)(2,1)S(1)}, u32[]{:S(2)}, u32[]{:S(2)}) %collective-permute-start.10) | collective-permute-done | bytes 405536 | tf_op jit(solution)/shard_map/ppermute | solution.py:93
  35.5 0.2 shard_map.95
  35.6 0.4 collective-permute-start.11
  36.1 1.6 %collective-permute-done.5.code = s16[272,384]{1,0:T(8,128)(2,1)S(1)} collective-permute-done((s16[272,384]{1,0:T(8,128)(2,1)S(1)}, s16[272,384]{1,0:T(8,128)(2,1)S(1)}, u32[]{:S(2)}, u32[]{:S(2)}) %collective-permute-start.5) | collective-permute-done | bytes 208928 | tf_op jit(solution)/shard_map/ppermute | solution.py:93
  37.8 1.5 %collective-permute-start.6 = (s16[144,512]{1,0:T(8,128)(2,1)S(1)}, s16[144,512]{1,0:T(8,128)(2,1)S(1)}, u32[]{:S(2)}, u32[]{:S(2)}) collective-permute-start(s16[144,512]{1,0:T(8,128)(2,1)S(1)} %get-tuple-element.56), channel_id=1, source_target_pairs={{0,2},{1,3},{2,0},{3,1},{4,6},{5,7},{6,4},{7,5},{8,10},{9,11},{10,... | collective-permute-start | bytes 442376 | tf_op jit(solution)/shard_map/ppermute | solution.py:93
  39.4 3.6 %collective-permute-start.9 = (s16[144,384]{1,0:T(8,128)(2,1)S(1)}, s16[144,384]{1,0:T(8,128)(2,1)S(1)}, u32[]{:S(2)}, u32[]{:S(2)}) collective-permute-start(s16[144,384]{1,0:T(8,128)(2,1)S(1)} %get-tuple-element.65), channel_id=1, source_target_pairs={{0,12},{1,13},{2,14},{3,15},{4,8},{5,9},{6,10},{7,11},{8,4},{9,5},... | collective-permute-start | bytes 331784 | tf_op jit(solution)/shard_map/ppermute | solution.py:93
  43.0 2.6 %collective-permute-start.12 = (s16[144,384]{1,0:T(8,128)(2,1)S(1)}, s16[144,384]{1,0:T(8,128)(2,1)S(1)}, u32[]{:S(2)}, u32[]{:S(2)}) collective-permute-start(s16[144,384]{1,0:T(8,128)(2,1)S(1)} %get-tuple-element.71), channel_id=1, source_target_pairs={{0,12},{1,13},{2,14},{3,15},{4,8},{5,9},{6,10},{7,11},{8,4},{9,5},... | collective-permute-start | bytes 331784 | tf_op jit(solution)/shard_map/ppermute | solution.py:93
  45.6 0.1 shard_map.90
  45.8 1.4 %collective-permute-start.14 = (bf16[288,128]{1,0:T(8,128)(2,1)S(1)}, bf16[288,128]{1,0:T(8,128)(2,1)S(1)}, u32[]{:S(2)}, u32[]{:S(2)}) collective-permute-start(bf16[288,128]{1,0:T(8,128)(2,1)S(1)} %get-tuple-element.74), channel_id=1, source_target_pairs={{0,12},{1,13},{2,14},{3,15},{4,10},{5,11},{6,8},{7,9},{8,4},{9,5},... | collective-permute-start | bytes 221192 | tf_op jit(solution)/shard_map/ppermute | solution.py:442
  47.1 1.1 %shard_map.93 = (f32[1,64]{1,0:T(1,128)}, bf16[1,128,128]{2,1,0:T(8,128)(2,1)}) custom-call(f32[1,128]{1,0:T(1,128)S(1)} %get-tuple-element.62.vector, f32[64,64]{1,0:T(8,128)S(1)} %copy-done.3, bf16[1,64,128,128]{3,2,1,0:T(8,128)(2,1)S(1)} %copy-done), custom_call_target="tpu_custom_call" | custom-call | flops 1024 | bytes 1024 | tf_op jit(solution)/shard_map/pallas_call | solution.py:386
  48.4 3.9 %collective-permute-start.16 = (bf16[272,128]{1,0:T(8,128)(2,1)S(1)}, bf16[272,128]{1,0:T(8,128)(2,1)S(1)}, u32[]{:S(2)}, u32[]{:S(2)}) collective-permute-start(bf16[272,128]{1,0:T(8,128)(2,1)S(1)} %get-tuple-element.75), channel_id=1, source_target_pairs={{0,4},{1,5},{2,6},{3,7},{4,2},{5,3},{6,0},{7,1},{8,12},{9,13},{10,... | collective-permute-start | bytes 208904 | tf_op jit(solution)/shard_map/ppermute | solution.py:442
  52.4 2.8 %collective-permute-start.18 = (bf16[256,128]{1,0:T(8,128)(2,1)S(1)}, bf16[256,128]{1,0:T(8,128)(2,1)S(1)}, u32[]{:S(2)}, u32[]{:S(2)}) collective-permute-start(bf16[256,128]{1,0:T(8,128)(2,1)S(1)} %get-tuple-element.76), channel_id=1, source_target_pairs={{0,8},{1,9},{2,10},{3,11},{4,12},{5,13},{6,14},{7,15},{8,2},{9,3},... | collective-permute-start | bytes 196616 | tf_op jit(solution)/shard_map/ppermute | solution.py:442
  55.2 0.5 collective-permute-start.15
  55.8 2.7 %collective-permute-done.18.refs_4_ = bf16[256,128]{1,0:T(8,128)(2,1)S(1)} collective-permute-done((bf16[256,128]{1,0:T(8,128)(2,1)S(1)}, bf16[256,128]{1,0:T(8,128)(2,1)S(1)}, u32[]{:S(2)}, u32[]{:S(2)}) %collective-permute-start.18) | collective-permute-done | bytes 65568 | tf_op jit(solution)/shard_map/ppermute | solution.py:442
  58.5 1.2 %collective-permute-done.19.refs_5_ = bf16[256,128]{1,0:T(8,128)(2,1)S(1)} collective-permute-done((bf16[256,128]{1,0:T(8,128)(2,1)S(1)}, bf16[256,128]{1,0:T(8,128)(2,1)S(1)}, u32[]{:S(2)}, u32[]{:S(2)}) %collective-permute-start.19) | collective-permute-done | bytes 65568 | tf_op jit(solution)/shard_map/ppermute | solution.py:93
  59.8 1.5 %shard_map.98 = bf16[1,128,2048]{2,1,0:T(8,128)(2,1)} custom-call(s32[16]{0:T(128)S(1)} %copy-done.4, bf16[128,384]{1,0:T(8,128)(2,1)S(1)} %get-tuple-element.57.early, bf16[128,384]{1,0:T(8,128)(2,1)S(1)} %get-tuple-element.66.late, bf16[128,384]{1,0:T(8,128)(2,1)S(1)} %get-tuple-element.72.later, bf16[304,128]{1,0:T(8,128)(2,1)S(1)} %get-tuple-element.73.extra, ...), custom_call_target="tpu_custom_call" | custom-call | flops 1024 | bytes 1024 | tf_op jit(solution)/shard_map/pallas_call | solution.py:478
  (41 shorter events, 1.2 us)
Async XLA Ops:
  0.6 4.0 %collective-permute-start.2 = (bf16[16,6,64,128]{3,2,1,0:T(8,128)(2,1)}, bf16[16,6,64,128]{3,2,1,0:T(8,128)(2,1)S(1)}, u32[]{:S(2)}, u32[]{:S(2)}) collective-permute-start(bf16[16,6,64,128]{3,2,1,0:T(8,128)(2,1)} %far), channel_id=1, source_target_pairs={{0,1},{1,0},{2,3},{3,2},{4,5},{5,4},{6,7},{7,6},{8,9},{9,8},{10,11... | collective-permute-start | bytes 4718600 | tf_op jit(solution)/shard_map/ppermute | solution.py:93
  2.1 2.5 %collective-permute-start.1 = (s32[6,16]{1,0:T(8,128)S(1)}, s32[6,16]{1,0:T(8,128)S(1)}, u32[]{:S(2)}, u32[]{:S(2)}) collective-permute-start(s32[6,16]{1,0:T(8,128)S(1)} %get-tuple-element.42.ranks), channel_id=1, source_target_pairs={{0,1},{1,0},{2,3},{3,2},{4,5},{5,4},{6,7},{7,6},{8,9},{9,8},{10,11... | collective-permute-start | bytes 1160 | tf_op jit(solution)/shard_map/ppermute | solution.py:93
  2.2 2.4 %collective-permute-start.3 = (f32[6,16,128]{2,1,0:T(8,128)}, f32[6,16,128]{2,1,0:T(8,128)S(1)}, u32[]{:S(2)}, u32[]{:S(2)}) collective-permute-start(f32[6,16,128]{2,1,0:T(8,128)} %bitcast.3), channel_id=1, source_target_pairs={{0,1},{1,0},{2,3},{3,2},{4,5},{5,4},{6,7},{7,6},{8,9},{9,8},{10,11... | collective-permute-start | bytes 147464 | tf_op jit(solution)/shard_map/ppermute | solution.py:93
  3.0 1.6 %collective-permute-start = (s32[16,6]{1,0:T(8,128)S(1)}, s32[16,6]{1,0:T(8,128)S(1)}, u32[]{:S(2)}, u32[]{:S(2)}) collective-permute-start(s32[16,6]{1,0:T(8,128)S(1)} %broadcast_add_fusion.listed), channel_id=1, source_target_pairs={{0,1},{1,0},{2,3},{3,2},{4,5},{5,4},{6,7},{7,6},{8,9},{9,8},{10,11... | collective-permute-start | bytes 1160 | tf_op jit(solution)/shard_map/ppermute | solution.py:93
  3.1 1.4 %copy-start.1 = (bf16[16,6,64,128]{3,2,1,0:T(8,128)(2,1)S(1)}, bf16[16,6,64,128]{3,2,1,0:T(8,128)(2,1)}, u32[]{:S(2)}) copy-start(bf16[16,6,64,128]{3,2,1,0:T(8,128)(2,1)} %far) | copy-start | bytes 4718596
  4.5 0.8 %copy-start.2 = (f32[16,6,128]{2,0,1:T(8,128)S(1)}, f32[16,6,128]{2,0,1:T(8,128)}, u32[]{:S(2)}) copy-start(f32[16,6,128]{2,0,1:T(8,128)} %param.9) | copy-start | bytes 147460
  12.6 12.7 %collective-permute-start.4 = (s16[528,384]{1,0:T(8,128)(2,1)S(1)}, s16[528,384]{1,0:T(8,128)(2,1)S(1)}, u32[]{:S(2)}, u32[]{:S(2)}) collective-permute-start(s16[528,384]{1,0:T(8,128)(2,1)S(1)} %get-tuple-element.45), channel_id=1, source_target_pairs={{0,4},{1,5},{2,6},{3,7},{4,0},{5,1},{6,2},{7,3},{8,12},{9,13},{10,... | collective-permute-start | bytes 1216520 | tf_op jit(solution)/shard_map/ppermute | solution.py:93
  15.7 12.6 %collective-permute-start.7 = (s16[528,384]{1,0:T(8,128)(2,1)S(1)}, s16[528,384]{1,0:T(8,128)(2,1)S(1)}, u32[]{:S(2)}, u32[]{:S(2)}) collective-permute-start(s16[528,384]{1,0:T(8,128)(2,1)S(1)} %get-tuple-element.44), channel_id=1, source_target_pairs={{0,2},{1,3},{2,0},{3,1},{4,6},{5,7},{6,4},{7,5},{8,10},{9,11},{10,... | collective-permute-start | bytes 1216520 | tf_op jit(solution)/shard_map/ppermute | solution.py:93
  17.2 18.2 %collective-permute-start.10 = (s16[528,384]{1,0:T(8,128)(2,1)S(1)}, s16[528,384]{1,0:T(8,128)(2,1)S(1)}, u32[]{:S(2)}, u32[]{:S(2)}) collective-permute-start(s16[528,384]{1,0:T(8,128)(2,1)S(1)} %get-tuple-element.46), channel_id=1, source_target_pairs={{0,2},{1,3},{2,0},{3,1},{4,6},{5,7},{6,4},{7,5},{8,10},{9,11},{10,... | collective-permute-start | bytes 1216520 | tf_op jit(solution)/shard_map/ppermute | solution.py:93
  25.5 12.2 %collective-permute-start.5 = (s16[272,384]{1,0:T(8,128)(2,1)S(1)}, s16[272,384]{1,0:T(8,128)(2,1)S(1)}, u32[]{:S(2)}, u32[]{:S(2)}) collective-permute-start(s16[272,384]{1,0:T(8,128)(2,1)S(1)} %get-tuple-element.52), channel_id=1, source_target_pairs={{0,8},{1,9},{2,10},{3,11},{4,12},{5,13},{6,14},{7,15},{8,0},{9,1},... | collective-permute-start | bytes 626696 | tf_op jit(solution)/shard_map/ppermute | solution.py:93
  28.5 10.8 %collective-permute-start.8 = (s16[288,384]{1,0:T(8,128)(2,1)S(1)}, s16[288,384]{1,0:T(8,128)(2,1)S(1)}, u32[]{:S(2)}, u32[]{:S(2)}) collective-permute-start(s16[288,384]{1,0:T(8,128)(2,1)S(1)} %get-tuple-element.60), channel_id=1, source_target_pairs={{0,4},{1,5},{2,6},{3,7},{4,0},{5,1},{6,2},{7,3},{8,12},{9,13},{10,... | collective-permute-start | bytes 663560 | tf_op jit(solution)/shard_map/ppermute | solution.py:93
  35.4 11.7 %copy-start = (bf16[1,64,128,128]{3,2,1,0:T(8,128)(2,1)S(1)}, bf16[1,64,128,128]{3,2,1,0:T(8,128)(2,1)}, u32[]{:S(2)}) copy-start(bf16[1,64,128,128]{3,2,1,0:T(8,128)(2,1)} %tiles.1) | copy-start | bytes 6291460
  35.4 11.7 %copy-start.3 = (f32[64,64]{1,0:T(8,128)S(1)}, f32[64,64]{1,0:T(8,128)}, u32[]{:S(2)}) copy-start(f32[64,64]{1,0:T(8,128)} %metric.1) | copy-start | bytes 49156
  35.6 7.3 %collective-permute-start.11 = (s16[272,384]{1,0:T(8,128)(2,1)S(1)}, s16[272,384]{1,0:T(8,128)(2,1)S(1)}, u32[]{:S(2)}, u32[]{:S(2)}) collective-permute-start(s16[272,384]{1,0:T(8,128)(2,1)S(1)} %get-tuple-element.69), channel_id=1, source_target_pairs={{0,4},{1,5},{2,6},{3,7},{4,0},{5,1},{6,2},{7,3},{8,12},{9,13},{10,... | collective-permute-start | bytes 626696 | tf_op jit(solution)/shard_map/ppermute | solution.py:93
  37.8 7.9 %collective-permute-start.6 = (s16[144,512]{1,0:T(8,128)(2,1)S(1)}, s16[144,512]{1,0:T(8,128)(2,1)S(1)}, u32[]{:S(2)}, u32[]{:S(2)}) collective-permute-start(s16[144,512]{1,0:T(8,128)(2,1)S(1)} %get-tuple-element.56), channel_id=1, source_target_pairs={{0,2},{1,3},{2,0},{3,1},{4,6},{5,7},{6,4},{7,5},{8,10},{9,11},{10,... | collective-permute-start | bytes 442376 | tf_op jit(solution)/shard_map/ppermute | solution.py:93
  39.4 8.9 %collective-permute-start.9 = (s16[144,384]{1,0:T(8,128)(2,1)S(1)}, s16[144,384]{1,0:T(8,128)(2,1)S(1)}, u32[]{:S(2)}, u32[]{:S(2)}) collective-permute-start(s16[144,384]{1,0:T(8,128)(2,1)S(1)} %get-tuple-element.65), channel_id=1, source_target_pairs={{0,12},{1,13},{2,14},{3,15},{4,8},{5,9},{6,10},{7,11},{8,4},{9,5},... | collective-permute-start | bytes 331784 | tf_op jit(solution)/shard_map/ppermute | solution.py:93
  43.0 9.2 %collective-permute-start.12 = (s16[144,384]{1,0:T(8,128)(2,1)S(1)}, s16[144,384]{1,0:T(8,128)(2,1)S(1)}, u32[]{:S(2)}, u32[]{:S(2)}) collective-permute-start(s16[144,384]{1,0:T(8,128)(2,1)S(1)} %get-tuple-element.71), channel_id=1, source_target_pairs={{0,12},{1,13},{2,14},{3,15},{4,8},{5,9},{6,10},{7,11},{8,4},{9,5},... | collective-permute-start | bytes 331784 | tf_op jit(solution)/shard_map/ppermute | solution.py:93
  45.6 14.1 %copy-start.4 = (s32[16]{0:T(128)S(1)}, s32[16]{0:T(128)}, u32[]{:S(2)}) copy-start(s32[16]{0:T(128)} %holders.1) | copy-start | bytes 196
  45.8 9.4 %collective-permute-start.14 = (bf16[288,128]{1,0:T(8,128)(2,1)S(1)}, bf16[288,128]{1,0:T(8,128)(2,1)S(1)}, u32[]{:S(2)}, u32[]{:S(2)}) collective-permute-start(bf16[288,128]{1,0:T(8,128)(2,1)S(1)} %get-tuple-element.74), channel_id=1, source_target_pairs={{0,12},{1,13},{2,14},{3,15},{4,10},{5,11},{6,8},{7,9},{8,4},{9,5},... | collective-permute-start | bytes 221192 | tf_op jit(solution)/shard_map/ppermute | solution.py:442
  48.4 7.4 %collective-permute-start.16 = (bf16[272,128]{1,0:T(8,128)(2,1)S(1)}, bf16[272,128]{1,0:T(8,128)(2,1)S(1)}, u32[]{:S(2)}, u32[]{:S(2)}) collective-permute-start(bf16[272,128]{1,0:T(8,128)(2,1)S(1)} %get-tuple-element.75), channel_id=1, source_target_pairs={{0,4},{1,5},{2,6},{3,7},{4,2},{5,3},{6,0},{7,1},{8,12},{9,13},{10,... | collective-permute-start | bytes 208904 | tf_op jit(solution)/shard_map/ppermute | solution.py:442
  52.4 6.1 %collective-permute-start.18 = (bf16[256,128]{1,0:T(8,128)(2,1)S(1)}, bf16[256,128]{1,0:T(8,128)(2,1)S(1)}, u32[]{:S(2)}, u32[]{:S(2)}) collective-permute-start(bf16[256,128]{1,0:T(8,128)(2,1)S(1)} %get-tuple-element.76), channel_id=1, source_target_pairs={{0,8},{1,9},{2,10},{3,11},{4,12},{5,13},{6,14},{7,15},{8,2},{9,3},... | collective-permute-start | bytes 196616 | tf_op jit(solution)/shard_map/ppermute | solution.py:442
  55.2 3.3 %collective-permute-start.13 = (bf16[304,128]{1,0:T(8,128)(2,1)S(1)}, bf16[304,128]{1,0:T(8,128)(2,1)S(1)}, u32[]{:S(2)}, u32[]{:S(2)}) collective-permute-start(bf16[304,128]{1,0:T(8,128)(2,1)S(1)} %get-tuple-element.73.extra), channel_id=1, source_target_pairs={{0,1},{1,0},{2,3},{3,2},{4,5},{5,4},{6,7},{7,6},{8,9},{9,8},{10,11... | collective-permute-start | bytes 233480 | tf_op jit(solution)/shard_map/ppermute | solution.py:93
  55.2 4.6 %collective-permute-start.15 = (bf16[288,128]{1,0:T(8,128)(2,1)S(1)}, bf16[288,128]{1,0:T(8,128)(2,1)S(1)}, u32[]{:S(2)}, u32[]{:S(2)}) collective-permute-start(bf16[288,128]{1,0:T(8,128)(2,1)S(1)} %collective-permute-done.14.refs_0_), channel_id=1, source_target_pairs={{0,1},{1,0},{2,3},{3,2},{4,5},{5,4},{6,7},{7,6},{8,9},{9,8},{10,11... | collective-permute-start | bytes 221192 | tf_op jit(solution)/shard_map/ppermute | solution.py:93
  55.7 4.1 %collective-permute-start.17 = (bf16[272,128]{1,0:T(8,128)(2,1)S(1)}, bf16[272,128]{1,0:T(8,128)(2,1)S(1)}, u32[]{:S(2)}, u32[]{:S(2)}) collective-permute-start(bf16[272,128]{1,0:T(8,128)(2,1)S(1)} %collective-permute-done.16.refs_2_), channel_id=1, source_target_pairs={{0,1},{1,0},{2,3},{3,2},{4,5},{5,4},{6,7},{7,6},{8,9},{9,8},{10,11... | collective-permute-start | bytes 208904 | tf_op jit(solution)/shard_map/ppermute | solution.py:93
  58.5 1.3 %collective-permute-start.19 = (bf16[256,128]{1,0:T(8,128)(2,1)S(1)}, bf16[256,128]{1,0:T(8,128)(2,1)S(1)}, u32[]{:S(2)}, u32[]{:S(2)}) collective-permute-start(bf16[256,128]{1,0:T(8,128)(2,1)S(1)} %collective-permute-done.18.refs_4_), channel_id=1, source_target_pairs={{0,1},{1,0},{2,3},{3,2},{4,5},{5,4},{6,7},{7,6},{8,9},{9,8},{10,11... | collective-permute-start | bytes 196616 | tf_op jit(solution)/shard_map/ppermute | solution.py:93

commit v7 on v6

--- a/solution.py
+++ b/solution.py
@@ -120,21 +120,31 @@
     return 2 if region in (1, 2, 3) else 1
 
 
-def encode(out, sums, vector=()):
-    height, columns = sums[0].shape
-    rest = out.shape[0] - len(sums) * height
-    line = lax.broadcasted_iota(jnp.int32, (rest, columns), 0)
-    tail = jnp.zeros((rest, columns), jnp.float32)
-    for j, x in enumerate(sums):
-        peak = jnp.maximum(jnp.max(jnp.abs(x), axis=0, keepdims=True), 2.0**-100)
-        exponent = jnp.ceil(jnp.log2(peak) * 8)
-        scaled = jnp.round(x * jnp.exp2(TOP - exponent * 0.125))
-        out[j * height : (j + 1) * height, :] = scaled.astype(jnp.int32).astype(jnp.int16)
-        tail = jnp.where(line == j, exponent, tail)
+def encode_row(out, j, x, tail):
+    height, columns = x.shape
+    if tail is None:
+        tail = jnp.zeros((out.shape[0] % height, columns), jnp.float32)
+    peak = jnp.maximum(jnp.max(jnp.abs(x), axis=0, keepdims=True), 2.0**-100)
+    exponent = jnp.ceil(jnp.log2(peak) * 8)
+    scaled = jnp.round(x * jnp.exp2(TOP - exponent * 0.125))
+    out[j * height : (j + 1) * height, :] = scaled.astype(jnp.int32).astype(jnp.int16)
+    return jnp.where(lax.broadcasted_iota(jnp.int32, tail.shape, 0) == j, exponent, tail)
+
+
+def encode_tail(out, tail, vector=()):
+    rest, columns = tail.shape
+    line = lax.broadcasted_iota(jnp.int32, tail.shape, 0)
     for j, x in enumerate(vector):
         beside = jnp.zeros((1, columns - x.shape[1]), jnp.float32)
         tail = jnp.where(line == VECTOR + j, jnp.concatenate([x, beside], axis=1), tail)
-    out[len(sums) * height :, :] = tail.astype(jnp.int32).astype(jnp.int16)
+    out[out.shape[0] - rest :, :] = tail.astype(jnp.int32).astype(jnp.int16)
+
+
+def encode(out, sums, vector=()):
+    tail = None
+    for j, x in enumerate(sums):
+        tail = encode_row(out, j, x, tail)
+    encode_tail(out, tail, vector)
 
 
 def encode_vector(x):
@@ -238,7 +248,7 @@
         total = jnp.sum((total + density_of(other, coeffs_other)).T, axis=0, keepdims=True)
         total = jnp.concatenate([total, jnp.zeros((1, width - aux), jnp.float32)], axis=1)
         vector, outs[-1][...] = encode_vector(total)
-    first, gathered = 0, {}
+    first, tails = 0, {}
     for step, (job, j) in enumerate(todo):
         gather(step, 1)
         picked, spread = picks[step % AHEAD], spreads[step % AHEAD]
@@ -263,9 +273,9 @@
             if not coded:
                 out[j] = row
                 continue
-            gathered.setdefault((job, k), []).append(row)
+            tails[job, k] = encode_row(out, j, row, tails.get((job, k)))
             if j + 1 == len(flips):
-                encode(out, gathered[job, k], vector if job + 1 == len(jobs) else ())
+                encode_tail(out, tails[job, k], vector if job + 1 == len(jobs) else ())
         if j + 1 == len(flips):
             first += len(groups)
 

time: 61.5 us -> 61.5 us (level)
  no operation moved by 1% of the time
where the time goes in v7:
time: 61.5 us; the launch traced here: 61.3 us
  starting transfers between devices  27.3 us (44%)
  Pallas kernels  17.9 us (29%)
  waiting for transfers between devices  12 us (20%)
  local copies, waits for them, and re-layouts  2.13 us (3%)
  other arithmetic  1.18 us (2%)
  between operations  0.78 us (1%)
    ppermute x17, starting transfers between devices, send(): return lax.ppermute(x, 'row', [(i, i ^ flip) for i in range(ROWS)])  19.4 us
    pallas_call x2, Pallas kernels, partial_rows(): pl.pallas_call(functools.partial(rows_kernel, jobs, len(coeffs)), in_spec...  13.9 us
    ppermute x17, waiting for transfers between devices, send(): return lax.ppermute(x, 'row', [(i, i ^ flip) for i in range(ROWS)])  9.15 us
    ppermute x3, starting transfers between devices, give_back(): lax.ppermute(blocks, 'row', [(i, i ^ first_place(i, region)) for i in ran...  7.94 us
    ppermute x3, waiting for transfers between devices, give_back(): lax.ppermute(blocks, 'row', [(i, i ^ first_place(i, region)) for i in ran...  2.8 us
    unnamed x10, local copies, waits for them, and re-layouts  2.05 us
    pallas_call x1, Pallas kernels, assemble(): pl.pallas_call(assemble_kernel, in_specs=[pl.BlockSpec(memory_space=pltpu...  1.49 us
    pallas_call x9, Pallas kernels, small_call(): pl.pallas_call(kernel, out_shape=shapes, compiler_params=pltpu.CompilerPa...  1.24 us
  transfers between devices with their start and end apart: 20, of which 5 were waited for; matrix products, arithmetic and copies ran while one was open for 2% of the time, Pallas kernels for 15%

profile of v7, /device:TPU:0, one launch (start us, length us, event | category | flops | bytes accessed | tf_op | source)
XLA Modules:
  0.0 61.3 jit_solution(12516328405617837386)
XLA Ops:
  0.6 0.5 collective-permute-start.2
  1.1 0.9 %fusion.2 = (s32[6,16]{1,0:T(8,128)S(1)}, s32[16,16]{1,0:T(8,128)S(1)}, s32[16,16]{1,0:T(8,128)S(1)}) fusion(s32[16]{0:T(128)} %holders.1, s32[6,16]{1,0:T(8,128)} %bitcast.5), kind=kLoop, calls=%fused_computation.6 | loop fusion | flops 10144 | bytes 2880 | tf_op jit(solution)/shard_map/reduce_sum | solution.py:501
  2.1 0.1 collective-permute-start.1
  2.2 0.5 collective-permute-start.3
  3.1 1.4 %copy-done.1 = bf16[16,6,64,128]{3,2,1,0:T(8,128)(2,1)S(1)} copy-done((bf16[16,6,64,128]{3,2,1,0:T(8,128)(2,1)S(1)}, bf16[16,6,64,128]{3,2,1,0:T(8,128)(2,1)}, u32[]{:S(2)}) %copy-start.1) | copy-done | bytes 1572888
  4.7 0.6 %copy-done.2 = f32[16,6,128]{2,0,1:T(8,128)S(1)} copy-done((f32[16,6,128]{2,0,1:T(8,128)S(1)}, f32[16,6,128]{2,0,1:T(8,128)}, u32[]{:S(2)}) %copy-start.2) | copy-done | bytes 49176
  5.3 7.4 %shard_map.86 = (s16[528,384]{1,0:T(8,128)(2,1)S(1)}, s16[528,384]{1,0:T(8,128)(2,1)S(1)}, s16[528,384]{1,0:T(8,128)(2,1)S(1)}, f32[1,128]{1,0:T(1,128)S(1)}) custom-call(s32[16,6]{1,0:T(8,128)S(1)} %broadcast_add_fusion.listed, s32[6,16]{1,0:T(8,128)S(1)} %get-tuple-element.42.ranks, s32[16,6]{1,0:T(8,128)S(1)} %collective-permute-done.listed_other, ...), custom_call_target="tpu_custom_call" | custom-call | flops 1024 | bytes 1024 | tf_op jit(solution)/shard_map/pallas_call | solution.py:299
  12.7 3.1 %collective-permute-start.4 = (s16[528,384]{1,0:T(8,128)(2,1)S(1)}, s16[528,384]{1,0:T(8,128)(2,1)S(1)}, u32[]{:S(2)}, u32[]{:S(2)}) collective-permute-start(s16[528,384]{1,0:T(8,128)(2,1)S(1)} %get-tuple-element.45), channel_id=1, source_target_pairs={{0,4},{1,5},{2,6},{3,7},{4,0},{5,1},{6,2},{7,3},{8,12},{9,13},{10,... | collective-permute-start | bytes 1216520 | tf_op jit(solution)/shard_map/ppermute | solution.py:93
  15.8 1.5 %collective-permute-start.7 = (s16[528,384]{1,0:T(8,128)(2,1)S(1)}, s16[528,384]{1,0:T(8,128)(2,1)S(1)}, u32[]{:S(2)}, u32[]{:S(2)}) collective-permute-start(s16[528,384]{1,0:T(8,128)(2,1)S(1)} %get-tuple-element.44), channel_id=1, source_target_pairs={{0,2},{1,3},{2,0},{3,1},{4,6},{5,7},{6,4},{7,5},{8,10},{9,11},{10,... | collective-permute-start | bytes 1216520 | tf_op jit(solution)/shard_map/ppermute | solution.py:93
  17.2 0.5 collective-permute-start.10
  17.8 6.6 %shard_map.87 = (f32[4,128,384]{2,1,0:T(8,128)S(1)}, f32[4,128,384]{2,1,0:T(8,128)S(1)}, f32[4,128,384]{2,1,0:T(8,128)S(1)}) custom-call(s32[16,6]{1,0:T(8,128)S(1)} %broadcast_add_fusion.listed, s32[6,16]{1,0:T(8,128)S(1)} %get-tuple-element.42.ranks, s32[16,6]{1,0:T(8,128)S(1)} %collective-permute-done.listed_other, ...), custom_call_target="tpu_custom_call" | custom-call | flops 1024 | bytes 1024 | tf_op jit(solution)/shard_map/pallas_call | solution.py:299
  24.4 1.0 %collective-permute-done.4.code = s16[528,384]{1,0:T(8,128)(2,1)S(1)} collective-permute-done((s16[528,384]{1,0:T(8,128)(2,1)S(1)}, s16[528,384]{1,0:T(8,128)(2,1)S(1)}, u32[]{:S(2)}, u32[]{:S(2)}) %collective-permute-start.4) | collective-permute-done | bytes 405536 | tf_op jit(solution)/shard_map/ppermute | solution.py:93
  25.4 0.2 shard_map.88
  25.6 2.8 %collective-permute-start.5 = (s16[272,384]{1,0:T(8,128)(2,1)S(1)}, s16[272,384]{1,0:T(8,128)(2,1)S(1)}, u32[]{:S(2)}, u32[]{:S(2)}) collective-permute-start(s16[272,384]{1,0:T(8,128)(2,1)S(1)} %get-tuple-element.52), channel_id=1, source_target_pairs={{0,8},{1,9},{2,10},{3,11},{4,12},{5,13},{6,14},{7,15},{8,0},{9,1},... | collective-permute-start | bytes 626696 | tf_op jit(solution)/shard_map/ppermute | solution.py:93
  28.4 0.2 shard_map.91
  28.6 1.7 %collective-permute-start.8 = (s16[288,384]{1,0:T(8,128)(2,1)S(1)}, s16[288,384]{1,0:T(8,128)(2,1)S(1)}, u32[]{:S(2)}, u32[]{:S(2)}) collective-permute-start(s16[288,384]{1,0:T(8,128)(2,1)S(1)} %get-tuple-element.60), channel_id=1, source_target_pairs={{0,4},{1,5},{2,6},{3,7},{4,0},{5,1},{6,2},{7,3},{8,12},{9,13},{10,... | collective-permute-start | bytes 663560 | tf_op jit(solution)/shard_map/ppermute | solution.py:93
  30.2 5.3 %collective-permute-done.10.code = s16[528,384]{1,0:T(8,128)(2,1)S(1)} collective-permute-done((s16[528,384]{1,0:T(8,128)(2,1)S(1)}, s16[528,384]{1,0:T(8,128)(2,1)S(1)}, u32[]{:S(2)}, u32[]{:S(2)}) %collective-permute-start.10) | collective-permute-done | bytes 405536 | tf_op jit(solution)/shard_map/ppermute | solution.py:93
  35.5 0.2 shard_map.95
  35.7 0.4 collective-permute-start.11
  36.1 1.6 %collective-permute-done.5.code = s16[272,384]{1,0:T(8,128)(2,1)S(1)} collective-permute-done((s16[272,384]{1,0:T(8,128)(2,1)S(1)}, s16[272,384]{1,0:T(8,128)(2,1)S(1)}, u32[]{:S(2)}, u32[]{:S(2)}) %collective-permute-start.5) | collective-permute-done | bytes 208928 | tf_op jit(solution)/shard_map/ppermute | solution.py:93
  37.8 1.4 %collective-permute-start.6 = (s16[144,512]{1,0:T(8,128)(2,1)S(1)}, s16[144,512]{1,0:T(8,128)(2,1)S(1)}, u32[]{:S(2)}, u32[]{:S(2)}) collective-permute-start(s16[144,512]{1,0:T(8,128)(2,1)S(1)} %get-tuple-element.56), channel_id=1, source_target_pairs={{0,2},{1,3},{2,0},{3,1},{4,6},{5,7},{6,4},{7,5},{8,10},{9,11},{10,... | collective-permute-start | bytes 442376 | tf_op jit(solution)/shard_map/ppermute | solution.py:93
  39.3 3.6 %collective-permute-start.9 = (s16[144,384]{1,0:T(8,128)(2,1)S(1)}, s16[144,384]{1,0:T(8,128)(2,1)S(1)}, u32[]{:S(2)}, u32[]{:S(2)}) collective-permute-start(s16[144,384]{1,0:T(8,128)(2,1)S(1)} %get-tuple-element.65), channel_id=1, source_target_pairs={{0,12},{1,13},{2,14},{3,15},{4,8},{5,9},{6,10},{7,11},{8,4},{9,5},... | collective-permute-start | bytes 331784 | tf_op jit(solution)/shard_map/ppermute | solution.py:93
  43.0 2.7 %collective-permute-start.12 = (s16[144,384]{1,0:T(8,128)(2,1)S(1)}, s16[144,384]{1,0:T(8,128)(2,1)S(1)}, u32[]{:S(2)}, u32[]{:S(2)}) collective-permute-start(s16[144,384]{1,0:T(8,128)(2,1)S(1)} %get-tuple-element.71), channel_id=1, source_target_pairs={{0,12},{1,13},{2,14},{3,15},{4,8},{5,9},{6,10},{7,11},{8,4},{9,5},... | collective-permute-start | bytes 331784 | tf_op jit(solution)/shard_map/ppermute | solution.py:93
  45.7 0.1 shard_map.90
  45.8 1.3 %collective-permute-start.14 = (bf16[288,128]{1,0:T(8,128)(2,1)S(1)}, bf16[288,128]{1,0:T(8,128)(2,1)S(1)}, u32[]{:S(2)}, u32[]{:S(2)}) collective-permute-start(bf16[288,128]{1,0:T(8,128)(2,1)S(1)} %get-tuple-element.74), channel_id=1, source_target_pairs={{0,12},{1,13},{2,14},{3,15},{4,10},{5,11},{6,8},{7,9},{8,4},{9,5},... | collective-permute-start | bytes 221192 | tf_op jit(solution)/shard_map/ppermute | solution.py:452
  47.1 1.1 %shard_map.93 = (f32[1,64]{1,0:T(1,128)}, bf16[1,128,128]{2,1,0:T(8,128)(2,1)}) custom-call(f32[1,128]{1,0:T(1,128)S(1)} %get-tuple-element.62.vector, f32[64,64]{1,0:T(8,128)S(1)} %copy-done.3, bf16[1,64,128,128]{3,2,1,0:T(8,128)(2,1)S(1)} %copy-done), custom_call_target="tpu_custom_call" | custom-call | flops 1024 | bytes 1024 | tf_op jit(solution)/shard_map/pallas_call | solution.py:396
  48.4 3.9 %collective-permute-start.16 = (bf16[272,128]{1,0:T(8,128)(2,1)S(1)}, bf16[272,128]{1,0:T(8,128)(2,1)S(1)}, u32[]{:S(2)}, u32[]{:S(2)}) collective-permute-start(bf16[272,128]{1,0:T(8,128)(2,1)S(1)} %get-tuple-element.75), channel_id=1, source_target_pairs={{0,4},{1,5},{2,6},{3,7},{4,2},{5,3},{6,0},{7,1},{8,12},{9,13},{10,... | collective-permute-start | bytes 208904 | tf_op jit(solution)/shard_map/ppermute | solution.py:452
  52.4 2.7 %collective-permute-start.18 = (bf16[256,128]{1,0:T(8,128)(2,1)S(1)}, bf16[256,128]{1,0:T(8,128)(2,1)S(1)}, u32[]{:S(2)}, u32[]{:S(2)}) collective-permute-start(bf16[256,128]{1,0:T(8,128)(2,1)S(1)} %get-tuple-element.76), channel_id=1, source_target_pairs={{0,8},{1,9},{2,10},{3,11},{4,12},{5,13},{6,14},{7,15},{8,2},{9,3},... | collective-permute-start | bytes 196616 | tf_op jit(solution)/shard_map/ppermute | solution.py:452
  55.1 0.5 collective-permute-start.15
  55.7 2.8 %collective-permute-done.18.refs_4_ = bf16[256,128]{1,0:T(8,128)(2,1)S(1)} collective-permute-done((bf16[256,128]{1,0:T(8,128)(2,1)S(1)}, bf16[256,128]{1,0:T(8,128)(2,1)S(1)}, u32[]{:S(2)}, u32[]{:S(2)}) %collective-permute-start.18) | collective-permute-done | bytes 65568 | tf_op jit(solution)/shard_map/ppermute | solution.py:452
  58.5 1.2 %collective-permute-done.19.refs_5_ = bf16[256,128]{1,0:T(8,128)(2,1)S(1)} collective-permute-done((bf16[256,128]{1,0:T(8,128)(2,1)S(1)}, bf16[256,128]{1,0:T(8,128)(2,1)S(1)}, u32[]{:S(2)}, u32[]{:S(2)}) %collective-permute-start.19) | collective-permute-done | bytes 65568 | tf_op jit(solution)/shard_map/ppermute | solution.py:93
  59.8 1.5 %shard_map.98 = bf16[1,128,2048]{2,1,0:T(8,128)(2,1)} custom-call(s32[16]{0:T(128)S(1)} %copy-done.4, bf16[128,384]{1,0:T(8,128)(2,1)S(1)} %get-tuple-element.57.early, bf16[128,384]{1,0:T(8,128)(2,1)S(1)} %get-tuple-element.66.late, bf16[128,384]{1,0:T(8,128)(2,1)S(1)} %get-tuple-element.72.later, bf16[304,128]{1,0:T(8,128)(2,1)S(1)} %get-tuple-element.73.extra, ...), custom_call_target="tpu_custom_call" | custom-call | flops 1024 | bytes 1024 | tf_op jit(solution)/shard_map/pallas_call | solution.py:488
  (41 shorter events, 1.2 us)
Async XLA Ops:
  0.6 4.0 %collective-permute-start.2 = (bf16[16,6,64,128]{3,2,1,0:T(8,128)(2,1)}, bf16[16,6,64,128]{3,2,1,0:T(8,128)(2,1)S(1)}, u32[]{:S(2)}, u32[]{:S(2)}) collective-permute-start(bf16[16,6,64,128]{3,2,1,0:T(8,128)(2,1)} %far), channel_id=1, source_target_pairs={{0,1},{1,0},{2,3},{3,2},{4,5},{5,4},{6,7},{7,6},{8,9},{9,8},{10,11... | collective-permute-start | bytes 4718600 | tf_op jit(solution)/shard_map/ppermute | solution.py:93
  2.1 2.5 %collective-permute-start.1 = (s32[6,16]{1,0:T(8,128)S(1)}, s32[6,16]{1,0:T(8,128)S(1)}, u32[]{:S(2)}, u32[]{:S(2)}) collective-permute-start(s32[6,16]{1,0:T(8,128)S(1)} %get-tuple-element.42.ranks), channel_id=1, source_target_pairs={{0,1},{1,0},{2,3},{3,2},{4,5},{5,4},{6,7},{7,6},{8,9},{9,8},{10,11... | collective-permute-start | bytes 1160 | tf_op jit(solution)/shard_map/ppermute | solution.py:93
  2.2 2.4 %collective-permute-start.3 = (f32[6,16,128]{2,1,0:T(8,128)}, f32[6,16,128]{2,1,0:T(8,128)S(1)}, u32[]{:S(2)}, u32[]{:S(2)}) collective-permute-start(f32[6,16,128]{2,1,0:T(8,128)} %bitcast.3), channel_id=1, source_target_pairs={{0,1},{1,0},{2,3},{3,2},{4,5},{5,4},{6,7},{7,6},{8,9},{9,8},{10,11... | collective-permute-start | bytes 147464 | tf_op jit(solution)/shard_map/ppermute | solution.py:93
  3.0 1.6 %collective-permute-start = (s32[16,6]{1,0:T(8,128)S(1)}, s32[16,6]{1,0:T(8,128)S(1)}, u32[]{:S(2)}, u32[]{:S(2)}) collective-permute-start(s32[16,6]{1,0:T(8,128)S(1)} %broadcast_add_fusion.listed), channel_id=1, source_target_pairs={{0,1},{1,0},{2,3},{3,2},{4,5},{5,4},{6,7},{7,6},{8,9},{9,8},{10,11... | collective-permute-start | bytes 1160 | tf_op jit(solution)/shard_map/ppermute | solution.py:93
  3.1 1.4 %copy-start.1 = (bf16[16,6,64,128]{3,2,1,0:T(8,128)(2,1)S(1)}, bf16[16,6,64,128]{3,2,1,0:T(8,128)(2,1)}, u32[]{:S(2)}) copy-start(bf16[16,6,64,128]{3,2,1,0:T(8,128)(2,1)} %far) | copy-start | bytes 4718596
  4.5 0.8 %copy-start.2 = (f32[16,6,128]{2,0,1:T(8,128)S(1)}, f32[16,6,128]{2,0,1:T(8,128)}, u32[]{:S(2)}) copy-start(f32[16,6,128]{2,0,1:T(8,128)} %param.9) | copy-start | bytes 147460
  12.7 12.7 %collective-permute-start.4 = (s16[528,384]{1,0:T(8,128)(2,1)S(1)}, s16[528,384]{1,0:T(8,128)(2,1)S(1)}, u32[]{:S(2)}, u32[]{:S(2)}) collective-permute-start(s16[528,384]{1,0:T(8,128)(2,1)S(1)} %get-tuple-element.45), channel_id=1, source_target_pairs={{0,4},{1,5},{2,6},{3,7},{4,0},{5,1},{6,2},{7,3},{8,12},{9,13},{10,... | collective-permute-start | bytes 1216520 | tf_op jit(solution)/shard_map/ppermute | solution.py:93
  15.8 12.6 %collective-permute-start.7 = (s16[528,384]{1,0:T(8,128)(2,1)S(1)}, s16[528,384]{1,0:T(8,128)(2,1)S(1)}, u32[]{:S(2)}, u32[]{:S(2)}) collective-permute-start(s16[528,384]{1,0:T(8,128)(2,1)S(1)} %get-tuple-element.44), channel_id=1, source_target_pairs={{0,2},{1,3},{2,0},{3,1},{4,6},{5,7},{6,4},{7,5},{8,10},{9,11},{10,... | collective-permute-start | bytes 1216520 | tf_op jit(solution)/shard_map/ppermute | solution.py:93
  17.2 18.3 %collective-permute-start.10 = (s16[528,384]{1,0:T(8,128)(2,1)S(1)}, s16[528,384]{1,0:T(8,128)(2,1)S(1)}, u32[]{:S(2)}, u32[]{:S(2)}) collective-permute-start(s16[528,384]{1,0:T(8,128)(2,1)S(1)} %get-tuple-element.46), channel_id=1, source_target_pairs={{0,2},{1,3},{2,0},{3,1},{4,6},{5,7},{6,4},{7,5},{8,10},{9,11},{10,... | collective-permute-start | bytes 1216520 | tf_op jit(solution)/shard_map/ppermute | solution.py:93
  25.6 12.1 %collective-permute-start.5 = (s16[272,384]{1,0:T(8,128)(2,1)S(1)}, s16[272,384]{1,0:T(8,128)(2,1)S(1)}, u32[]{:S(2)}, u32[]{:S(2)}) collective-permute-start(s16[272,384]{1,0:T(8,128)(2,1)S(1)} %get-tuple-element.52), channel_id=1, source_target_pairs={{0,8},{1,9},{2,10},{3,11},{4,12},{5,13},{6,14},{7,15},{8,0},{9,1},... | collective-permute-start | bytes 626696 | tf_op jit(solution)/shard_map/ppermute | solution.py:93
  28.6 10.6 %collective-permute-start.8 = (s16[288,384]{1,0:T(8,128)(2,1)S(1)}, s16[288,384]{1,0:T(8,128)(2,1)S(1)}, u32[]{:S(2)}, u32[]{:S(2)}) collective-permute-start(s16[288,384]{1,0:T(8,128)(2,1)S(1)} %get-tuple-element.60), channel_id=1, source_target_pairs={{0,4},{1,5},{2,6},{3,7},{4,0},{5,1},{6,2},{7,3},{8,12},{9,13},{10,... | collective-permute-start | bytes 663560 | tf_op jit(solution)/shard_map/ppermute | solution.py:93
  35.5 11.6 %copy-start = (bf16[1,64,128,128]{3,2,1,0:T(8,128)(2,1)S(1)}, bf16[1,64,128,128]{3,2,1,0:T(8,128)(2,1)}, u32[]{:S(2)}) copy-start(bf16[1,64,128,128]{3,2,1,0:T(8,128)(2,1)} %tiles.1) | copy-start | bytes 6291460
  35.5 11.6 %copy-start.3 = (f32[64,64]{1,0:T(8,128)S(1)}, f32[64,64]{1,0:T(8,128)}, u32[]{:S(2)}) copy-start(f32[64,64]{1,0:T(8,128)} %metric.1) | copy-start | bytes 49156
  35.7 7.2 %collective-permute-start.11 = (s16[272,384]{1,0:T(8,128)(2,1)S(1)}, s16[272,384]{1,0:T(8,128)(2,1)S(1)}, u32[]{:S(2)}, u32[]{:S(2)}) collective-permute-start(s16[272,384]{1,0:T(8,128)(2,1)S(1)} %get-tuple-element.69), channel_id=1, source_target_pairs={{0,4},{1,5},{2,6},{3,7},{4,0},{5,1},{6,2},{7,3},{8,12},{9,13},{10,... | collective-permute-start | bytes 626696 | tf_op jit(solution)/shard_map/ppermute | solution.py:93
  37.8 7.9 %collective-permute-start.6 = (s16[144,512]{1,0:T(8,128)(2,1)S(1)}, s16[144,512]{1,0:T(8,128)(2,1)S(1)}, u32[]{:S(2)}, u32[]{:S(2)}) collective-permute-start(s16[144,512]{1,0:T(8,128)(2,1)S(1)} %get-tuple-element.56), channel_id=1, source_target_pairs={{0,2},{1,3},{2,0},{3,1},{4,6},{5,7},{6,4},{7,5},{8,10},{9,11},{10,... | collective-permute-start | bytes 442376 | tf_op jit(solution)/shard_map/ppermute | solution.py:93
  39.3 8.9 %collective-permute-start.9 = (s16[144,384]{1,0:T(8,128)(2,1)S(1)}, s16[144,384]{1,0:T(8,128)(2,1)S(1)}, u32[]{:S(2)}, u32[]{:S(2)}) collective-permute-start(s16[144,384]{1,0:T(8,128)(2,1)S(1)} %get-tuple-element.65), channel_id=1, source_target_pairs={{0,12},{1,13},{2,14},{3,15},{4,8},{5,9},{6,10},{7,11},{8,4},{9,5},... | collective-permute-start | bytes 331784 | tf_op jit(solution)/shard_map/ppermute | solution.py:93
  43.0 9.3 %collective-permute-start.12 = (s16[144,384]{1,0:T(8,128)(2,1)S(1)}, s16[144,384]{1,0:T(8,128)(2,1)S(1)}, u32[]{:S(2)}, u32[]{:S(2)}) collective-permute-start(s16[144,384]{1,0:T(8,128)(2,1)S(1)} %get-tuple-element.71), channel_id=1, source_target_pairs={{0,12},{1,13},{2,14},{3,15},{4,8},{5,9},{6,10},{7,11},{8,4},{9,5},... | collective-permute-start | bytes 331784 | tf_op jit(solution)/shard_map/ppermute | solution.py:93
  45.7 14.1 %copy-start.4 = (s32[16]{0:T(128)S(1)}, s32[16]{0:T(128)}, u32[]{:S(2)}) copy-start(s32[16]{0:T(128)} %holders.1) | copy-start | bytes 196
  45.8 9.3 %collective-permute-start.14 = (bf16[288,128]{1,0:T(8,128)(2,1)S(1)}, bf16[288,128]{1,0:T(8,128)(2,1)S(1)}, u32[]{:S(2)}, u32[]{:S(2)}) collective-permute-start(bf16[288,128]{1,0:T(8,128)(2,1)S(1)} %get-tuple-element.74), channel_id=1, source_target_pairs={{0,12},{1,13},{2,14},{3,15},{4,10},{5,11},{6,8},{7,9},{8,4},{9,5},... | collective-permute-start | bytes 221192 | tf_op jit(solution)/shard_map/ppermute | solution.py:452
  48.4 7.3 %collective-permute-start.16 = (bf16[272,128]{1,0:T(8,128)(2,1)S(1)}, bf16[272,128]{1,0:T(8,128)(2,1)S(1)}, u32[]{:S(2)}, u32[]{:S(2)}) collective-permute-start(bf16[272,128]{1,0:T(8,128)(2,1)S(1)} %get-tuple-element.75), channel_id=1, source_target_pairs={{0,4},{1,5},{2,6},{3,7},{4,2},{5,3},{6,0},{7,1},{8,12},{9,13},{10,... | collective-permute-start | bytes 208904 | tf_op jit(solution)/shard_map/ppermute | solution.py:452
  52.4 6.1 %collective-permute-start.18 = (bf16[256,128]{1,0:T(8,128)(2,1)S(1)}, bf16[256,128]{1,0:T(8,128)(2,1)S(1)}, u32[]{:S(2)}, u32[]{:S(2)}) collective-permute-start(bf16[256,128]{1,0:T(8,128)(2,1)S(1)} %get-tuple-element.76), channel_id=1, source_target_pairs={{0,8},{1,9},{2,10},{3,11},{4,12},{5,13},{6,14},{7,15},{8,2},{9,3},... | collective-permute-start | bytes 196616 | tf_op jit(solution)/shard_map/ppermute | solution.py:452
  55.1 3.4 %collective-permute-start.13 = (bf16[304,128]{1,0:T(8,128)(2,1)S(1)}, bf16[304,128]{1,0:T(8,128)(2,1)S(1)}, u32[]{:S(2)}, u32[]{:S(2)}) collective-permute-start(bf16[304,128]{1,0:T(8,128)(2,1)S(1)} %get-tuple-element.73.extra), channel_id=1, source_target_pairs={{0,1},{1,0},{2,3},{3,2},{4,5},{5,4},{6,7},{7,6},{8,9},{9,8},{10,11... | collective-permute-start | bytes 233480 | tf_op jit(solution)/shard_map/ppermute | solution.py:93
  55.1 4.6 %collective-permute-start.15 = (bf16[288,128]{1,0:T(8,128)(2,1)S(1)}, bf16[288,128]{1,0:T(8,128)(2,1)S(1)}, u32[]{:S(2)}, u32[]{:S(2)}) collective-permute-start(bf16[288,128]{1,0:T(8,128)(2,1)S(1)} %collective-permute-done.14.refs_0_), channel_id=1, source_target_pairs={{0,1},{1,0},{2,3},{3,2},{4,5},{5,4},{6,7},{7,6},{8,9},{9,8},{10,11... | collective-permute-start | bytes 221192 | tf_op jit(solution)/shard_map/ppermute | solution.py:93
  55.7 4.1 %collective-permute-start.17 = (bf16[272,128]{1,0:T(8,128)(2,1)S(1)}, bf16[272,128]{1,0:T(8,128)(2,1)S(1)}, u32[]{:S(2)}, u32[]{:S(2)}) collective-permute-start(bf16[272,128]{1,0:T(8,128)(2,1)S(1)} %collective-permute-done.16.refs_2_), channel_id=1, source_target_pairs={{0,1},{1,0},{2,3},{3,2},{4,5},{5,4},{6,7},{7,6},{8,9},{9,8},{10,11... | collective-permute-start | bytes 208904 | tf_op jit(solution)/shard_map/ppermute | solution.py:93
  58.5 1.3 %collective-permute-start.19 = (bf16[256,128]{1,0:T(8,128)(2,1)S(1)}, bf16[256,128]{1,0:T(8,128)(2,1)S(1)}, u32[]{:S(2)}, u32[]{:S(2)}) collective-permute-start(bf16[256,128]{1,0:T(8,128)(2,1)S(1)} %collective-permute-done.18.refs_4_), channel_id=1, source_target_pairs={{0,1},{1,0},{2,3},{3,2},{4,5},{5,4},{6,7},{7,6},{8,9},{9,8},{10,11... | collective-permute-start | bytes 196616 | tf_op jit(solution)/shard_map/ppermute | solution.py:93

commit v8 on v7

--- a/solution.py
+++ b/solution.py
@@ -84,7 +84,7 @@
 TOP = 14.99
 SPARE = 0
 VECTOR = 4
-AHEAD = 6
+AHEAD = 8
 SHORT = pl.CostEstimate(flops=1024, bytes_accessed=1024, transcendentals=0)
 LONG = pl.CostEstimate(flops=1 << 32, bytes_accessed=1024, transcendentals=0)
 
@@ -304,7 +304,7 @@
         scratch_shapes=[pltpu.VMEM((depth, width), jnp.bfloat16)] * AHEAD
         + [pltpu.VMEM((depth, PLACES * width), jnp.bfloat16)] * AHEAD
         + [pltpu.VMEM(panels[1].shape, jnp.bfloat16), pltpu.SemaphoreType.DMA],
-        compiler_params=pltpu.CompilerParams(vmem_limit_bytes=28 << 20),
+        compiler_params=pltpu.CompilerParams(vmem_limit_bytes=40 << 20),
         cost_estimate=SHORT,
     )(lists[0], ranks[0], lists[1], ranks[1], *panels, *coeffs)
 

time: 61.5 us -> 61.5 us (level)
  no operation moved by 1% of the time
where the time goes in v8:
time: 61.5 us; the launch traced here: 61.3 us
  starting transfers between devices  27.5 us (45%)
  Pallas kernels  18 us (29%)
  waiting for transfers between devices  11.6 us (19%)
  local copies, waits for them, and re-layouts  2.13 us (3%)
  other arithmetic  1.18 us (2%)
  between operations  0.78 us (1%)
    ppermute x17, starting transfers between devices, send(): return lax.ppermute(x, 'row', [(i, i ^ flip) for i in range(ROWS)])  19.6 us
    pallas_call x2, Pallas kernels, partial_rows(): pl.pallas_call(functools.partial(rows_kernel, jobs, len(coeffs)), in_spec...  14.1 us
    ppermute x17, waiting for transfers between devices, send(): return lax.ppermute(x, 'row', [(i, i ^ flip) for i in range(ROWS)])  8.8 us
    ppermute x3, starting transfers between devices, give_back(): lax.ppermute(blocks, 'row', [(i, i ^ first_place(i, region)) for i in ran...  7.98 us
    ppermute x3, waiting for transfers between devices, give_back(): lax.ppermute(blocks, 'row', [(i, i ^ first_place(i, region)) for i in ran...  2.78 us
    unnamed x10, local copies, waits for them, and re-layouts  2.05 us
    pallas_call x1, Pallas kernels, assemble(): pl.pallas_call(assemble_kernel, in_specs=[pl.BlockSpec(memory_space=pltpu...  1.49 us
    pallas_call x9, Pallas kernels, small_call(): pl.pallas_call(kernel, out_shape=shapes, compiler_params=pltpu.CompilerPa...  1.24 us
  transfers between devices with their start and end apart: 20, of which 5 were waited for; matrix products, arithmetic and copies ran while one was open for 2% of the time, Pallas kernels for 15%

profile of v8, /device:TPU:0, one launch (start us, length us, event | category | flops | bytes accessed | tf_op | source)
XLA Modules:
  0.0 61.3 jit_solution(16489576712564370520)
XLA Ops:
  0.6 0.5 collective-permute-start.2
  1.1 0.9 %fusion.2 = (s32[6,16]{1,0:T(8,128)S(1)}, s32[16,16]{1,0:T(8,128)S(1)}, s32[16,16]{1,0:T(8,128)S(1)}) fusion(s32[16]{0:T(128)} %holders.1, s32[6,16]{1,0:T(8,128)} %bitcast.5), kind=kLoop, calls=%fused_computation.6 | loop fusion | flops 10144 | bytes 2880 | tf_op jit(solution)/shard_map/reduce_sum | solution.py:501
  2.1 0.1 collective-permute-start.1
  2.2 0.5 collective-permute-start.3
  3.1 1.4 %copy-done.1 = bf16[16,6,64,128]{3,2,1,0:T(8,128)(2,1)S(1)} copy-done((bf16[16,6,64,128]{3,2,1,0:T(8,128)(2,1)S(1)}, bf16[16,6,64,128]{3,2,1,0:T(8,128)(2,1)}, u32[]{:S(2)}) %copy-start.1) | copy-done | bytes 1572888
  4.7 0.6 %copy-done.2 = f32[16,6,128]{2,0,1:T(8,128)S(1)} copy-done((f32[16,6,128]{2,0,1:T(8,128)S(1)}, f32[16,6,128]{2,0,1:T(8,128)}, u32[]{:S(2)}) %copy-start.2) | copy-done | bytes 49176
  5.3 7.3 %shard_map.86 = (s16[528,384]{1,0:T(8,128)(2,1)S(1)}, s16[528,384]{1,0:T(8,128)(2,1)S(1)}, s16[528,384]{1,0:T(8,128)(2,1)S(1)}, f32[1,128]{1,0:T(1,128)S(1)}) custom-call(s32[16,6]{1,0:T(8,128)S(1)} %broadcast_add_fusion.listed, s32[6,16]{1,0:T(8,128)S(1)} %get-tuple-element.42.ranks, s32[16,6]{1,0:T(8,128)S(1)} %collective-permute-done.listed_other, ...), custom_call_target="tpu_custom_call" | custom-call | flops 1024 | bytes 1024 | tf_op jit(solution)/shard_map/pallas_call | solution.py:299
  12.6 3.1 %collective-permute-start.4 = (s16[528,384]{1,0:T(8,128)(2,1)S(1)}, s16[528,384]{1,0:T(8,128)(2,1)S(1)}, u32[]{:S(2)}, u32[]{:S(2)}) collective-permute-start(s16[528,384]{1,0:T(8,128)(2,1)S(1)} %get-tuple-element.45), channel_id=1, source_target_pairs={{0,4},{1,5},{2,6},{3,7},{4,0},{5,1},{6,2},{7,3},{8,12},{9,13},{10,... | collective-permute-start | bytes 1216520 | tf_op jit(solution)/shard_map/ppermute | solution.py:93
  15.7 1.5 %collective-permute-start.7 = (s16[528,384]{1,0:T(8,128)(2,1)S(1)}, s16[528,384]{1,0:T(8,128)(2,1)S(1)}, u32[]{:S(2)}, u32[]{:S(2)}) collective-permute-start(s16[528,384]{1,0:T(8,128)(2,1)S(1)} %get-tuple-element.44), channel_id=1, source_target_pairs={{0,2},{1,3},{2,0},{3,1},{4,6},{5,7},{6,4},{7,5},{8,10},{9,11},{10,... | collective-permute-start | bytes 1216520 | tf_op jit(solution)/shard_map/ppermute | solution.py:93
  17.2 0.5 collective-permute-start.10
  17.7 6.8 %shard_map.87 = (f32[4,128,384]{2,1,0:T(8,128)S(1)}, f32[4,128,384]{2,1,0:T(8,128)S(1)}, f32[4,128,384]{2,1,0:T(8,128)S(1)}) custom-call(s32[16,6]{1,0:T(8,128)S(1)} %broadcast_add_fusion.listed, s32[6,16]{1,0:T(8,128)S(1)} %get-tuple-element.42.ranks, s32[16,6]{1,0:T(8,128)S(1)} %collective-permute-done.listed_other, ...), custom_call_target="tpu_custom_call" | custom-call | flops 1024 | bytes 1024 | tf_op jit(solution)/shard_map/pallas_call | solution.py:299
  24.5 0.7 %collective-permute-done.4.code = s16[528,384]{1,0:T(8,128)(2,1)S(1)} collective-permute-done((s16[528,384]{1,0:T(8,128)(2,1)S(1)}, s16[528,384]{1,0:T(8,128)(2,1)S(1)}, u32[]{:S(2)}, u32[]{:S(2)}) %collective-permute-start.4) | collective-permute-done | bytes 405536 | tf_op jit(solution)/shard_map/ppermute | solution.py:93
  25.3 0.2 shard_map.88
  25.4 2.9 %collective-permute-start.5 = (s16[272,384]{1,0:T(8,128)(2,1)S(1)}, s16[272,384]{1,0:T(8,128)(2,1)S(1)}, u32[]{:S(2)}, u32[]{:S(2)}) collective-permute-start(s16[272,384]{1,0:T(8,128)(2,1)S(1)} %get-tuple-element.52), channel_id=1, source_target_pairs={{0,8},{1,9},{2,10},{3,11},{4,12},{5,13},{6,14},{7,15},{8,0},{9,1},... | collective-permute-start | bytes 626696 | tf_op jit(solution)/shard_map/ppermute | solution.py:93
  28.3 0.2 shard_map.91
  28.5 1.6 %collective-permute-start.8 = (s16[288,384]{1,0:T(8,128)(2,1)S(1)}, s16[288,384]{1,0:T(8,128)(2,1)S(1)}, u32[]{:S(2)}, u32[]{:S(2)}) collective-permute-start(s16[288,384]{1,0:T(8,128)(2,1)S(1)} %get-tuple-element.60), channel_id=1, source_target_pairs={{0,4},{1,5},{2,6},{3,7},{4,0},{5,1},{6,2},{7,3},{8,12},{9,13},{10,... | collective-permute-start | bytes 663560 | tf_op jit(solution)/shard_map/ppermute | solution.py:93
  30.1 5.3 %collective-permute-done.10.code = s16[528,384]{1,0:T(8,128)(2,1)S(1)} collective-permute-done((s16[528,384]{1,0:T(8,128)(2,1)S(1)}, s16[528,384]{1,0:T(8,128)(2,1)S(1)}, u32[]{:S(2)}, u32[]{:S(2)}) %collective-permute-start.10) | collective-permute-done | bytes 405536 | tf_op jit(solution)/shard_map/ppermute | solution.py:93
  35.4 0.2 shard_map.95
  35.6 0.4 collective-permute-start.11
  36.0 1.5 %collective-permute-done.5.code = s16[272,384]{1,0:T(8,128)(2,1)S(1)} collective-permute-done((s16[272,384]{1,0:T(8,128)(2,1)S(1)}, s16[272,384]{1,0:T(8,128)(2,1)S(1)}, u32[]{:S(2)}, u32[]{:S(2)}) %collective-permute-start.5) | collective-permute-done | bytes 208928 | tf_op jit(solution)/shard_map/ppermute | solution.py:93
  37.7 1.5 %collective-permute-start.6 = (s16[144,512]{1,0:T(8,128)(2,1)S(1)}, s16[144,512]{1,0:T(8,128)(2,1)S(1)}, u32[]{:S(2)}, u32[]{:S(2)}) collective-permute-start(s16[144,512]{1,0:T(8,128)(2,1)S(1)} %get-tuple-element.56), channel_id=1, source_target_pairs={{0,2},{1,3},{2,0},{3,1},{4,6},{5,7},{6,4},{7,5},{8,10},{9,11},{10,... | collective-permute-start | bytes 442376 | tf_op jit(solution)/shard_map/ppermute | solution.py:93
  39.3 3.6 %collective-permute-start.9 = (s16[144,384]{1,0:T(8,128)(2,1)S(1)}, s16[144,384]{1,0:T(8,128)(2,1)S(1)}, u32[]{:S(2)}, u32[]{:S(2)}) collective-permute-start(s16[144,384]{1,0:T(8,128)(2,1)S(1)} %get-tuple-element.65), channel_id=1, source_target_pairs={{0,12},{1,13},{2,14},{3,15},{4,8},{5,9},{6,10},{7,11},{8,4},{9,5},... | collective-permute-start | bytes 331784 | tf_op jit(solution)/shard_map/ppermute | solution.py:93
  43.0 2.7 %collective-permute-start.12 = (s16[144,384]{1,0:T(8,128)(2,1)S(1)}, s16[144,384]{1,0:T(8,128)(2,1)S(1)}, u32[]{:S(2)}, u32[]{:S(2)}) collective-permute-start(s16[144,384]{1,0:T(8,128)(2,1)S(1)} %get-tuple-element.71), channel_id=1, source_target_pairs={{0,12},{1,13},{2,14},{3,15},{4,8},{5,9},{6,10},{7,11},{8,4},{9,5},... | collective-permute-start | bytes 331784 | tf_op jit(solution)/shard_map/ppermute | solution.py:93
  45.7 0.1 shard_map.90
  45.8 1.3 %collective-permute-start.14 = (bf16[288,128]{1,0:T(8,128)(2,1)S(1)}, bf16[288,128]{1,0:T(8,128)(2,1)S(1)}, u32[]{:S(2)}, u32[]{:S(2)}) collective-permute-start(bf16[288,128]{1,0:T(8,128)(2,1)S(1)} %get-tuple-element.74), channel_id=1, source_target_pairs={{0,12},{1,13},{2,14},{3,15},{4,10},{5,11},{6,8},{7,9},{8,4},{9,5},... | collective-permute-start | bytes 221192 | tf_op jit(solution)/shard_map/ppermute | solution.py:452
  47.1 1.1 %shard_map.93 = (f32[1,64]{1,0:T(1,128)}, bf16[1,128,128]{2,1,0:T(8,128)(2,1)}) custom-call(f32[1,128]{1,0:T(1,128)S(1)} %get-tuple-element.62.vector, f32[64,64]{1,0:T(8,128)S(1)} %copy-done.3, bf16[1,64,128,128]{3,2,1,0:T(8,128)(2,1)S(1)} %copy-done), custom_call_target="tpu_custom_call" | custom-call | flops 1024 | bytes 1024 | tf_op jit(solution)/shard_map/pallas_call | solution.py:396
  48.3 4.0 %collective-permute-start.16 = (bf16[272,128]{1,0:T(8,128)(2,1)S(1)}, bf16[272,128]{1,0:T(8,128)(2,1)S(1)}, u32[]{:S(2)}, u32[]{:S(2)}) collective-permute-start(bf16[272,128]{1,0:T(8,128)(2,1)S(1)} %get-tuple-element.75), channel_id=1, source_target_pairs={{0,4},{1,5},{2,6},{3,7},{4,2},{5,3},{6,0},{7,1},{8,12},{9,13},{10,... | collective-permute-start | bytes 208904 | tf_op jit(solution)/shard_map/ppermute | solution.py:452
  52.4 2.8 %collective-permute-start.18 = (bf16[256,128]{1,0:T(8,128)(2,1)S(1)}, bf16[256,128]{1,0:T(8,128)(2,1)S(1)}, u32[]{:S(2)}, u32[]{:S(2)}) collective-permute-start(bf16[256,128]{1,0:T(8,128)(2,1)S(1)} %get-tuple-element.76), channel_id=1, source_target_pairs={{0,8},{1,9},{2,10},{3,11},{4,12},{5,13},{6,14},{7,15},{8,2},{9,3},... | collective-permute-start | bytes 196616 | tf_op jit(solution)/shard_map/ppermute | solution.py:452
  55.1 0.5 collective-permute-start.15
  55.7 2.8 %collective-permute-done.18.refs_4_ = bf16[256,128]{1,0:T(8,128)(2,1)S(1)} collective-permute-done((bf16[256,128]{1,0:T(8,128)(2,1)S(1)}, bf16[256,128]{1,0:T(8,128)(2,1)S(1)}, u32[]{:S(2)}, u32[]{:S(2)}) %collective-permute-start.18) | collective-permute-done | bytes 65568 | tf_op jit(solution)/shard_map/ppermute | solution.py:452
  58.5 1.2 %collective-permute-done.19.refs_5_ = bf16[256,128]{1,0:T(8,128)(2,1)S(1)} collective-permute-done((bf16[256,128]{1,0:T(8,128)(2,1)S(1)}, bf16[256,128]{1,0:T(8,128)(2,1)S(1)}, u32[]{:S(2)}, u32[]{:S(2)}) %collective-permute-start.19) | collective-permute-done | bytes 65568 | tf_op jit(solution)/shard_map/ppermute | solution.py:93
  59.8 1.5 %shard_map.98 = bf16[1,128,2048]{2,1,0:T(8,128)(2,1)} custom-call(s32[16]{0:T(128)S(1)} %copy-done.4, bf16[128,384]{1,0:T(8,128)(2,1)S(1)} %get-tuple-element.57.early, bf16[128,384]{1,0:T(8,128)(2,1)S(1)} %get-tuple-element.66.late, bf16[128,384]{1,0:T(8,128)(2,1)S(1)} %get-tuple-element.72.later, bf16[304,128]{1,0:T(8,128)(2,1)S(1)} %get-tuple-element.73.extra, ...), custom_call_target="tpu_custom_call" | custom-call | flops 1024 | bytes 1024 | tf_op jit(solution)/shard_map/pallas_call | solution.py:488
  (41 shorter events, 1.2 us)
Async XLA Ops:
  0.6 4.0 %collective-permute-start.2 = (bf16[16,6,64,128]{3,2,1,0:T(8,128)(2,1)}, bf16[16,6,64,128]{3,2,1,0:T(8,128)(2,1)S(1)}, u32[]{:S(2)}, u32[]{:S(2)}) collective-permute-start(bf16[16,6,64,128]{3,2,1,0:T(8,128)(2,1)} %far), channel_id=1, source_target_pairs={{0,1},{1,0},{2,3},{3,2},{4,5},{5,4},{6,7},{7,6},{8,9},{9,8},{10,11... | collective-permute-start | bytes 4718600 | tf_op jit(solution)/shard_map/ppermute | solution.py:93
  2.1 2.5 %collective-permute-start.1 = (s32[6,16]{1,0:T(8,128)S(1)}, s32[6,16]{1,0:T(8,128)S(1)}, u32[]{:S(2)}, u32[]{:S(2)}) collective-permute-start(s32[6,16]{1,0:T(8,128)S(1)} %get-tuple-element.42.ranks), channel_id=1, source_target_pairs={{0,1},{1,0},{2,3},{3,2},{4,5},{5,4},{6,7},{7,6},{8,9},{9,8},{10,11... | collective-permute-start | bytes 1160 | tf_op jit(solution)/shard_map/ppermute | solution.py:93
  2.2 2.4 %collective-permute-start.3 = (f32[6,16,128]{2,1,0:T(8,128)}, f32[6,16,128]{2,1,0:T(8,128)S(1)}, u32[]{:S(2)}, u32[]{:S(2)}) collective-permute-start(f32[6,16,128]{2,1,0:T(8,128)} %bitcast.3), channel_id=1, source_target_pairs={{0,1},{1,0},{2,3},{3,2},{4,5},{5,4},{6,7},{7,6},{8,9},{9,8},{10,11... | collective-permute-start | bytes 147464 | tf_op jit(solution)/shard_map/ppermute | solution.py:93
  3.0 1.6 %collective-permute-start = (s32[16,6]{1,0:T(8,128)S(1)}, s32[16,6]{1,0:T(8,128)S(1)}, u32[]{:S(2)}, u32[]{:S(2)}) collective-permute-start(s32[16,6]{1,0:T(8,128)S(1)} %broadcast_add_fusion.listed), channel_id=1, source_target_pairs={{0,1},{1,0},{2,3},{3,2},{4,5},{5,4},{6,7},{7,6},{8,9},{9,8},{10,11... | collective-permute-start | bytes 1160 | tf_op jit(solution)/shard_map/ppermute | solution.py:93
  3.1 1.4 %copy-start.1 = (bf16[16,6,64,128]{3,2,1,0:T(8,128)(2,1)S(1)}, bf16[16,6,64,128]{3,2,1,0:T(8,128)(2,1)}, u32[]{:S(2)}) copy-start(bf16[16,6,64,128]{3,2,1,0:T(8,128)(2,1)} %far) | copy-start | bytes 4718596
  4.5 0.8 %copy-start.2 = (f32[16,6,128]{2,0,1:T(8,128)S(1)}, f32[16,6,128]{2,0,1:T(8,128)}, u32[]{:S(2)}) copy-start(f32[16,6,128]{2,0,1:T(8,128)} %param.9) | copy-start | bytes 147460
  12.6 12.7 %collective-permute-start.4 = (s16[528,384]{1,0:T(8,128)(2,1)S(1)}, s16[528,384]{1,0:T(8,128)(2,1)S(1)}, u32[]{:S(2)}, u32[]{:S(2)}) collective-permute-start(s16[528,384]{1,0:T(8,128)(2,1)S(1)} %get-tuple-element.45), channel_id=1, source_target_pairs={{0,4},{1,5},{2,6},{3,7},{4,0},{5,1},{6,2},{7,3},{8,12},{9,13},{10,... | collective-permute-start | bytes 1216520 | tf_op jit(solution)/shard_map/ppermute | solution.py:93
  15.7 12.6 %collective-permute-start.7 = (s16[528,384]{1,0:T(8,128)(2,1)S(1)}, s16[528,384]{1,0:T(8,128)(2,1)S(1)}, u32[]{:S(2)}, u32[]{:S(2)}) collective-permute-start(s16[528,384]{1,0:T(8,128)(2,1)S(1)} %get-tuple-element.44), channel_id=1, source_target_pairs={{0,2},{1,3},{2,0},{3,1},{4,6},{5,7},{6,4},{7,5},{8,10},{9,11},{10,... | collective-permute-start | bytes 1216520 | tf_op jit(solution)/shard_map/ppermute | solution.py:93
  17.2 18.2 %collective-permute-start.10 = (s16[528,384]{1,0:T(8,128)(2,1)S(1)}, s16[528,384]{1,0:T(8,128)(2,1)S(1)}, u32[]{:S(2)}, u32[]{:S(2)}) collective-permute-start(s16[528,384]{1,0:T(8,128)(2,1)S(1)} %get-tuple-element.46), channel_id=1, source_target_pairs={{0,2},{1,3},{2,0},{3,1},{4,6},{5,7},{6,4},{7,5},{8,10},{9,11},{10,... | collective-permute-start | bytes 1216520 | tf_op jit(solution)/shard_map/ppermute | solution.py:93
  25.4 12.1 %collective-permute-start.5 = (s16[272,384]{1,0:T(8,128)(2,1)S(1)}, s16[272,384]{1,0:T(8,128)(2,1)S(1)}, u32[]{:S(2)}, u32[]{:S(2)}) collective-permute-start(s16[272,384]{1,0:T(8,128)(2,1)S(1)} %get-tuple-element.52), channel_id=1, source_target_pairs={{0,8},{1,9},{2,10},{3,11},{4,12},{5,13},{6,14},{7,15},{8,0},{9,1},... | collective-permute-start | bytes 626696 | tf_op jit(solution)/shard_map/ppermute | solution.py:93
  28.5 10.7 %collective-permute-start.8 = (s16[288,384]{1,0:T(8,128)(2,1)S(1)}, s16[288,384]{1,0:T(8,128)(2,1)S(1)}, u32[]{:S(2)}, u32[]{:S(2)}) collective-permute-start(s16[288,384]{1,0:T(8,128)(2,1)S(1)} %get-tuple-element.60), channel_id=1, source_target_pairs={{0,4},{1,5},{2,6},{3,7},{4,0},{5,1},{6,2},{7,3},{8,12},{9,13},{10,... | collective-permute-start | bytes 663560 | tf_op jit(solution)/shard_map/ppermute | solution.py:93
  35.4 11.7 %copy-start = (bf16[1,64,128,128]{3,2,1,0:T(8,128)(2,1)S(1)}, bf16[1,64,128,128]{3,2,1,0:T(8,128)(2,1)}, u32[]{:S(2)}) copy-start(bf16[1,64,128,128]{3,2,1,0:T(8,128)(2,1)} %tiles.1) | copy-start | bytes 6291460
  35.4 11.7 %copy-start.3 = (f32[64,64]{1,0:T(8,128)S(1)}, f32[64,64]{1,0:T(8,128)}, u32[]{:S(2)}) copy-start(f32[64,64]{1,0:T(8,128)} %metric.1) | copy-start | bytes 49156
  35.6 7.3 %collective-permute-start.11 = (s16[272,384]{1,0:T(8,128)(2,1)S(1)}, s16[272,384]{1,0:T(8,128)(2,1)S(1)}, u32[]{:S(2)}, u32[]{:S(2)}) collective-permute-start(s16[272,384]{1,0:T(8,128)(2,1)S(1)} %get-tuple-element.69), channel_id=1, source_target_pairs={{0,4},{1,5},{2,6},{3,7},{4,0},{5,1},{6,2},{7,3},{8,12},{9,13},{10,... | collective-permute-start | bytes 626696 | tf_op jit(solution)/shard_map/ppermute | solution.py:93
  37.7 8.0 %collective-permute-start.6 = (s16[144,512]{1,0:T(8,128)(2,1)S(1)}, s16[144,512]{1,0:T(8,128)(2,1)S(1)}, u32[]{:S(2)}, u32[]{:S(2)}) collective-permute-start(s16[144,512]{1,0:T(8,128)(2,1)S(1)} %get-tuple-element.56), channel_id=1, source_target_pairs={{0,2},{1,3},{2,0},{3,1},{4,6},{5,7},{6,4},{7,5},{8,10},{9,11},{10,... | collective-permute-start | bytes 442376 | tf_op jit(solution)/shard_map/ppermute | solution.py:93
  39.3 8.9 %collective-permute-start.9 = (s16[144,384]{1,0:T(8,128)(2,1)S(1)}, s16[144,384]{1,0:T(8,128)(2,1)S(1)}, u32[]{:S(2)}, u32[]{:S(2)}) collective-permute-start(s16[144,384]{1,0:T(8,128)(2,1)S(1)} %get-tuple-element.65), channel_id=1, source_target_pairs={{0,12},{1,13},{2,14},{3,15},{4,8},{5,9},{6,10},{7,11},{8,4},{9,5},... | collective-permute-start | bytes 331784 | tf_op jit(solution)/shard_map/ppermute | solution.py:93
  43.0 9.3 %collective-permute-start.12 = (s16[144,384]{1,0:T(8,128)(2,1)S(1)}, s16[144,384]{1,0:T(8,128)(2,1)S(1)}, u32[]{:S(2)}, u32[]{:S(2)}) collective-permute-start(s16[144,384]{1,0:T(8,128)(2,1)S(1)} %get-tuple-element.71), channel_id=1, source_target_pairs={{0,12},{1,13},{2,14},{3,15},{4,8},{5,9},{6,10},{7,11},{8,4},{9,5},... | collective-permute-start | bytes 331784 | tf_op jit(solution)/shard_map/ppermute | solution.py:93
  45.7 14.1 %copy-start.4 = (s32[16]{0:T(128)S(1)}, s32[16]{0:T(128)}, u32[]{:S(2)}) copy-start(s32[16]{0:T(128)} %holders.1) | copy-start | bytes 196
  45.8 9.4 %collective-permute-start.14 = (bf16[288,128]{1,0:T(8,128)(2,1)S(1)}, bf16[288,128]{1,0:T(8,128)(2,1)S(1)}, u32[]{:S(2)}, u32[]{:S(2)}) collective-permute-start(bf16[288,128]{1,0:T(8,128)(2,1)S(1)} %get-tuple-element.74), channel_id=1, source_target_pairs={{0,12},{1,13},{2,14},{3,15},{4,10},{5,11},{6,8},{7,9},{8,4},{9,5},... | collective-permute-start | bytes 221192 | tf_op jit(solution)/shard_map/ppermute | solution.py:452
  48.3 7.4 %collective-permute-start.16 = (bf16[272,128]{1,0:T(8,128)(2,1)S(1)}, bf16[272,128]{1,0:T(8,128)(2,1)S(1)}, u32[]{:S(2)}, u32[]{:S(2)}) collective-permute-start(bf16[272,128]{1,0:T(8,128)(2,1)S(1)} %get-tuple-element.75), channel_id=1, source_target_pairs={{0,4},{1,5},{2,6},{3,7},{4,2},{5,3},{6,0},{7,1},{8,12},{9,13},{10,... | collective-permute-start | bytes 208904 | tf_op jit(solution)/shard_map/ppermute | solution.py:452
  52.4 6.1 %collective-permute-start.18 = (bf16[256,128]{1,0:T(8,128)(2,1)S(1)}, bf16[256,128]{1,0:T(8,128)(2,1)S(1)}, u32[]{:S(2)}, u32[]{:S(2)}) collective-permute-start(bf16[256,128]{1,0:T(8,128)(2,1)S(1)} %get-tuple-element.76), channel_id=1, source_target_pairs={{0,8},{1,9},{2,10},{3,11},{4,12},{5,13},{6,14},{7,15},{8,2},{9,3},... | collective-permute-start | bytes 196616 | tf_op jit(solution)/shard_map/ppermute | solution.py:452
  55.1 3.4 %collective-permute-start.13 = (bf16[304,128]{1,0:T(8,128)(2,1)S(1)}, bf16[304,128]{1,0:T(8,128)(2,1)S(1)}, u32[]{:S(2)}, u32[]{:S(2)}) collective-permute-start(bf16[304,128]{1,0:T(8,128)(2,1)S(1)} %get-tuple-element.73.extra), channel_id=1, source_target_pairs={{0,1},{1,0},{2,3},{3,2},{4,5},{5,4},{6,7},{7,6},{8,9},{9,8},{10,11... | collective-permute-start | bytes 233480 | tf_op jit(solution)/shard_map/ppermute | solution.py:93
  55.1 4.6 %collective-permute-start.15 = (bf16[288,128]{1,0:T(8,128)(2,1)S(1)}, bf16[288,128]{1,0:T(8,128)(2,1)S(1)}, u32[]{:S(2)}, u32[]{:S(2)}) collective-permute-start(bf16[288,128]{1,0:T(8,128)(2,1)S(1)} %collective-permute-done.14.refs_0_), channel_id=1, source_target_pairs={{0,1},{1,0},{2,3},{3,2},{4,5},{5,4},{6,7},{7,6},{8,9},{9,8},{10,11... | collective-permute-start | bytes 221192 | tf_op jit(solution)/shard_map/ppermute | solution.py:93
  55.7 4.1 %collective-permute-start.17 = (bf16[272,128]{1,0:T(8,128)(2,1)S(1)}, bf16[272,128]{1,0:T(8,128)(2,1)S(1)}, u32[]{:S(2)}, u32[]{:S(2)}) collective-permute-start(bf16[272,128]{1,0:T(8,128)(2,1)S(1)} %collective-permute-done.16.refs_2_), channel_id=1, source_target_pairs={{0,1},{1,0},{2,3},{3,2},{4,5},{5,4},{6,7},{7,6},{8,9},{9,8},{10,11... | collective-permute-start | bytes 208904 | tf_op jit(solution)/shard_map/ppermute | solution.py:93
  58.5 1.3 %collective-permute-start.19 = (bf16[256,128]{1,0:T(8,128)(2,1)S(1)}, bf16[256,128]{1,0:T(8,128)(2,1)S(1)}, u32[]{:S(2)}, u32[]{:S(2)}) collective-permute-start(bf16[256,128]{1,0:T(8,128)(2,1)S(1)} %collective-permute-done.18.refs_4_), channel_id=1, source_target_pairs={{0,1},{1,0},{2,3},{3,2},{4,5},{5,4},{6,7},{7,6},{8,9},{9,8},{10,11... | collective-permute-start | bytes 196616 | tf_op jit(solution)/shard_map/ppermute | solution.py:93
